TPU v7x, 32 devices: a whole 2x2x4 slice. The times are simulated.
32 devices in a mesh: section: 2 (over core), row: 4 (over z), col: 4 (over y, x).
Axes of the slice: x: 2, y: 2, z: 4, core: 2. Of those that a mesh axis runs over, the one named last changes fastest.
Arguments:
- tokens: bfloat16 [4, 1024, 1536], P(None, 'row'), may hold values from -6 to 6
- cotangent: bfloat16 [4, 1024, 1536], P(None, 'row'), may hold values from -6 to 6
- lengths: int32 [4, 3], replicated, may hold values from 1 to 1022, as said below
- norm_attn: bfloat16 [2, 1536], P('section'), may hold values from 0.5 to 1.5
- w_query: bfloat16 [2, 1536, 1536], P('section', 'row', 'col'), may hold values from -0.15625 to 0.15625
- b_query: bfloat16 [2, 1536], P('section', 'col'), may hold values from -3 to 3
- w_keyval: bfloat16 [2, 1536, 512], P('section', ('row', 'col')), may hold values from -0.15625 to 0.15625
- b_keyval: bfloat16 [2, 512], P('section'), may hold values from -3 to 3
- w_out: bfloat16 [2, 1536, 1536], P('section', 'col', 'row'), may hold values from -0.5 to 0.5
- norm_ffn: bfloat16 [2, 1536], P('section'), may hold values from 0.5 to 1.5
- w_gate: bfloat16 [2, 1536, 8960], P('section', 'row', 'col'), may hold values from -0.15625 to 0.15625
- w_up: bfloat16 [2, 1536, 8960], P('section', 'row', 'col'), may hold values from -0.15625 to 0.15625
- w_down: bfloat16 [2, 8960, 1536], P('section', 'col', 'row'), may hold values from -0.0625 to 0.0625
Outputs:
- activations: bfloat16 [2, 4, 1024, 1536], P('section', None, 'row')
- input_grads: bfloat16 [2, 4, 1024, 1536], P('section', None, 'row')
- grad_norm_attn: float32 [2, 1536], P('section')
- grad_w_query: float32 [2, 1536, 1536], P('section', 'row', 'col')
- grad_b_query: float32 [2, 1536], P('section', 'col')
- grad_w_keyval: float32 [2, 1536, 512], P('section', ('row', 'col'))
- grad_b_keyval: float32 [2, 512], P('section')
- grad_w_out: float32 [2, 1536, 1536], P('section', 'col', 'row')
- grad_norm_ffn: float32 [2, 1536], P('section')
- grad_w_gate: float32 [2, 1536, 8960], P('section', 'row', 'col')
- grad_w_up: float32 [2, 1536, 8960], P('section', 'row', 'col')
- grad_w_down: float32 [2, 8960, 1536], P('section', 'col', 'row')
Inputs may be any that keep to these rules, and one draw needn't show every extreme that they name: `lengths`: each micro-batch holds three sequences: the first and the last have fewer than 256 tokens each, the middle one the rest of the 1024; in one micro-batch the first and the last have one token each.
All inputs are finite; a program needn't handle non-finite values.
Results may differ from a plain program's by a relative error of at most 0.025.
Values may be sent and summed in bfloat16 or wider, within the bound.
A program may use at most 320 MiB of HBM per device.

v0:
```python
import math

import jax
import jax.numpy as jnp
from jax import lax
from jax.sharding import PartitionSpec as P

HEADS = 12
KV = 2
HEAD = 128


EPS = 1e-06
THETA = 1000000.0


def partner(value, axis, distance):
    mask = 2**distance
    pairs = [(source, source ^ mask) for source in range(lax.axis_size(axis))]
    return lax.ppermute(value, axis, pairs)


def from_behind(x, axis, by):
    peers = lax.axis_size(axis)
    pairs = [(i, i + by) for i in range(peers) if 0 <= i + by < peers]
    return lax.ppermute(x, axis, pairs)


def rope_tables(positions):
    inverse = THETA ** (-(jnp.arange(HEAD // 2, dtype=jnp.float32) * 2.0 / HEAD))
    angle = positions.astype(jnp.float32)[:, None] * inverse[None, :]
    return (jnp.cos(angle)[:, None, :], jnp.sin(angle)[:, None, :])


def rotate(vectors, cosine, sine):
    half_size = vectors.shape[-1] // 2
    first_half = vectors[..., :half_size]
    second_half = vectors[..., half_size:]
    return jnp.concatenate(
        [first_half * cosine - second_half * sine, second_half * cosine + first_half * sine],
        axis=-1,
    )


def unrotate(gradient, cosine, sine):
    half_size = gradient.shape[-1] // 2
    first_half = gradient[..., :half_size]
    second_half = gradient[..., half_size:]
    return jnp.concatenate(
        [first_half * cosine + second_half * sine, second_half * cosine - first_half * sine],
        axis=-1,
    )


def norm_forward(stream, gain):
    inverse = lax.rsqrt(jnp.mean(stream * stream, axis=-1, keepdims=True) + EPS)
    return (stream * inverse * gain, inverse)


def norm_backward(stream, inverse, gain, gradient):
    inner = jnp.mean(gradient * gain * stream, axis=-1, keepdims=True)
    d_stream = gain * gradient * inverse - stream * (inverse * inverse * inverse) * inner
    return (d_stream, jnp.sum(gradient * stream * inverse, axis=0))


def column_sum(partial_sum):
    return lax.psum(partial_sum.astype(jnp.bfloat16), "col").astype(jnp.float32)


def column_back(partial_sum):
    return lax.psum(partial_sum.astype(jnp.bfloat16), "col").astype(jnp.float32)


def own_columns(matrix, group_id, along):
    key_part = lax.dynamic_slice_in_dim(matrix, group_id * HEAD, HEAD, along)
    value_part = lax.dynamic_slice_in_dim(matrix, (KV + group_id) * HEAD, HEAD, along)
    return jnp.concatenate([key_part, value_part], axis=along)


def add_columns(totals, addend, group_id, along):
    for piece_index, offset in ((0, group_id * HEAD), (1, (KV + group_id) * HEAD)):
        addend_part = lax.slice_in_dim(
            addend, piece_index * HEAD, (piece_index + 1) * HEAD, axis=along
        )
        current = lax.dynamic_slice_in_dim(totals, offset, HEAD, along)
        totals = lax.dynamic_update_slice_in_dim(totals, current + addend_part, offset, along)
    return totals


def layout(lengths, micro_slot, row_count):
    lengths_row = lax.dynamic_index_in_dim(lengths, micro_slot, 0, keepdims=False)
    total_rows = row_count * lax.axis_size("row")
    token_index = jnp.arange(total_rows, dtype=jnp.int32)
    seq_ends = jnp.cumsum(lengths_row)
    segment = jnp.sum((token_index[:, None] >= seq_ends[None, :]).astype(jnp.int32), axis=1)
    seq_starts = seq_ends - lengths_row
    piece_ids = jnp.arange(lengths_row.shape[0], dtype=jnp.int32)
    first_index = jnp.sum(
        jnp.where(segment[:, None] == piece_ids[None, :], seq_starts[None, :], 0), axis=1
    )
    first_row = lax.axis_index("row") * row_count
    own_index = first_row + jnp.arange(row_count, dtype=jnp.int32)
    own_segment = lax.dynamic_slice_in_dim(segment, first_row, row_count)
    own_position = own_index - lax.dynamic_slice_in_dim(first_index, first_row, row_count)
    cosine, sine = rope_tables(own_position)
    allowed = (own_segment[:, None] == segment[None, :]) & (
        token_index[None, :] <= own_index[:, None]
    )
    return (allowed, cosine, sine)


def forward_layer(hidden, whole, small, context, group_id):
    w_query, w_keyval, w_out, w_gate, w_up, w_down = whole
    gain_attn, b_query, b_keyval, gain_ffn = small
    allowed, cosine, sine = context
    row_count = hidden.shape[0]
    score_scale = 1.0 / math.sqrt(HEAD)
    stream = hidden.astype(jnp.float32)
    normed, inverse_one = norm_forward(stream, gain_attn)
    normed_low = normed.astype(jnp.bfloat16)
    w_pair = own_columns(w_keyval, group_id, 1)
    query = jnp.dot(normed_low, w_query, preferred_element_type=jnp.float32) + b_query
    query_low = rotate(query.reshape(row_count, -1, HEAD), cosine, sine).astype(jnp.bfloat16)
    pair = jnp.dot(normed_low, w_pair, preferred_element_type=jnp.float32) + own_columns(
        b_keyval, group_id, 0
    )
    key_low = rotate(pair[:, None, :HEAD], cosine, sine)[:, 0].astype(jnp.bfloat16)
    local_pair = jnp.concatenate([key_low, pair[:, HEAD:].astype(jnp.bfloat16)], axis=1)
    gathered = lax.all_gather(local_pair, "row", axis=0, tiled=True)
    key_rows = gathered[:, :HEAD]
    value_rows = gathered[:, HEAD:]
    scores = (
        jnp.einsum("thd,sd->hts", query_low, key_rows, preferred_element_type=jnp.float32)
        * score_scale
    )
    masked = jnp.where(allowed[None], scores, -1e30)
    row_max = jnp.max(masked, axis=-1, keepdims=True)
    weights = jnp.exp(masked - row_max)
    probs = weights / jnp.sum(weights, axis=-1, keepdims=True)
    probs_low = probs.astype(jnp.bfloat16)
    mixed = jnp.einsum("hts,sd->thd", probs_low, value_rows, preferred_element_type=jnp.float32)
    mixed_low = mixed.reshape(row_count, -1).astype(jnp.bfloat16)
    second = stream + column_sum(jnp.dot(mixed_low, w_out, preferred_element_type=jnp.float32))
    normed_two, inverse_two = norm_forward(second, gain_ffn)
    normed_two_low = normed_two.astype(jnp.bfloat16)
    gate = jnp.dot(normed_two_low, w_gate, preferred_element_type=jnp.float32)
    up_proj = jnp.dot(normed_two_low, w_up, preferred_element_type=jnp.float32)
    act_low = (jax.nn.silu(gate) * up_proj).astype(jnp.bfloat16)
    result = second + column_sum(jnp.dot(act_low, w_down, preferred_element_type=jnp.float32))
    saved = (
        stream,
        inverse_one,
        normed_low,
        query_low,
        key_rows,
        value_rows,
        probs,
        probs_low,
        mixed_low,
        second,
        inverse_two,
        normed_two_low,
        gate,
        up_proj,
        act_low,
    )
    return (result, saved)


def backward_layer(saved, grad_low, whole, small, context, group_id, pair_share, totals):
    (
        stream,
        inverse_one,
        normed_low,
        query_low,
        key_rows,
        value_rows,
        probs,
        probs_low,
        mixed_low,
        second,
        inverse_two,
        normed_two_low,
        gate,
        up_proj,
        act_low,
    ) = saved
    w_query, w_keyval, w_out, w_gate, w_up, w_down = whole
    gain_attn, b_query, b_keyval, gain_ffn = small
    allowed, cosine, sine = context
    (
        acc_query,
        acc_keyval,
        acc_out,
        acc_gate,
        acc_up,
        acc_down,
        acc_gain_one,
        acc_bias_query,
        acc_bias_keyval,
        acc_gain_two,
    ) = totals
    row_count = grad_low.shape[0]
    score_scale = 1.0 / math.sqrt(HEAD)
    w_pair = own_columns(w_keyval, group_id, 1)
    d_output = grad_low.astype(jnp.float32)
    acc_down = acc_down + jnp.einsum(
        "tf,td->fd", act_low, grad_low, preferred_element_type=jnp.float32
    )
    d_act = jnp.einsum("td,fd->tf", grad_low, w_down, preferred_element_type=jnp.float32)
    sigma = jax.nn.sigmoid(gate)
    d_gate = (d_act * up_proj * sigma * (1.0 + gate * (1.0 - sigma))).astype(jnp.bfloat16)
    d_up = (d_act * gate * sigma).astype(jnp.bfloat16)
    acc_gate = acc_gate + jnp.einsum(
        "td,tf->df", normed_two_low, d_gate, preferred_element_type=jnp.float32
    )
    acc_up = acc_up + jnp.einsum(
        "td,tf->df", normed_two_low, d_up, preferred_element_type=jnp.float32
    )
    d_normed_two = column_back(
        jnp.einsum("tf,df->td", d_gate, w_gate, preferred_element_type=jnp.float32)
        + jnp.einsum("tf,df->td", d_up, w_up, preferred_element_type=jnp.float32)
    )
    d_second_norm, d_gain_two = norm_backward(second, inverse_two, gain_ffn, d_normed_two)
    d_second = d_output + d_second_norm
    d_attn_low = d_second.astype(jnp.bfloat16)
    acc_out = acc_out + jnp.einsum(
        "tc,td->cd", mixed_low, d_attn_low, preferred_element_type=jnp.float32
    )
    d_mixed = jnp.einsum("td,cd->tc", d_attn_low, w_out, preferred_element_type=jnp.float32)
    d_mixed_low = d_mixed.astype(jnp.bfloat16).reshape(row_count, -1, HEAD)
    d_probs = jnp.einsum("thd,sd->hts", d_mixed_low, value_rows, preferred_element_type=jnp.float32)
    d_values = jnp.einsum("hts,thd->sd", probs_low, d_mixed_low, preferred_element_type=jnp.float32)
    delta = jnp.sum(d_probs * probs, axis=-1, keepdims=True)
    d_scores = (probs * (d_probs - delta)).astype(jnp.bfloat16)
    d_query = (
        jnp.einsum("hts,sd->thd", d_scores, key_rows, preferred_element_type=jnp.float32)
        * score_scale
    )
    d_keys = (
        jnp.einsum("hts,thd->sd", d_scores, query_low, preferred_element_type=jnp.float32)
        * score_scale
    )
    summed = lax.psum_scatter(
        jnp.concatenate([d_keys, d_values], axis=1).astype(jnp.bfloat16),
        "row",
        scatter_dimension=0,
        tiled=True,
    ).astype(jnp.float32)
    summed = summed + partner(summed.astype(jnp.bfloat16), "col", 0).astype(summed.dtype)
    d_key_low = unrotate(summed[:, None, :HEAD], cosine, sine)[:, 0].astype(jnp.bfloat16)
    d_pair = (
        jnp.concatenate([d_key_low, summed[:, HEAD:].astype(jnp.bfloat16)], axis=1) * pair_share
    )
    d_query_low = unrotate(d_query, cosine, sine).reshape(row_count, -1).astype(jnp.bfloat16)
    acc_query = acc_query + jnp.einsum(
        "td,tc->dc", normed_low, d_query_low, preferred_element_type=jnp.float32
    )
    acc_keyval = add_columns(
        acc_keyval,
        jnp.einsum("td,tc->dc", normed_low, d_pair, preferred_element_type=jnp.float32),
        group_id,
        1,
    )
    acc_bias_query = acc_bias_query + jnp.sum(d_query_low.astype(jnp.float32), axis=0)
    acc_bias_keyval = add_columns(
        acc_bias_keyval, jnp.sum(d_pair.astype(jnp.float32), axis=0), group_id, 0
    )
    d_normed = column_back(
        jnp.einsum("tc,dc->td", d_query_low, w_query, preferred_element_type=jnp.float32)
        + jnp.einsum("tc,dc->td", d_pair, w_pair, preferred_element_type=jnp.float32)
    )
    d_first_norm, d_gain_one = norm_backward(stream, inverse_one, gain_attn, d_normed)
    d_input = (d_second + d_first_norm).astype(jnp.bfloat16)
    totals = (
        acc_query,
        acc_keyval,
        acc_out,
        acc_gate,
        acc_up,
        acc_down,
        acc_gain_one + d_gain_one,
        acc_bias_query,
        acc_bias_keyval,
        acc_gain_two + d_gain_two,
    )
    return (d_input, totals)


def local(
    tokens,
    cotangent,
    lengths,
    norm_attn,
    w_query,
    b_query,
    w_keyval,
    b_keyval,
    w_out,
    norm_ffn,
    w_gate,
    w_up,
    w_down,
):
    micro_count = tokens.shape[0]
    row_count = tokens.shape[1]
    width = tokens.shape[2]
    sections = lax.axis_size("section")
    section_index = lax.axis_index("section")
    col_index = lax.axis_index("col")
    heads_here = w_query.shape[2] // HEAD
    group_id = col_index * heads_here // (HEADS // KV)
    pair_share = jnp.asarray(0.5, jnp.bfloat16)
    is_first = section_index == 0
    is_last = section_index == sections - 1
    small = (
        norm_attn[0].astype(jnp.float32),
        b_query[0].astype(jnp.float32),
        b_keyval[0].astype(jnp.float32),
        norm_ffn[0].astype(jnp.float32),
    )
    keyval_whole = lax.all_gather(w_keyval[0], ("row", "col"), axis=0, tiled=True)
    whole = (
        lax.all_gather(w_query[0], "row", axis=0, tiled=True),
        keyval_whole,
        lax.all_gather(w_out[0], "row", axis=1, tiled=True),
        lax.all_gather(w_gate[0], "row", axis=0, tiled=True),
        lax.all_gather(w_up[0], "row", axis=0, tiled=True),
        lax.all_gather(w_down[0], "row", axis=1, tiled=True),
    )
    received = jnp.zeros((row_count, width), jnp.bfloat16)
    outputs = jnp.zeros((micro_count, row_count, width), jnp.bfloat16)
    inputs = jnp.zeros((micro_count, row_count, width), jnp.bfloat16)
    for tick_step in range(micro_count + sections - 1):
        micro_index = tick_step - section_index
        valid = (micro_index >= 0) & (micro_index < micro_count)
        micro_slot = jnp.clip(micro_index, 0, micro_count - 1)
        own_tokens = tokens[min(tick_step, micro_count - 1)]
        hidden = jnp.where(is_first, own_tokens, received)
        context = layout(lengths, micro_slot, row_count)
        result, saved = forward_layer(hidden, whole, small, context, group_id)
        result_low = result.astype(jnp.bfloat16)
        inputs = jnp.where(
            valid, lax.dynamic_update_index_in_dim(inputs, hidden, micro_slot, 0), inputs
        )
        outputs = jnp.where(
            valid, lax.dynamic_update_index_in_dim(outputs, result_low, micro_slot, 0), outputs
        )
        received = from_behind(result_low, "section", 1)
    totals = (
        jnp.zeros(whole[0].shape, jnp.float32),
        jnp.zeros(whole[1].shape, jnp.float32),
        jnp.zeros(whole[2].shape, jnp.float32),
        jnp.zeros(whole[3].shape, jnp.float32),
        jnp.zeros(whole[4].shape, jnp.float32),
        jnp.zeros(whole[5].shape, jnp.float32),
        jnp.zeros((width,), jnp.float32),
        jnp.zeros((heads_here * HEAD,), jnp.float32),
        jnp.zeros(b_keyval.shape[1:], jnp.float32),
        jnp.zeros((width,), jnp.float32),
    )
    incoming = jnp.zeros((row_count, width), jnp.bfloat16)
    grads_in = jnp.zeros((micro_count, row_count, width), jnp.bfloat16)
    for tick_step in range(micro_count + sections - 1):
        micro_index = tick_step - (sections - 1 - section_index)
        valid = (micro_index >= 0) & (micro_index < micro_count)
        micro_slot = jnp.clip(micro_index, 0, micro_count - 1)
        own_grad = cotangent[min(tick_step, micro_count - 1)]
        grad_low = jnp.where(is_last, own_grad, incoming)
        grad_low = jnp.where(valid, grad_low, jnp.zeros_like(grad_low))
        context = layout(lengths, micro_slot, row_count)
        hidden = lax.dynamic_index_in_dim(inputs, micro_slot, 0, keepdims=False)
        result, saved = forward_layer(hidden, whole, small, context, group_id)
        d_input, totals = backward_layer(
            saved, grad_low, whole, small, context, group_id, pair_share, totals
        )
        grads_in = jnp.where(
            valid, lax.dynamic_update_index_in_dim(grads_in, d_input, micro_slot, 0), grads_in
        )
        incoming = from_behind(d_input, "section", -1)
    (
        acc_query,
        acc_keyval,
        acc_out,
        acc_gate,
        acc_up,
        acc_down,
        acc_gain_one,
        acc_bias_query,
        acc_bias_keyval,
        acc_gain_two,
    ) = totals
    weight_sums = (
        lax.psum_scatter(
            acc_query.astype(jnp.bfloat16), "row", scatter_dimension=0, tiled=True
        ).astype(jnp.float32),
        lax.psum_scatter(
            acc_out.astype(jnp.bfloat16), "row", scatter_dimension=1, tiled=True
        ).astype(jnp.float32),
        lax.psum_scatter(
            acc_gate.astype(jnp.bfloat16), "row", scatter_dimension=0, tiled=True
        ).astype(jnp.float32),
        lax.psum_scatter(
            acc_up.astype(jnp.bfloat16), "row", scatter_dimension=0, tiled=True
        ).astype(jnp.float32),
        lax.psum_scatter(
            acc_down.astype(jnp.bfloat16), "row", scatter_dimension=1, tiled=True
        ).astype(jnp.float32),
    )
    keyval_sum = lax.psum_scatter(acc_keyval, ("row", "col"), scatter_dimension=0, tiled=True)
    small_sums = lax.psum((acc_gain_one, acc_bias_query, acc_bias_keyval, acc_gain_two), "row")
    keyval_bias = lax.psum(small_sums[2], "col")
    return (
        outputs[None],
        grads_in[None],
        small_sums[0][None],
        weight_sums[0][None],
        small_sums[1][None],
        keyval_sum[None],
        keyval_bias[None],
        weight_sums[1][None],
        small_sums[3][None],
        weight_sums[2][None],
        weight_sums[3][None],
        weight_sums[4][None],
    )


def solution(mesh):
    in_specs = (
        P(None, "row", None),
        P(None, "row", None),
        P(),
        P("section", None),
        P("section", "row", "col"),
        P("section", "col"),
        P("section", ("row", "col"), None),
        P("section", None),
        P("section", "col", "row"),
        P("section", None),
        P("section", "row", "col"),
        P("section", "row", "col"),
        P("section", "col", "row"),
    )
    out_specs = (
        P("section", None, "row", None),
        P("section", None, "row", None),
        P("section", None),
        P("section", "row", "col"),
        P("section", "col"),
        P("section", ("row", "col"), None),
        P("section", None),
        P("section", "col", "row"),
        P("section", None),
        P("section", "row", "col"),
        P("section", "row", "col"),
        P("section", "col", "row"),
    )
    return jax.shard_map(local, mesh=mesh, in_specs=in_specs, out_specs=out_specs, check_vma=False)
```

profile of v0, /device:TPU:9, one launch (start us, length us, event | category | flops | bytes accessed | tf_op | source)
XLA Modules:
  0.0 2845.2 jit_solution(9086136617336831391)
XLA Ops:
  43.5 56.0 %all-gather.13.cloned.1.call-done = bf16[1,1536,512]{2,1,0:T(8,128)(2,1)} async-done(((bf16[1,96,512]{2,1,0:T(8,128)(2,1)}), bf16[1,1536,512]{2,1,0:T(8,128)(2,1)}) %all-gather.13.cloned.1.call-update) | async-done | bytes 1572880 | tf_op jit(solution)/shard_map/all_gather | solution.py:322
  141.7 46.1 %all-reduce.25.cloned.1.call-done = bf16[256,1536]{1,0:T(8,128)(2,1)} async-done(((bf16[256,1536]{1,0:T(8,128)(2,1)}), bf16[256,1536]{1,0:T(8,128)(2,1)}) %all-reduce.25.cloned.1.call-update) | async-done | bytes 786448 | tf_op jit(solution)/shard_map/psum | solution.py:67
  189.9 121.7 %all-gather.19.cloned.1.call-done = bf16[1,1536,2240]{1,2,0:T(8,128)(2,1)} async-done(((bf16[1,384,2240]{1,2,0:T(8,128)(2,1)}), bf16[1,1536,2240]{1,2,0:T(8,128)(2,1)}) %all-gather.19.cloned.1.call-update) | async-done | bytes 6881296 | tf_op jit(solution)/shard_map/all_gather | solution.py:327
  318.3 118.1 %all-gather.23.cloned.1.call-done = bf16[1,2240,1536]{2,1,0:T(8,128)(2,1)} async-done(((bf16[1,2240,384]{2,1,0:T(8,128)(2,1)}), bf16[1,2240,1536]{2,1,0:T(8,128)(2,1)}) %all-gather.23.cloned.1.call-update) | async-done | bytes 6881296 | tf_op jit(solution)/shard_map/all_gather | solution.py:329
  436.3 124.9 %all-gather.21.cloned.1.call-done = bf16[1,1536,2240]{1,2,0:T(8,128)(2,1)} async-done(((bf16[1,384,2240]{1,2,0:T(8,128)(2,1)}), bf16[1,1536,2240]{1,2,0:T(8,128)(2,1)}) %all-gather.21.cloned.1.call-update) | async-done | bytes 6881296 | tf_op jit(solution)/shard_map/all_gather | solution.py:328
  575.2 49.8 %all-reduce.27.cloned.1.call-done = bf16[256,1536]{1,0:T(8,128)(2,1)} async-done(((bf16[256,1536]{1,0:T(8,128)(2,1)}), bf16[256,1536]{1,0:T(8,128)(2,1)}) %all-reduce.27.cloned.1.call-update) | async-done | bytes 786448 | tf_op jit(solution)/shard_map/psum | solution.py:67
  685.6 53.6 %all-reduce.29.cloned.1.call-done = bf16[256,1536]{1,0:T(8,128)(2,1)} async-done(((bf16[256,1536]{1,0:T(8,128)(2,1)}), bf16[256,1536]{1,0:T(8,128)(2,1)}) %all-reduce.29.cloned.1.call-update) | async-done | bytes 786448 | tf_op jit(solution)/shard_map/psum | solution.py:67
  762.1 48.8 %all-reduce.31.cloned.1.call-done = bf16[256,1536]{1,0:T(8,128)(2,1)} async-done(((bf16[256,1536]{1,0:T(8,128)(2,1)}), bf16[256,1536]{1,0:T(8,128)(2,1)}) %all-reduce.31.cloned.1.call-update) | async-done | bytes 786448 | tf_op jit(solution)/shard_map/psum | solution.py:67
  856.0 50.7 %all-reduce.33.cloned.1.call-done = bf16[256,1536]{1,0:T(8,128)(2,1)} async-done(((bf16[256,1536]{1,0:T(8,128)(2,1)}), bf16[256,1536]{1,0:T(8,128)(2,1)}) %all-reduce.33.cloned.1.call-update) | async-done | bytes 786448 | tf_op jit(solution)/shard_map/psum | solution.py:67
  929.6 48.8 %all-reduce.35.cloned.1.call-done = bf16[256,1536]{1,0:T(8,128)(2,1)} async-done(((bf16[256,1536]{1,0:T(8,128)(2,1)}), bf16[256,1536]{1,0:T(8,128)(2,1)}) %all-reduce.35.cloned.1.call-update) | async-done | bytes 786448 | tf_op jit(solution)/shard_map/psum | solution.py:67
  1023.7 50.7 %all-reduce.37.cloned.1.call-done = bf16[256,1536]{1,0:T(8,128)(2,1)} async-done(((bf16[256,1536]{1,0:T(8,128)(2,1)}), bf16[256,1536]{1,0:T(8,128)(2,1)}) %all-reduce.37.cloned.1.call-update) | async-done | bytes 786448 | tf_op jit(solution)/shard_map/psum | solution.py:67
  1097.4 48.8 %all-reduce.39.cloned.1.call-done = bf16[256,1536]{1,0:T(8,128)(2,1)} async-done(((bf16[256,1536]{1,0:T(8,128)(2,1)}), bf16[256,1536]{1,0:T(8,128)(2,1)}) %all-reduce.39.cloned.1.call-update) | async-done | bytes 786448 | tf_op jit(solution)/shard_map/psum | solution.py:67
  1200.2 44.1 %all-reduce.41.cloned.1.call-done = bf16[256,1536]{1,0:T(8,128)(2,1)} async-done(((bf16[256,1536]{1,0:T(8,128)(2,1)}), bf16[256,1536]{1,0:T(8,128)(2,1)}) %all-reduce.41.cloned.1.call-update) | async-done | bytes 786448 | tf_op jit(solution)/shard_map/psum | solution.py:67
  1295.8 65.3 %all-reduce.61.cloned.1.call-done = (bf16[256,1536]{1,0:T(8,128)(2,1)}, bf16[256,1536]{1,0:T(8,128)(2,1)}) async-done(((bf16[256,1536]{1,0:T(8,128)(2,1)}, bf16[256,1536]{1,0:T(8,128)(2,1)}), (bf16[256,1536]{1,0:T(8,128)(2,1)}, bf16[256,1536]{1,0:T(8,128)(2,1)})) %all-reduce.61.cloned.1.call-update) | async-done | bytes 1572880 | tf_op jit(solution)/shard_map/psum | solution.py:71
  1554.9 87.1 %all-reduce.59.cloned.1.call-done = (bf16[256,1536]{1,0:T(8,128)(2,1)}, bf16[256,1536]{1,0:T(8,128)(2,1)}, bf16[256,1536]{1,0:T(8,128)(2,1)}, bf16[256,1536]{1,0:T(8,128)(2,1)}) async-done(((bf16[256,1536]{1,0:T(8,128)(2,1)}, bf16[256,1536]{1,0:T(8,128)(2,1)}, bf16[256,1536]{1,0:T(8,128)(2,1)}, bf16[256,1536]{1,0:T(8,128)(2,1)}), (bf16[256,1536]{1,0:T(8,128)(2,1)}, bf16[256,1536]{1,0:T(8,128)(2,1)}, ...) | async-done | bytes 3145744 | tf_op jit(solution)/shard_map/psum | solution.py:71
  1686.4 52.1 %all-reduce.45.cloned.1.call-done = bf16[256,1536]{1,0:T(8,128)(2,1)} async-done(((bf16[256,1536]{1,0:T(8,128)(2,1)}), bf16[256,1536]{1,0:T(8,128)(2,1)}) %all-reduce.45.cloned.1.call-update) | async-done | bytes 786448 | tf_op jit(solution)/shard_map/psum | solution.py:71
  1767.0 46.3 %all-reduce.47.cloned.1.call-done = bf16[256,1536]{1,0:T(8,128)(2,1)} async-done(((bf16[256,1536]{1,0:T(8,128)(2,1)}), bf16[256,1536]{1,0:T(8,128)(2,1)}) %all-reduce.47.cloned.1.call-update) | async-done | bytes 786448 | tf_op jit(solution)/shard_map/psum | solution.py:71
  1866.7 37.8 %all-reduce.49.cloned.1.call-done = bf16[256,1536]{1,0:T(8,128)(2,1)} async-done(((bf16[256,1536]{1,0:T(8,128)(2,1)}), bf16[256,1536]{1,0:T(8,128)(2,1)}) %all-reduce.49.cloned.1.call-update) | async-done | bytes 786448 | tf_op jit(solution)/shard_map/psum | solution.py:71
  1944.3 34.6 %all-reduce.51.cloned.1.call-done = bf16[256,1536]{1,0:T(8,128)(2,1)} async-done(((bf16[256,1536]{1,0:T(8,128)(2,1)}), bf16[256,1536]{1,0:T(8,128)(2,1)}) %all-reduce.51.cloned.1.call-update) | async-done | bytes 786448 | tf_op jit(solution)/shard_map/psum | solution.py:71
  2039.6 31.2 %all-reduce.53.cloned.1.call-done = bf16[256,1536]{1,0:T(8,128)(2,1)} async-done(((bf16[256,1536]{1,0:T(8,128)(2,1)}), bf16[256,1536]{1,0:T(8,128)(2,1)}) %all-reduce.53.cloned.1.call-update) | async-done | bytes 786448 | tf_op jit(solution)/shard_map/psum | solution.py:71
  2123.9 39.2 %all-reduce.57.cloned.1.call-done = (bf16[256,1536]{1,0:T(8,128)(2,1)}, bf16[256,1536]{1,0:T(8,128)(2,1)}) async-done(((bf16[256,1536]{1,0:T(8,128)(2,1)}, bf16[256,1536]{1,0:T(8,128)(2,1)}), (bf16[256,1536]{1,0:T(8,128)(2,1)}, bf16[256,1536]{1,0:T(8,128)(2,1)})) %all-reduce.57.cloned.1.call-update) | async-done | bytes 1572880 | tf_op jit(solution)/shard_map/psum | solution.py:67
  2452.4 123.7 %reduce-scatter.36.cloned.1.call-done = bf16[384,2240]{1,0:T(8,128)(2,1)} async-done(((bf16[1536,2240]{1,0:T(8,128)(2,1)}), bf16[384,2240]{1,0:T(8,128)(2,1)}) %reduce-scatter.36.cloned.1.call-update) | async-done | bytes 1720336
  2579.9 122.6 %reduce-scatter.38.cloned.1.call-done = bf16[384,2240]{1,0:T(8,128)(2,1)} async-done(((bf16[1536,2240]{1,0:T(8,128)(2,1)}), bf16[384,2240]{1,0:T(8,128)(2,1)}) %reduce-scatter.38.cloned.1.call-update) | async-done | bytes 1720336
  2713.9 124.3 %reduce-scatter.32.cloned.1.call-done = f32[96,512]{1,0:T(8,128)} async-done(((f32[1536,512]{1,0:T(8,128)}), f32[96,512]{1,0:T(8,128)}) %reduce-scatter.32.cloned.1.call-update) | async-done | bytes 196624 | tf_op jit(solution)/shard_map/reduce_scatter | solution.py:410
  (1398 shorter events, 1199.6 us)
Async XLA Ops:
  8.7 127.3 %all-gather.17.cloned.1.call-start = ((), (), s32[]{:S(2)}) async-start(), calls=%async_computation.35 | async-start | bytes 1474560 | tf_op jit(solution)/shard_map/all_gather | solution.py:326
  9.4 178.4 %all-reduce.25.cloned.1.call-start = ((), (), s32[]{:S(2)}) async-start(), calls=%async_computation.11 | async-start | bytes 1572864 | tf_op jit(solution)/shard_map/psum | solution.py:67
  138.8 172.8 %all-gather.19.cloned.1.call-start = ((), (), s32[]{:S(2)}) async-start(), calls=%async_computation.36 | async-start | bytes 8601600 | tf_op jit(solution)/shard_map/all_gather | solution.py:327
  139.4 296.9 %all-gather.23.cloned.1.call-start = ((), (), s32[]{:S(2)}) async-start(), calls=%async_computation.38 | async-start | bytes 8601600 | tf_op jit(solution)/shard_map/all_gather | solution.py:329
  140.0 421.2 %all-gather.21.cloned.1.call-start = ((), (), s32[]{:S(2)}) async-start(), calls=%async_computation.37 | async-start | bytes 8601600 | tf_op jit(solution)/shard_map/all_gather | solution.py:328
  140.7 484.2 %all-reduce.27.cloned.1.call-start = ((), (), s32[]{:S(2)}) async-start(), calls=%async_computation.12 | async-start | bytes 1572864 | tf_op jit(solution)/shard_map/psum | solution.py:67
  575.1 164.0 %all-reduce.29.cloned.1.call-start = ((), (), s32[]{:S(2)}) async-start(), calls=%async_computation.13 | async-start | bytes 1572864 | tf_op jit(solution)/shard_map/psum | solution.py:67
  762.1 144.6 %all-reduce.33.cloned.1.call-start = ((), (), s32[]{:S(2)}) async-start(), calls=%async_computation.15 | async-start | bytes 1572864 | tf_op jit(solution)/shard_map/psum | solution.py:67
  929.6 144.8 %all-reduce.37.cloned.1.call-start = ((), (), s32[]{:S(2)}) async-start(), calls=%async_computation.17 | async-start | bytes 1572864 | tf_op jit(solution)/shard_map/psum | solution.py:67
  1097.3 146.9 %all-reduce.41.cloned.1.call-start = ((), (), s32[]{:S(2)}) async-start(), calls=%async_computation.19 | async-start | bytes 1572864 | tf_op jit(solution)/shard_map/psum | solution.py:67
  1193.6 167.6 %all-reduce.61.cloned.1.call-start = ((), (), s32[]{:S(2)}) async-start(), calls=%async_computation.46 | async-start | bytes 3145728 | tf_op jit(solution)/shard_map/psum | solution.py:71
  1295.6 169.8 %reduce-scatter.20.cloned.1.call-start = ((), (), s32[]{:S(2)}) async-start(), calls=%async_computation.20 | async-start | bytes 655360 | tf_op jit(solution)/shard_map/reduce_scatter | solution.py:244
  1388.3 141.8 %all-reduce.43.cloned.1.call-start = ((), (), s32[]{:S(2)}) async-start(), calls=%async_computation.21 | async-start | bytes 1572864 | tf_op jit(solution)/shard_map/psum | solution.py:71
  1476.1 165.9 %all-reduce.59.cloned.1.call-start = ((), (), s32[]{:S(2)}) async-start(), calls=%async_computation.45 | async-start | bytes 6291456 | tf_op jit(solution)/shard_map/psum | solution.py:71
  1686.4 127.0 %all-reduce.47.cloned.1.call-start = ((), (), s32[]{:S(2)}) async-start(), calls=%async_computation.24 | async-start | bytes 1572864 | tf_op jit(solution)/shard_map/psum | solution.py:71
  2018.7 144.3 %all-reduce.57.cloned.1.call-start = ((), (), s32[]{:S(2)}) async-start(), calls=%async_computation.44 | async-start | bytes 3145728 | tf_op jit(solution)/shard_map/psum | solution.py:67
  2102.3 132.7 %reduce-scatter.28.cloned.1.call-start = ((), (), s32[]{:S(2)}) async-start(), calls=%async_computation.30 | async-start | bytes 655360 | tf_op jit(solution)/shard_map/reduce_scatter | solution.py:244
  2177.5 221.0 %reduce-scatter.34.cloned.1.call-start = ((), (), s32[]{:S(2)}) async-start(), calls=%async_computation.39 | async-start | bytes 1474560
  2192.5 208.1 %reduce-scatter.30.cloned.1.call-start = ((), (), s32[]{:S(2)}) async-start(), calls=%async_computation.31 | async-start | bytes 1474560 | tf_op jit(solution)/shard_map/reduce_scatter | solution.py:394
  2214.0 188.3 %all-reduce.55.cloned.1.call-start = ((), (), s32[]{:S(2)}) async-start(), calls=%async_computation.43 | async-start | bytes 3145728 | tf_op jit(solution)/shard_map/psum | solution.py:67
  2242.4 207.2 %reduce-scatter.40.cloned.1.call-start = ((), (), s32[]{:S(2)}) async-start(), calls=%async_computation.42 | async-start | bytes 8847360
  2272.7 303.4 %reduce-scatter.36.cloned.1.call-start = ((), (), s32[]{:S(2)}) async-start(), calls=%async_computation.40 | async-start | bytes 8847360
  2317.1 385.5 %reduce-scatter.38.cloned.1.call-start = ((), (), s32[]{:S(2)}) async-start(), calls=%async_computation.41 | async-start | bytes 8847360
  2362.5 475.7 %reduce-scatter.32.cloned.1.call-start = ((), (), s32[]{:S(2)}) async-start(), calls=%async_computation.32 | async-start | bytes 3342336 | tf_op jit(solution)/shard_map/reduce_scatter | solution.py:410
  (411 other events, 6729.4 us)
Sparse Core Ops, SparseCore 0:
  43.3 56.1 all-gather.12
  189.3 122.2 all-gather.18
  313.1 123.1 all-gather.22
  438.0 123.1 all-gather.20
  575.2 49.6 all-reduce.26
  685.6 53.4 all-reduce.28
  762.2 48.7 all-reduce.30
  856.0 50.5 all-reduce.32
  929.7 48.7 all-reduce.34
  1023.8 50.5 all-reduce.36
  1097.5 48.7 all-reduce.38
  1193.7 50.5 all-reduce.40
  1295.7 65.4 all-reduce.60
  1476.3 53.7 all-reduce.42
  1554.8 87.2 all-reduce.58
  1686.5 51.9 all-reduce.44
  1852.5 51.9 all-reduce.48
  2018.9 51.8 all-reduce.52
  2102.5 60.5 all-reduce.56
  2261.5 61.7 all-reduce.54
  2325.5 124.0 reduce-scatter.39
  2452.1 124.0 reduce-scatter.35
  2578.5 124.0 reduce-scatter.37
  2708.7 129.4 reduce-scatter.31
  (12 shorter events, 355.9 us)
where the time goes:
time: 2860 us; the launch traced here: 2850 us
  waiting for transfers between devices  1730 us (60%)
  matrix products  506 us (18%)
  other arithmetic  201 us (7%)
  local copies, waits for them, and re-layouts  196 us (7%)
  blocking collectives  167 us (6%)
    psum x11, waiting for transfers between devices, column_sum(): return lax.psum(partial_sum.astype(jnp.bfloat16), 'col').astype(jnp.float32)  480 us
    psum x8, waiting for transfers between devices, column_back(): return lax.psum(partial_sum.astype(jnp.bfloat16), 'col').astype(jnp.float32)  364 us
    unnamed x40, waiting for transfers between devices  266 us
    all_gather x10, blocking collectives, forward_layer(): gathered = lax.all_gather(local_pair, 'row', axis=0, tiled=True)  142 us
    all_gather x1, waiting for transfers between devices, local(): lax.all_gather(w_up[0], 'row', axis=0, tiled=True)  125 us
    reduce_scatter x1, waiting for transfers between devices, local(): lax.psum_scatter(acc_keyval, ('row', 'col'), scatter_dimension=0, tiled=T...  124 us
    all_gather x1, waiting for transfers between devices, local(): lax.all_gather(w_gate[0], 'row', axis=0, tiled=True)  122 us
    unnamed x803, local copies, waits for them, and re-layouts  120 us
  transfers between devices with their start and end apart: 49, of which 39 were waited for; matrix products, arithmetic and copies ran while one was open for 17% of the time, Pallas kernels for 0%

commit v1 on v0

v1 whole, which is shorter than its diff:
```python
import functools
import math

import jax
import jax.numpy as jnp
from jax import lax
from jax.experimental import pallas as pl
from jax.experimental.pallas import tpu as pltpu
from jax.sharding import PartitionSpec as P

HEADS = 12
KV = 2
HEAD = 128

EPS = 1e-06
THETA = 1000000.0

F32 = jnp.float32
BF16 = jnp.bfloat16

COL_LOW = ("col", 1)
COL_HIGH = ("col", 2)
ROW_LOW = ("row", 1)
SECTION = ("section", 1)


def swap(value, axis, flip):
    pairs = [(i, i ^ flip) for i in range(lax.axis_size(axis))]
    return lax.ppermute(value, axis, pairs)


def bit_of(index, bit):
    return (index >> bit) & 1


def pick(array, index, axis=0):
    return lax.dynamic_index_in_dim(array, index, axis, keepdims=False)


def ordered(mine, other, bit, axis):
    first = jnp.where(bit == 0, mine, other)
    second = jnp.where(bit == 0, other, mine)
    return jnp.concatenate([first, second], axis=axis)


def row_bits():
    return lax.axis_size("row").bit_length() - 1


def norm_backward(stream, inverse, gain, gradient):
    inner = jnp.mean(gradient * gain * stream, axis=-1, keepdims=True)
    d_stream = gain * gradient * inverse - stream * (inverse * inverse * inverse) * inner
    return (d_stream, jnp.sum(gradient * stream * inverse, axis=0, keepdims=True))


def dot(left, right, left_dim, right_dim):
    return lax.dot_general(
        left, right, (((left_dim,), (right_dim,)), ((), ())), preferred_element_type=F32
    )


def layout(lengths, place, row_count):
    section, row, low, high = place
    rows = lax.axis_size("row")
    half = row_count // 2
    inside = jnp.arange(row_count, dtype=jnp.int32)
    inside = (((inside // half) ^ low) * half) + inside % half
    own_index = row * row_count + inside
    key_index = ((jnp.arange(rows, dtype=jnp.int32) ^ row) * row_count)[:, None] + inside[None, :]
    slots = 2 * section + (jnp.arange(2, dtype=jnp.int32) ^ high)
    picked = jnp.stack([pick(lengths, slots[0]), pick(lengths, slots[1])])
    ends = jnp.cumsum(picked, axis=1)
    starts = ends - picked
    inside_piece = (own_index[None, None, :] >= starts[:, :, None]) & (
        own_index[None, None, :] < ends[:, :, None]
    )
    first = jnp.sum(jnp.where(inside_piece, starts[:, :, None], 0), axis=1)
    inverse = THETA ** (-(jnp.arange(HEAD // 2, dtype=F32) * 2.0 / HEAD))
    angle = (own_index[None, :] - first).astype(F32).reshape(-1, 1) * inverse
    cosine, sine = jnp.cos(angle), jnp.sin(angle)
    return (
        jnp.concatenate([cosine, cosine], axis=1),
        jnp.concatenate([-sine, sine], axis=1),
        first,
        own_index[None, :],
        key_index.reshape(-1, 1),
    )


MESH = pl.DeviceIdType.MESH
VMEM_LIMIT = 60 * 1024 * 1024


def partner_of(way):
    axis, flip = way
    return {axis: lax.axis_index(axis) ^ flip}


def enter(ways):
    barrier = pltpu.get_barrier_semaphore()
    for way in ways:
        pl.semaphore_signal(barrier, inc=1, device_id=partner_of(way), device_id_type=MESH)
    pl.semaphore_wait(barrier, len(ways))


class Links:
    def __init__(self, send, recv):
        self.send, self.recv, self.used = send, recv, 0

    def copy(self, source, target, way):
        slot = self.used
        self.used += 1
        return pltpu.make_async_remote_copy(
            src_ref=source,
            dst_ref=target,
            send_sem=self.send.at[slot],
            recv_sem=self.recv.at[slot],
            device_id=partner_of(way),
            device_id_type=MESH,
        )


def gather_copies(links, blocks, a, b, sides=True, own=None):
    h = blocks.shape[2] // 2
    own = blocks.at[0, 0] if own is None else own
    copies = {
        "a": links.copy(own, blocks.at[1, 0], a),
        "b": links.copy(own, blocks.at[2, 0], b),
        "ab": links.copy(blocks.at[1, 0, pl.ds(0, h)], blocks.at[3, 0, pl.ds(0, h)], b),
        "ba": links.copy(blocks.at[2, 0, pl.ds(h, h)], blocks.at[3, 0, pl.ds(h, h)], a),
    }
    if sides:
        copies["s0"] = links.copy(own, blocks.at[0, 1], SECTION)
        for k in (1, 2, 3):
            copies[f"s{k}"] = links.copy(blocks.at[k, 0], blocks.at[k, 1], SECTION)
    return copies


def ffn_exchange(links, a, b, blocks, gathers, buffers, step, moves):
    mine, side_out, side_in, corner_out, corner_in, edge_out, edge_in = buffers
    n = blocks.shape[2]
    h = n // 2
    gather = gather_copies(links, blocks, a, b) if gathers else {}
    sides = [links.copy(side_out.at[k], side_in.at[k], SECTION) for k in range(4)]
    corner_b, corner_a, edge_a, edge_b = scatter_copies(
        links, corner_out, corner_in, edge_out, edge_in, a, b
    )
    lead, rest = moves[:1], moves[1:]

    def start(*names):
        for name in names:
            if gathers:
                gather[name].start()

    def wait(*names):
        for name in names:
            if gathers:
                gather[name].wait_recv()

    start("a", "b", "s0")
    for move in lead:
        move.advance()
    wait("s0")
    step(0)
    sides[0].start()
    wait("a")
    start("ab", "s1")
    wait("b")
    start("ba", "s2")
    wait("s1")
    step(1)
    sides[1].start()
    wait("ab", "ba")
    start("s3")
    wait("s3")
    step(3)
    sides[3].start()
    sides[3].wait_recv()
    total = mine[3] + side_in[3].astype(F32)
    corner_out[...] = total.astype(BF16).reshape(corner_out.shape)
    corner_b.start()
    corner_a.start()
    for move in moves:
        move.advance()
    wait("s2")
    step(2)
    sides[2].start()
    sides[1].wait_recv()
    corner_b.wait_recv()
    edge_out[0, :h] = (mine[1, :h] + side_in[1, :h].astype(F32) + corner_in[0].astype(F32)).astype(BF16)
    edge_out[0, h:] = (mine[1, h:] + side_in[1, h:].astype(F32)).astype(BF16)
    edge_a.start()
    sides[2].wait_recv()
    corner_a.wait_recv()
    edge_out[1, :h] = (mine[2, :h] + side_in[2, :h].astype(F32)).astype(BF16)
    edge_out[1, h:] = (mine[2, h:] + side_in[2, h:].astype(F32) + corner_in[1].astype(F32)).astype(BF16)
    edge_b.start()
    for move in rest:
        move.advance()
    sides[0].wait_recv()
    total = mine[0] + side_in[0].astype(F32)
    edge_a.wait_recv()
    edge_b.wait_recv()
    total = total + edge_in[0].astype(F32) + edge_in[1].astype(F32)
    for move in rest:
        move.advance()
    for move in moves:
        move.end()
    wait_all([], [*gather.values(), *sides, corner_a, corner_b, edge_a, edge_b])
    return total


def hidden_tiles(hidden):
    return [(at, min(384, hidden - at)) for at in range(0, hidden, 384)]


def padded(hidden):
    return -(-hidden // 128) * 128


def width_tiles(width):
    return [(at, 512) for at in range(0, width, 512)]


def load_copies(sources, targets, sems):
    each = len(sources) // len(targets)
    copies = []
    for i, source in enumerate(sources):
        rows, columns = source.shape[1:]
        for block in range(source.shape[0]):
            place = (pl.ds((i % each) * rows, rows), pl.ds(block * columns, columns))
            copies.append(
                pltpu.make_async_copy(
                    source.at[block], targets[i // each].at[place], sems.at[len(copies)]
                )
            )
    return copies


def load_count(sources):
    return sum(source.shape[0] for source in sources)


def pad_weights(sources, targets):
    filled = sources[0].shape[1] * (len(sources) // len(targets))
    for target in targets:
        if filled < target.shape[0]:
            target[filled:] = jnp.zeros((target.shape[0] - filled, target.shape[1]), target.dtype)


def save(started, sems, sources, targets):
    for source, target in zip(sources, targets, strict=True):
        started.append(pltpu.make_async_copy(source, target, sems.at[len(started)]))
        started[-1].start()


def put_partial(k, at, size, value, mine, side_out):
    n = mine.shape[1]
    mine[k, :, pl.ds(at, size)] = value[:n]
    side_out[k, :, pl.ds(at, size)] = value[n:].astype(BF16)


def ffn_forward_kernel(
    a, b, run,
    second_ref, gain_ref, *refs,
):
    weights_hbm, refs = refs[:-23], refs[-23:]
    (
        result_ref, blocks_hbm, gate_hbm, up_hbm, act_hbm,
        w_gate, w_up, w_down, blocks, gate_out, up_out, act_out, *buffers,
        load_sem, save_sem, send, recv,
    ) = refs
    loads = load_copies(weights_hbm, (w_gate, w_up, w_down), load_sem)
    for copy in loads:
        copy.start()
    pad_weights(weights_hbm, (w_gate, w_up, w_down))
    second = second_ref[...]
    inverse = lax.rsqrt(jnp.mean(second * second, axis=-1, keepdims=True) + EPS)
    blocks[0, 0] = (second * inverse * gain_ref[...]).astype(BF16)
    run.enter()
    n = blocks.shape[2]
    width = blocks.shape[3]
    hidden = w_gate.shape[0]
    saves = []

    def step(k):
        if k == 0:
            for copy in loads:
                copy.wait()
        x = blocks[k].reshape(2 * n, width)
        rows = pl.ds(k * 2 * n, 2 * n)
        for at, size in hidden_tiles(hidden):
            gate = dot(x, w_gate[pl.ds(at, size)], 1, 1)
            up = dot(x, w_up[pl.ds(at, size)], 1, 1)
            act = gate / (1.0 + jnp.exp(-gate)) * up
            gate_out[rows, pl.ds(at, size)] = gate.astype(BF16)
            up_out[rows, pl.ds(at, size)] = up.astype(BF16)
            act_out[rows, pl.ds(at, size)] = act.astype(BF16)
        save(saves, save_sem, (blocks.at[k], gate_out.at[rows], up_out.at[rows], act_out.at[rows]),
             (blocks_hbm.at[k], gate_hbm.at[rows], up_hbm.at[rows], act_hbm.at[rows]))
        act = act_out[rows]
        for at, size in width_tiles(width):
            put_partial(k, at, size, dot(act, w_down[:, pl.ds(at, size)], 1, 0), *buffers[:2])

    total = ffn_exchange(Links(send, recv), a, b, blocks, True, buffers, step, run.moves)
    result_ref[...] = second_ref[...] + total
    for copy in saves:
        copy.wait()


def ffn_backward_kernel(
    gathers, a, b, run,
    grad_ref, second_ref, gain_ref, gate_hbm, up_hbm, *refs,
):
    weights_hbm, refs = refs[:-24], refs[-24:]
    (
        result_ref, d_gain_ref, blocks_hbm, d_gate_hbm, d_up_hbm,
        w_gate, w_up, w_down, blocks, gate_in, up_in, d_gate_out, d_up_out, *buffers,
        load_sem, save_sem, send, recv,
    ) = refs
    more = [(gate_hbm, gate_in), (up_hbm, up_in)]
    if not gathers:
        gathered, *weights_hbm = weights_hbm
        more.append((gathered, blocks))
    loads = load_copies(weights_hbm, (w_gate, w_up, w_down), load_sem)
    pad_weights(weights_hbm, (w_gate, w_up, w_down))
    for source, target in more:
        loads.append(pltpu.make_async_copy(source, target, load_sem.at[len(loads)]))
    for copy in loads:
        copy.start()
    if gathers:
        blocks[0, 0] = grad_ref[...]
    run.enter()
    n = blocks.shape[2]
    width = blocks.shape[3]
    hidden = w_gate.shape[0]
    saves = []

    def step(k):
        if k == 0:
            for copy in loads:
                copy.wait()
        g = blocks[k].reshape(2 * n, width)
        rows = pl.ds(k * 2 * n, 2 * n)
        for at, size in hidden_tiles(hidden):
            d_act = dot(g, w_down[pl.ds(at, size)], 1, 1)
            gate = gate_in[rows, pl.ds(at, size)].astype(F32)
            up = up_in[rows, pl.ds(at, size)].astype(F32)
            sigma = 1.0 / (1.0 + jnp.exp(-gate))
            d_gate_out[rows, pl.ds(at, size)] = (
                d_act * up * sigma * (1.0 + gate * (1.0 - sigma))
            ).astype(BF16)
            d_up_out[rows, pl.ds(at, size)] = (d_act * gate * sigma).astype(BF16)
        save(saves, save_sem, (blocks.at[k], d_gate_out.at[rows], d_up_out.at[rows]),
             (blocks_hbm.at[k], d_gate_hbm.at[rows], d_up_hbm.at[rows]))
        d_gate = d_gate_out[rows]
        d_up = d_up_out[rows]
        for at, size in width_tiles(width):
            value = dot(d_gate, w_gate[:, pl.ds(at, size)], 1, 0)
            value = value + dot(d_up, w_up[:, pl.ds(at, size)], 1, 0)
            put_partial(k, at, size, value, *buffers[:2])

    d_normed = ffn_exchange(Links(send, recv), a, b, blocks, gathers, buffers, step, run.moves)
    second = second_ref[...]
    inverse = lax.rsqrt(jnp.mean(second * second, axis=-1, keepdims=True) + EPS)
    d_second, d_gain = norm_backward(second, inverse, gain_ref[...], d_normed)
    d_gain_ref[...] = d_gain
    result_ref[...] = grad_ref[...].astype(F32) + d_second
    for copy in saves:
        copy.wait()


class Run:
    def __init__(self, ways, moves):
        self.ways, self.moves = ways, moves

    def enter(self):
        enter(self.ways)


def kernel_call(kernel, collective_id, ways, operands, after, outs, scratch, flops, moves=()):
    vmem = pl.BlockSpec(memory_space=pltpu.VMEM)
    hbm = pl.BlockSpec(memory_space=pl.ANY)
    moved_in = [array for move in moves for array in move.operands]
    moved_out = [out for move in moves for out in move.outs]
    every = list(ways)
    for move in moves:
        every += [way for way in move.ways if way not in every]

    def body(*refs):
        refs = list(refs)

        def take(count):
            taken, refs[:] = refs[:count], refs[count:]
            return taken

        own_in = take(len(operands))
        take(len(after))
        moves_in = [take(len(move.operands)) for move in moves]
        token = take(1)[0]
        own_out = take(len(outs))
        moves_out = [take(len(move.outs)) for move in moves]
        own_scratch = take(len(scratch))
        for move, sources, targets in zip(moves, moves_in, moves_out, strict=True):
            move.bind(sources, targets, take(len(move.scratch)))
        token[...] = jnp.zeros_like(token)
        kernel(Run(every, moves), *own_in, *own_out, *own_scratch)

    token, *results = pl.pallas_call(
        body,
        out_shape=[
            jax.ShapeDtypeStruct((8, 128), jnp.int32),
            *[jax.ShapeDtypeStruct(shape, dtype) for shape, dtype, _ in outs],
            *[jax.ShapeDtypeStruct(shape, BF16) for shape in moved_out],
        ],
        in_specs=[vmem if inside else hbm for _, inside in operands]
        + [hbm] * (len(after) + len(moved_in)),
        out_specs=[vmem]
        + [vmem if inside else hbm for _, _, inside in outs]
        + [hbm] * len(moved_out),
        scratch_shapes=[*scratch, *[ref for move in moves for ref in move.scratch]],
        compiler_params=pltpu.CompilerParams(
            collective_id=collective_id, has_side_effects=True, vmem_limit_bytes=VMEM_LIMIT
        ),
        cost_estimate=pl.CostEstimate(flops=flops, bytes_accessed=16 << 20, transcendentals=1 << 20),
    )(*[array for array, _ in operands], *after, *moved_in)
    results, moved = results[: len(outs)], results[len(outs) :]
    lists = []
    for move in moves:
        lists.append(moved[: len(move.outs)])
        moved = moved[len(move.outs) :]
    return token[0, 0], results, lists


def remote(source, target, send, recv, way):
    return pltpu.make_async_remote_copy(
        src_ref=source,
        dst_ref=target,
        send_sem=send,
        recv_sem=recv,
        device_id=partner_of(way),
        device_id_type=MESH,
    )


def row_hops(bits):
    hops, known = [], [0]
    for bit in reversed(range(bits)):
        step = 1 << bit
        hops += [(slot, slot | step, bit) for slot in known]
        known += [slot | step for slot in known]
    return hops


class Move:
    def __init__(self, operands, outs, scratch, ways):
        self.operands, self.outs, self.scratch, self.ways = operands, outs, scratch, ways
        self.steps, self.at = [], 0

    def advance(self):
        if self.at < len(self.steps):
            self.steps[self.at]()
            self.at += 1

    def end(self):
        while self.at < len(self.steps):
            self.advance()


def semaphores(*counts):
    return [pltpu.SemaphoreType.DMA((count,)) for count in counts]


def wait_all(arriving, leaving):
    for copy in arriving:
        copy.wait_recv()
    for copy in leaving:
        copy.wait_send()


class FfnGather(Move):
    def __init__(self, part, across):
        rows = lax.axis_size("row")
        self.flips, self.across = list(range(1, rows)), across
        outs = [(rows, *part.shape[1:])] * 2
        ways = [("row", flip) for flip in self.flips] + [across]
        super().__init__([part], outs, semaphores(rows, rows, rows, rows, 1), ways)

    def bind(self, sources, targets, scratch):
        (part,), (own, other) = sources, targets
        row_send, row_recv, far_send, far_recv, local_sem = scratch
        row = lax.axis_index("row")
        near = part.at[row & 1]
        local = pltpu.make_async_copy(near, own.at[row], local_sem.at[0])
        hops = {
            flip: remote(
                part.at[(row ^ flip) & 1], own.at[row], row_send.at[flip], row_recv.at[flip], ("row", flip)
            )
            for flip in self.flips
        }
        far = [
            remote(
                own.at[row ^ flip] if flip else near,
                other.at[row ^ flip],
                far_send.at[flip],
                far_recv.at[flip],
                self.across,
            )
            for flip in [0] + self.flips
        ]

        def start():
            local.start()
            for flip in self.flips:
                hops[flip].start()

        def forward():
            far[0].start()
            for flip in self.flips:
                hops[flip].wait_recv()
                far[flip].start()

        def finish():
            local.wait()
            wait_all(far, [*hops.values(), *far])

        self.steps = [start, forward, finish]


class AttnGather(Move):
    def __init__(self, part):
        rows = lax.axis_size("row")
        self.bits = rows.bit_length() - 1
        ways = [("row", 1 << bit) for bit in range(self.bits)] + [SECTION]
        super().__init__([part], [(2, rows, *part.shape)], semaphores(rows, rows, rows, rows, 1), ways)

    def bind(self, sources, targets, scratch):
        (part,), (blocks,) = sources, targets
        row_send, row_recv, side_send, side_recv, local_sem = scratch
        section, row = lax.axis_index("section"), lax.axis_index("row")

        def place(slot):
            return blocks.at[section, row ^ slot]

        def source(slot):
            return place(slot) if slot else part

        local = pltpu.make_async_copy(part, place(0), local_sem.at[0])
        hops = [
            (slot, filled, remote(source(slot), place(slot), row_send.at[filled], row_recv.at[filled], ("row", 1 << bit)))
            for slot, filled, bit in row_hops(self.bits)
        ]
        sides = [
            remote(source(slot), place(slot), side_send.at[slot], side_recv.at[slot], SECTION)
            for slot in range(1 << self.bits)
        ]
        arrived = {0}

        def arrive(slot):
            if slot not in arrived:
                arrived.add(slot)
                for _, filled, copy in hops:
                    if filled == slot:
                        copy.wait_recv()
                sides[slot].start()

        def start():
            local.start()
            for slot, _, copy in hops:
                if slot == 0:
                    copy.start()
            sides[0].start()

        def forward():
            for slot, _, copy in hops:
                if slot:
                    arrive(slot)
                    copy.start()

        def finish():
            for slot in range(len(sides)):
                arrive(slot)
            local.wait()
            wait_all(sides, [copy for _, _, copy in hops] + sides)

        self.steps = [start, forward, finish]


class TokenGather(Move):
    def __init__(self, own, a, b, sides):
        self.a, self.b, self.sides = a, b, sides
        ways = [a, b] + ([SECTION] if sides else [])
        super().__init__([own], [(4, 1 + sides, *own.shape)], semaphores(8, 8, 1), ways)

    def bind(self, sources, targets, scratch):
        (own,), (blocks,) = sources, targets
        send, recv, local_sem = scratch
        local = pltpu.make_async_copy(own, blocks.at[0, 0], local_sem.at[0])
        copies = gather_copies(Links(send, recv), blocks, self.a, self.b, self.sides, own)
        sides = [name for name in ("s0", "s1", "s2", "s3") if self.sides]

        def start():
            local.start()
            for name in ["a", "b"] + sides[:1]:
                copies[name].start()

        def forward():
            copies["a"].wait_recv()
            copies["ab"].start()
            copies["b"].wait_recv()
            copies["ba"].start()
            for name in sides[1:3]:
                copies[name].start()

        def last():
            copies["ab"].wait_recv()
            copies["ba"].wait_recv()
            for name in sides[3:]:
                copies[name].start()

        def finish():
            local.wait()
            wait_all([copies[name] for name in sides], copies.values())

        self.steps = [start, forward, last, finish]


class Across(Move):
    def __init__(self, grad, n, way):
        self.n, self.way = n, way
        super().__init__([grad], [(n, grad.shape[1])], semaphores(1, 1), [way])

    def bind(self, sources, targets, scratch):
        (grad,), (arrived,) = sources, targets
        send, recv = scratch
        copy = remote(grad.at[pl.ds(self.n, self.n)], arrived, send.at[0], recv.at[0], self.way)
        self.steps = [copy.start, lambda: wait_all([copy], [copy])]


class Rows(Move):
    def __init__(self, total):
        rows = total.shape[0]
        self.flips = list(range(1, rows))
        ways = [("row", flip) for flip in self.flips]
        super().__init__([total], [total.shape], semaphores(rows, rows), ways)

    def bind(self, sources, targets, scratch):
        (total,), (arrived,) = sources, targets
        send, recv = scratch
        copies = row_copies(total, arrived, send, recv, self.flips)

        def start():
            for copy in copies:
                copy.start()

        self.steps = [start, lambda: wait_all(copies, copies)]


def row_copies(total, arrived, send, recv, flips):
    row = lax.axis_index("row")
    return [
        remote(total.at[row ^ flip], arrived.at[flip], send.at[flip], recv.at[flip], ("row", flip))
        for flip in flips
    ]


class GradScatter(Move):
    def __init__(self, grad, n, way):
        rows, width = lax.axis_size("row"), grad.shape[1]
        self.n, self.way, self.flips = n, way, list(range(1, rows))
        shape = (rows, n, width // rows)
        scratch = [pltpu.VMEM((n, width), BF16), pltpu.VMEM((n, width), BF16), pltpu.VMEM(shape, BF16)]
        scratch += semaphores(1, 1, 1, 1, rows, rows)
        ways = [way] + [("row", flip) for flip in self.flips]
        super().__init__([grad], [shape[1:], shape], scratch, ways)

    def bind(self, sources, targets, scratch):
        (grad,), (own, arrived) = sources, targets
        mine, theirs, total, local_sem, own_sem, far_send, far_recv, row_send, row_recv = scratch
        n, row = self.n, lax.axis_index("row")
        depth = total.shape[2]
        local = pltpu.make_async_copy(grad.at[pl.ds(0, n)], mine, local_sem.at[0])
        far = remote(grad.at[pl.ds(n, n)], theirs, far_send.at[0], far_recv.at[0], self.way)
        keep = pltpu.make_async_copy(total.at[row], own, own_sem.at[0])
        copies = row_copies(total, arrived, row_send, row_recv, self.flips)

        def start():
            local.start()
            far.start()

        def forward():
            local.wait()
            far.wait_recv()
            for block in range(total.shape[0]):
                at = slice(block * depth, (block + 1) * depth)
                total[block] = (mine[:, at].astype(F32) + theirs[:, at].astype(F32)).astype(BF16)
            for copy in copies + [keep]:
                copy.start()

        def finish():
            keep.wait()
            wait_all(copies, copies + [far])

        self.steps = [start, forward, finish]


class AttnScatter(Move):
    def __init__(self, grad):
        rows, width, m = lax.axis_size("row"), grad.shape[1], grad.shape[0] // 2
        self.bits, self.m = rows.bit_length() - 1, m
        blocks = (rows, m, width // rows)
        scratch = [
            pltpu.VMEM((m, width), BF16),
            pltpu.VMEM((m, width), BF16),
            pltpu.VMEM(blocks, F32),
            pltpu.VMEM(blocks, BF16),
            pltpu.VMEM(blocks, BF16),
        ]
        scratch += semaphores(1, 1, 1, 1, rows, rows)
        ways = [SECTION] + [("row", 1 << bit) for bit in range(self.bits)]
        super().__init__([grad], [blocks[1:]], scratch, ways)

    def bind(self, sources, targets, scratch):
        (grad,), (out,) = sources, targets
        mine, theirs, total, going, coming, local_sem, out_sem, side_send, side_recv, send, recv = scratch
        m, row, section = self.m, lax.axis_index("row"), lax.axis_index("section")
        depth = total.shape[2]
        local = pltpu.make_async_copy(
            grad.at[pl.ds(pl.multiple_of(section * m, m), m)], mine, local_sem.at[0]
        )
        side = remote(
            grad.at[pl.ds(pl.multiple_of((1 - section) * m, m), m)],
            theirs,
            side_send.at[0],
            side_recv.at[0],
            SECTION,
        )
        keep = pltpu.make_async_copy(going.at[0], out, out_sem.at[0])
        hops = [
            (slot, filled, remote(going.at[filled], coming.at[filled], send.at[filled], recv.at[filled], ("row", 1 << bit)))
            for slot, filled, bit in reversed(row_hops(self.bits))
        ]

        def start():
            local.start()
            side.start()

        def sum_sides():
            local.wait()
            side.wait_recv()
            for block in range(total.shape[0]):
                at = slice(block * depth, (block + 1) * depth)
                total[row ^ block] = mine[:, at].astype(F32) + theirs[:, at].astype(F32)
            send_bit(0)

        def send_bit(bit):
            for slot, filled, copy in hops:
                if filled - slot == 1 << bit:
                    going[filled] = total[filled].astype(BF16)
                    copy.start()

        def add_bit(bit):
            for slot, filled, copy in hops:
                if filled - slot == 1 << bit:
                    copy.wait_recv()
                    total[slot] = total[slot] + coming[filled].astype(F32)

        def hop(bit):
            def step():
                add_bit(bit - 1)
                send_bit(bit)

            return step

        def finish():
            add_bit(self.bits - 1)
            going[0] = total[0].astype(BF16)
            keep.start()
            keep.wait()
            wait_all([], [copy for _, _, copy in hops] + [side])

        self.steps = [start, sum_sides, *[hop(bit) for bit in range(1, self.bits)], finish]


def move_kernel(run):
    run.enter()
    while any(move.at < len(move.steps) for move in run.moves):
        for move in run.moves:
            move.advance()


def loadable(blocks):
    if blocks.shape[-1] % 128 == 0:
        return blocks
    whole = jnp.swapaxes(blocks, -3, -2)
    return whole.reshape(*whole.shape[:-3], 1, whole.shape[-3], -1)


def ffn_call(kernel, a, b, collective_id, operands, big, weights, after, sizes, small_outs, hidden_outs, moves=()):
    n, width, _, hidden = sizes
    tokens = 8 * n
    hidden = padded(hidden)
    weights = [loadable(half) for halves in weights for half in halves]
    token, outs, moved = kernel_call(
        functools.partial(kernel, a, b),
        collective_id,
        (a, b, SECTION),
        [(array, True) for array in operands] + [(array, False) for array in (*big, *weights)],
        after,
        [(shape, F32, True) for shape in small_outs]
        + [((4, 2, n, width), BF16, False)]
        + [((tokens, hidden), BF16, False)] * hidden_outs,
        [
            *[pltpu.VMEM((hidden, width), BF16) for _ in range(3)],
            pltpu.VMEM((4, 2, n, width), BF16),
            *[pltpu.VMEM((tokens, hidden), BF16) for _ in range(min(len(big), 2) + hidden_outs)],
            pltpu.VMEM((4, n, width), F32),
            pltpu.VMEM((4, n, width), BF16),
            pltpu.VMEM((4, n, width), BF16),
            pltpu.VMEM((2, n // 2, width), BF16),
            pltpu.VMEM((2, n // 2, width), BF16),
            pltpu.VMEM((2, n, width), BF16),
            pltpu.VMEM((2, n, width), BF16),
            pltpu.SemaphoreType.DMA((load_count(weights) + len(big),)),
            pltpu.SemaphoreType.DMA((4 * (1 + hidden_outs),)),
            pltpu.SemaphoreType.DMA((16,)),
            pltpu.SemaphoreType.DMA((16,)),
        ],
        3 * 2 * tokens * width * hidden,
        moves,
    )
    at = len(small_outs)
    outs[at] = outs[at].reshape(tokens, width)
    return token, outs, moved


def turn(vectors, cosine, sine):
    return vectors * cosine + pltpu.roll(vectors, HEAD // 2, 1) * sine


def scatter_copies(links, corner_out, corner_in, edge_out, edge_in, a, b):
    return (
        links.copy(corner_out.at[0], corner_in.at[0], b),
        links.copy(corner_out.at[1], corner_in.at[1], a),
        links.copy(edge_out.at[0], edge_in.at[0], a),
        links.copy(edge_out.at[1], edge_in.at[1], b),
    )


def seen(start_ref, own_ref, key_ref, slot):
    key = key_ref[...]
    visible = (key >= start_ref[pl.ds(slot, 1)]) & (key <= own_ref[...])
    return jnp.where(visible, 0.0, -1e30)


def attention_weights(blocks, weights, sems):
    loads = load_copies([blocks.at[0], blocks.at[1]], [weights], sems)
    for copy in loads:
        copy.start()
    heads_width = (weights.shape[0] - 2 * HEAD) // 2
    return (
        loads,
        weights.at[pl.ds(0, heads_width)],
        weights.at[pl.ds(heads_width, heads_width)],
        weights.at[pl.ds(2 * heads_width, 2 * HEAD)],
    )


def attention_forward_kernel(
    gathers, run,
    entry_ref, gain_ref, b_query_ref, b_pair_ref, cos_ref, sin_ref, start_ref, own_ref, key_ref,
    weights_hbm,
    second_ref, normed, query, mixed, lse_ref, kv_hbm, entry_hbm,
    weights, entry, kv, bias, partial, corner_out, corner_in, edge_out, edge_in,
    load_sem, save_sem, send, recv,
):
    loads, w_query, w_out, w_pair = attention_weights(weights_hbm, weights, load_sem)
    links = Links(send, recv)
    n, width = entry.shape[1:]
    h = n // 2
    tokens = 2 * n
    rows, heads = kv.shape[1], w_query.shape[0] // HEAD
    bits = rows.bit_length() - 1
    scale = 1.0 / math.sqrt(HEAD)
    if gathers:
        entry[0] = entry_ref[...].astype(BF16)
    else:
        entry[...] = entry_ref[...]
    run.enter()
    moves = run.moves

    def normalise(k):
        x = entry[k].astype(F32)
        inverse = lax.rsqrt(jnp.mean(x * x, axis=-1, keepdims=True) + EPS)
        normed[pl.ds(k * n, n)] = (x * inverse * gain_ref[...]).astype(BF16)

    saves, copies = [], []
    if gathers:
        to_low = links.copy(entry.at[0], entry.at[1], COL_LOW)
        to_high = links.copy(entry.at[0], entry.at[2], COL_HIGH)
        corner_high = links.copy(entry.at[1, pl.ds(0, h)], entry.at[3, pl.ds(0, h)], COL_HIGH)
        corner_low = links.copy(entry.at[2, pl.ds(h, h)], entry.at[3, pl.ds(h, h)], COL_LOW)
        to_low.start()
        to_high.start()
        normalise(0)
        to_low.wait_recv()
        corner_high.start()
        to_high.wait_recv()
        corner_low.start()
        normalise(1)
        normalise(2)
        copies += [to_low, to_high, corner_high, corner_low]

    hops = [
        [(slot, filled, links.copy(kv.at[b, slot], kv.at[b, filled], ("row", 1 << bit)))
         for slot, filled, bit in row_hops(bits)]
        for b in range(2)
    ]

    def project_pair(b):
        at = pl.ds(b * tokens, tokens)
        pair = dot(normed[at], w_pair[...], 1, 1) + b_pair_ref[...]
        kv[b, 0, :, :HEAD] = turn(pair[:, :HEAD], cos_ref[at], sin_ref[at]).astype(BF16)
        kv[b, 0, :, HEAD:] = pair[:, HEAD:].astype(BF16)
        for slot, _, copy in hops[b]:
            if slot == 0:
                copy.start()

    def project_query(b):
        at = pl.ds(b * tokens, tokens)
        projected = dot(normed[at], w_query[...], 1, 1) + b_query_ref[...]
        for head in range(heads):
            lanes = slice(head * HEAD, (head + 1) * HEAD)
            query[at, lanes] = turn(projected[:, lanes], cos_ref[at], sin_ref[at]).astype(BF16)

    arrived = [set(), set()]

    def arrive(b, slot):
        for _, filled, copy in hops[b]:
            if filled == slot and slot not in arrived[b]:
                copy.wait_recv()
                arrived[b].add(slot)

    for move in moves[:1]:
        move.advance()
    for copy in loads:
        copy.wait()
    if gathers:
        project_pair(0)
        corner_high.wait_recv()
        corner_low.wait_recv()
        normalise(3)
        project_pair(1)
    else:
        normalise(2)
        normalise(3)
        project_pair(1)
        normalise(0)
        normalise(1)
        project_pair(0)
    project_query(1)
    project_query(0)
    for move in moves[:1]:
        move.advance()
    for b in (1, 0):
        for slot, _, copy in hops[b]:
            if slot:
                arrive(b, slot)
                copy.start()
    for move in moves[1:]:
        move.advance()

    corner_b, corner_a, edge_a, edge_b = scatter_copies(
        links, corner_out, corner_in, edge_out, edge_in, COL_LOW, COL_HIGH
    )
    for b in (1, 0):
        for slot in range(1, rows):
            arrive(b, slot)
        save(saves, save_sem, (kv.at[b],), (kv_hbm.at[b],))
        keys = kv[b, :, :, :HEAD].reshape(rows * tokens, HEAD)
        values = kv[b, :, :, HEAD:].reshape(rows * tokens, HEAD)
        at = pl.ds(b * tokens, tokens)
        bias[...] = seen(start_ref, own_ref, key_ref, b)
        for head in range(heads):
            lanes = slice(head * HEAD, (head + 1) * HEAD)
            scores = dot(keys, query[at, lanes], 1, 1) * scale + bias[...]
            top = jnp.max(scores, axis=0, keepdims=True)
            raised = jnp.exp(scores - top)
            total = jnp.sum(raised, axis=0, keepdims=True)
            lse_ref[b, pl.ds(head, 1)] = top + jnp.log(total)
            probs = (raised * (1.0 / total)).astype(BF16)
            mixed[at, lanes] = dot(probs, values, 0, 0).astype(BF16)
        for k in (2 * b + 1, 2 * b):
            for lane, size in width_tiles(width):
                partial[k, :, pl.ds(lane, size)] = dot(
                    mixed[pl.ds(k * n, n)], w_out[:, pl.ds(lane, size)], 1, 0
                )
        if b == 1:
            corner_out[...] = partial[3].astype(BF16).reshape(corner_out.shape)
            corner_b.start()
            corner_a.start()
    corner_a.wait_recv()
    edge_out[1, :h] = partial[2, :h].astype(BF16)
    edge_out[1, h:] = (partial[2, h:] + corner_in[1].astype(F32)).astype(BF16)
    edge_b.start()
    corner_b.wait_recv()
    edge_out[0, :h] = (partial[1, :h] + corner_in[0].astype(F32)).astype(BF16)
    edge_out[0, h:] = partial[1, h:].astype(BF16)
    edge_a.start()
    if gathers:
        save(saves, save_sem, (entry,), (entry_hbm,))
    for move in moves[1:2]:
        move.advance()
    own = entry[0].astype(F32) + partial[0]
    edge_b.wait_recv()
    edge_a.wait_recv()
    second_ref[...] = own + edge_in[0].astype(F32) + edge_in[1].astype(F32)
    for move in moves[2:]:
        move.advance()
    for move in moves:
        move.end()
    copies += [copy for group in hops for _, _, copy in group] + [corner_a, corner_b, edge_a, edge_b]
    wait_all([], copies)
    for copy in saves:
        copy.wait()


def attention_backward_kernel(
    run,
    d_second_ref, entry_ref, gain_ref, cos_ref, sin_ref, start_ref, own_ref, key_ref,
    query, kv, lse_ref, weights_hbm,
    d_entry_ref, d_gain_ref, d_query, d_pair, d_bias_query_ref, d_bias_pair_ref, blocks_hbm,
    weights, blocks, d_mixed, bias, d_kv, d_kv_out, d_kv_in, share_out, share_in,
    partial, corner_out, corner_in, edge_out, edge_in,
    load_sem, save_sem, send, recv,
):
    loads, w_query, w_out, w_pair = attention_weights(weights_hbm, weights, load_sem)
    links = Links(send, recv)
    n, width = blocks.shape[1:]
    h = n // 2
    tokens = 2 * n
    rows, heads = kv.shape[1], w_query.shape[0] // HEAD
    bits = rows.bit_length() - 1
    scale = 1.0 / math.sqrt(HEAD)
    blocks[0] = d_second_ref[...].astype(BF16)
    run.enter()
    to_low = links.copy(blocks.at[0], blocks.at[1], COL_LOW)
    to_high = links.copy(blocks.at[0], blocks.at[2], COL_HIGH)
    corner_high = links.copy(blocks.at[1, pl.ds(0, h)], blocks.at[3, pl.ds(0, h)], COL_HIGH)
    corner_low = links.copy(blocks.at[2, pl.ds(h, h)], blocks.at[3, pl.ds(h, h)], COL_LOW)
    hops = [
        [(slot, filled, links.copy(d_kv_out.at[b, filled], d_kv_in.at[b, filled], ("row", 1 << bit)))
         for slot, filled, bit in reversed(row_hops(bits))]
        for b in range(2)
    ]
    share = [links.copy(share_out.at[b], share_in.at[b], COL_LOW) for b in range(2)]
    corner_b, corner_a, edge_a, edge_b = scatter_copies(
        links, corner_out, corner_in, edge_out, edge_in, COL_LOW, COL_HIGH
    )

    def unmix(k):
        d_mixed[pl.ds(k * n, n)] = dot(blocks[k], w_out[...], 1, 1).astype(BF16)

    def attend(b):
        keys = kv[b, :, :, :HEAD].reshape(rows * tokens, HEAD)
        values = kv[b, :, :, HEAD:].reshape(rows * tokens, HEAD)
        at = pl.ds(b * tokens, tokens)
        bias[...] = seen(start_ref, own_ref, key_ref, b)
        for head in range(heads):
            lanes = slice(head * HEAD, (head + 1) * HEAD)
            q = query[at, lanes]
            d_o = d_mixed[at, lanes]
            scores = dot(keys, q, 1, 1) * scale + bias[...]
            probs = jnp.exp(scores - lse_ref[b, pl.ds(head, 1)])
            d_probs = dot(values, d_o, 1, 1)
            delta = jnp.sum(d_probs * probs, axis=0, keepdims=True)
            d_scores = (probs * (d_probs - delta)).astype(BF16)
            d_keys = dot(d_scores, q, 1, 0) * scale
            d_values = dot(probs.astype(BF16), d_o, 1, 0)
            d_keys = d_keys.reshape(rows, tokens, HEAD)
            d_values = d_values.reshape(rows, tokens, HEAD)
            if head:
                d_keys = d_keys + d_kv[b, :, :, :HEAD]
                d_values = d_values + d_kv[b, :, :, HEAD:]
            d_kv[b, :, :, :HEAD] = d_keys
            d_kv[b, :, :, HEAD:] = d_values
            turned = dot(d_scores, keys, 0, 0) * scale
            d_query[at, lanes] = turn(turned, cos_ref[at], -sin_ref[at]).astype(BF16)

    def send_bit(b, step):
        for slot, filled, copy in hops[b]:
            if filled - slot == step:
                d_kv_out[b, filled] = d_kv[b, filled].astype(BF16)
                copy.start()

    def add_bit(b, step):
        for slot, filled, copy in hops[b]:
            if filled - slot == step:
                copy.wait_recv()
                d_kv[b, slot] = d_kv[b, slot] + d_kv_in[b, filled].astype(F32)

    def share_pair(b):
        share_out[b] = d_kv[b, 0, n:].astype(BF16)
        share[b].start()

    def finish_pair(b):
        share[b].wait_recv()
        total = d_kv[b, 0, :n] + share_in[b].astype(F32)
        at = pl.ds(b * tokens, n)
        d_pair[pl.ds(b * n, n), :HEAD] = turn(total[:, :HEAD], cos_ref[at], -sin_ref[at]).astype(BF16)
        d_pair[pl.ds(b * n, n), HEAD:] = total[:, HEAD:].astype(BF16)

    def unproject(k):
        for lane, size in width_tiles(width):
            value = dot(d_query[pl.ds(k * n, n)], w_query[:, pl.ds(lane, size)], 1, 0)
            if k % 2 == 0:
                value = value + dot(
                    d_pair[pl.ds(k // 2 * n, n)], w_pair[:, pl.ds(lane, size)], 1, 0
                )
            partial[k, :, pl.ds(lane, size)] = value

    moves = run.moves
    to_low.start()
    to_high.start()
    for move in moves[:1]:
        move.advance()
    for copy in loads:
        copy.wait()
    unmix(0)
    to_low.wait_recv()
    corner_high.start()
    to_high.wait_recv()
    corner_low.start()
    for move in moves[1:2]:
        move.advance()
    unmix(1)
    unmix(2)
    corner_high.wait_recv()
    corner_low.wait_recv()
    unmix(3)
    saves = []
    save(saves, save_sem, (blocks,), (blocks_hbm,))
    attend(1)
    send_bit(1, 1)
    unproject(3)
    corner_out[...] = partial[3].astype(BF16).reshape(corner_out.shape)
    corner_b.start()
    corner_a.start()
    for move in moves[:1]:
        move.advance()
    attend(0)
    send_bit(0, 1)
    for bit in range(1, bits):
        for b in (1, 0):
            add_bit(b, 1 << (bit - 1))
            send_bit(b, 1 << bit)
    unproject(1)
    corner_b.wait_recv()
    edge_out[0, :h] = (partial[1, :h] + corner_in[0].astype(F32)).astype(BF16)
    edge_out[0, h:] = partial[1, h:].astype(BF16)
    edge_a.start()
    for b in (1, 0):
        add_bit(b, 1 << (bits - 1))
        share_pair(b)
    finish_pair(1)
    unproject(2)
    corner_a.wait_recv()
    edge_out[1, :h] = partial[2, :h].astype(BF16)
    edge_out[1, h:] = (partial[2, h:] + corner_in[1].astype(F32)).astype(BF16)
    edge_b.start()
    for move in moves[2:]:
        move.advance()
    for move in moves[:2]:
        move.advance()
    finish_pair(0)
    unproject(0)
    d_bias_query_ref[...] = jnp.sum(d_query[...].astype(F32), axis=0, keepdims=True)
    d_bias_pair_ref[...] = jnp.sum(d_pair[...].astype(F32), axis=0, keepdims=True)
    edge_a.wait_recv()
    edge_b.wait_recv()
    d_normed = partial[0] + edge_in[0].astype(F32) + edge_in[1].astype(F32)
    stream = entry_ref[...].astype(F32)
    inverse = lax.rsqrt(jnp.mean(stream * stream, axis=-1, keepdims=True) + EPS)
    d_first, d_gain = norm_backward(stream, inverse, gain_ref[...], d_normed)
    d_gain_ref[...] = d_gain
    d_entry_ref[...] = (d_second_ref[...] + d_first).astype(BF16)
    while any(move.at < len(move.steps) for move in moves):
        for move in moves:
            move.advance()
    copies = [to_low, to_high, corner_high, corner_low, corner_a, corner_b, edge_a, edge_b, *share]
    wait_all([], copies + [copy for group in hops for _, _, copy in group])
    for copy in saves:
        copy.wait()


def scatter_scratch(n, width):
    return [
        pltpu.VMEM((4, n, width), F32),
        pltpu.VMEM((2, n // 2, width), BF16),
        pltpu.VMEM((2, n // 2, width), BF16),
        pltpu.VMEM((2, n, width), BF16),
        pltpu.VMEM((2, n, width), BF16),
    ]


def attention_ways(rows):
    return [COL_LOW, COL_HIGH] + [("row", 1 << bit) for bit in range(rows.bit_length() - 1)]


def attention_forward(gathers, collective_id, entry, vectors, tables, weights, after, sizes, moves):
    n, width, rows, _ = sizes
    tokens = 2 * n
    weights = loadable(weights)
    count = 2 * weights.shape[2]
    heads_width = (count - 2 * HEAD) // 2
    heads = heads_width // HEAD
    copies = 8 + 2 * (rows - 1)
    return kernel_call(
        functools.partial(attention_forward_kernel, gathers),
        collective_id,
        attention_ways(rows),
        [(array, True) for array in (entry, *vectors, *tables)] + [(weights, False)],
        after,
        [
            ((n, width), F32, True),
            ((4 * n, width), BF16, True),
            ((4 * n, heads_width), BF16, True),
            ((4 * n, heads_width), BF16, True),
            ((2, heads, tokens), F32, True),
            ((2, rows, tokens, 2 * HEAD), BF16, False),
            ((4, n, width), BF16, False),
        ],
        [
            pltpu.VMEM((count, width), BF16),
            pltpu.VMEM((4, n, width), BF16),
            pltpu.VMEM((2, rows, tokens, 2 * HEAD), BF16),
            pltpu.VMEM((rows * tokens, tokens), F32),
            *scatter_scratch(n, width),
            pltpu.SemaphoreType.DMA((2 * weights.shape[1],)),
            pltpu.SemaphoreType.DMA((4,)),
            pltpu.SemaphoreType.DMA((copies,)),
            pltpu.SemaphoreType.DMA((copies,)),
        ],
        4 * 2 * n * width * 5 * heads_width // 2,
        moves,
    )


def attention_backward(collective_id, operands, weights, after, sizes, moves):
    n, width, rows, _ = sizes
    tokens = 2 * n
    weights = loadable(weights)
    count = 2 * weights.shape[2]
    heads_width = (count - 2 * HEAD) // 2
    copies = 10 + 2 * (rows - 1)
    return kernel_call(
        attention_backward_kernel,
        collective_id,
        attention_ways(rows),
        [(array, True) for array in operands] + [(weights, False)],
        after,
        [
            ((n, width), BF16, True),
            ((1, width), F32, True),
            ((4 * n, heads_width), BF16, True),
            ((2 * n, 2 * HEAD), BF16, True),
            ((1, heads_width), F32, True),
            ((1, 2 * HEAD), F32, True),
            ((4, n, width), BF16, False),
        ],
        [
            pltpu.VMEM((count, width), BF16),
            pltpu.VMEM((4, n, width), BF16),
            pltpu.VMEM((4 * n, heads_width), BF16),
            pltpu.VMEM((rows * tokens, tokens), F32),
            pltpu.VMEM((2, rows, tokens, 2 * HEAD), F32),
            pltpu.VMEM((2, rows, tokens, 2 * HEAD), BF16),
            pltpu.VMEM((2, rows, tokens, 2 * HEAD), BF16),
            pltpu.VMEM((2, n, 2 * HEAD), BF16),
            pltpu.VMEM((2, n, 2 * HEAD), BF16),
            *scatter_scratch(n, width),
            pltpu.SemaphoreType.DMA((2 * weights.shape[1],)),
            pltpu.SemaphoreType.DMA((4,)),
            pltpu.SemaphoreType.DMA((copies,)),
            pltpu.SemaphoreType.DMA((copies,)),
        ],
        4 * 2 * n * width * 5 * heads_width // 2,
        moves,
    )


def sum_kernel(ways, run, value_ref, total_ref, outgoing, incoming, send, recv):
    run.enter()
    links = Links(send, recv)
    total = value_ref[...]
    copies = []
    for i, way in enumerate(ways):
        outgoing[i] = total
        copies.append(links.copy(outgoing.at[i], incoming.at[i], way))
        copies[-1].start()
        copies[-1].wait_recv()
        total = total + incoming[i]
        for move in run.moves:
            move.advance()
    total_ref[...] = total
    for move in run.moves:
        move.end()
    wait_all([], copies)


def sum_all(value, collective_id, moves):
    ways = [SECTION, COL_LOW, COL_HIGH] + [("row", 1 << bit) for bit in range(row_bits())]
    buffers = [pltpu.VMEM((len(ways), *value.shape), F32) for _ in range(2)]
    return kernel_call(
        functools.partial(sum_kernel, ways),
        collective_id,
        ways,
        [(value, True)],
        (),
        [(value.shape, F32, True)],
        buffers + semaphores(len(ways), len(ways)),
        1 << 20,
        moves,
    )


def exchange_halves(parts, section):
    return pick(parts, section), swap(pick(parts, 1 - section), *SECTION)


def of_layer(layer, parts, section, token):
    own, other = parts
    return jnp.where(section + token == layer, own, other)


def to_owner(first, second, section):
    keep = jnp.where(section == 0, first, second)
    away = jnp.where(section == 0, second, first)
    other = swap(away, *SECTION)
    return jnp.where(section == 0, keep, other), jnp.where(section == 0, other, keep)


def local(
    tokens,
    cotangent,
    lengths,
    norm_attn,
    w_query,
    b_query,
    w_keyval,
    b_keyval,
    w_out,
    norm_ffn,
    w_gate,
    w_up,
    w_down,
):
    section = lax.axis_index("section")
    row = lax.axis_index("row")
    col = lax.axis_index("col")
    rows = lax.axis_size("row")
    cols = lax.axis_size("col")
    low, high = bit_of(col, 0), bit_of(col, 1)
    place = (section, row, low, high)
    row_count = tokens.shape[1]
    width = tokens.shape[2]
    half = row_count // 2
    depth = w_query.shape[1]
    heads_width = w_query.shape[2]

    def blocks_of(array):
        return jnp.concatenate(
            [
                lax.dynamic_slice(
                    array, (2 * section + (high ^ j), (low ^ k) * half, 0), (1, half, width)
                )
                for j in range(2)
                for k in range(2)
            ]
        )

    small = jnp.concatenate([norm_attn[0], norm_ffn[0], b_keyval[0], b_query[0]])
    small = (small, swap(small, *SECTION))
    small = [of_layer(layer, small, section, 0).astype(F32) for layer in range(2)]

    pair_cols = w_keyval[0].reshape(-1, 2, KV, HEAD)
    mine = pick(pair_cols, high, 2).reshape(-1, 2 * HEAD)
    away = pick(pair_cols, 1 - high, 2).reshape(-1, 2 * HEAD)
    pair_rows = ordered(mine[None, None], swap(away, *COL_HIGH)[None, None], high, 0)
    pair_rows = ordered(pair_rows, swap(pair_rows, *COL_LOW), low, 1)
    pair_rows = pair_rows.reshape(depth, 2 * HEAD)
    attn_own = jnp.concatenate([w_query[0].T, w_out[0], pair_rows.T])
    attn_halves = exchange_halves(attn_own.reshape(2, -1, depth), section)

    def ffn_parts(shard):
        hidden = shard.shape[0]
        parts = shard.reshape(2, 2, hidden // 4, shard.shape[1]).transpose(1, 0, 2, 3)
        return exchange_halves(parts, section)

    parts = [ffn_parts(shard) for shard in (w_gate[0].T, w_up[0].T, w_down[0])]
    ways = [(COL_LOW, COL_HIGH), (COL_HIGH, COL_LOW)]

    hidden = w_gate.shape[2] // 2

    tables = layout(lengths, place, row_count)
    sizes = (half, width, rows, hidden)
    entry = blocks_of(tokens)
    saved = []

    def vectors_of(layer):
        gain_attn = small[layer][None, :width]
        gain_ffn = small[layer][None, width : 2 * width]
        bias_pair = small[layer][2 * width : 2 * width + 2 * KV * HEAD].reshape(2, KV, HEAD)
        bias_pair = pick(bias_pair, high, 1).reshape(1, -1)
        bias_query = small[layer][None, 2 * width + 2 * KV * HEAD :]
        return gain_attn, gain_ffn, bias_query, bias_pair

    def attend(layer, entry, weights, moves):
        gain_attn, _, bias_query, bias_pair = vectors_of(layer)
        return attention_forward(
            layer > 0, 4 + layer, entry, (gain_attn, bias_query, bias_pair), tables, weights, (), sizes, moves
        )

    def feed(layer, second, weights, moves):
        return ffn_call(
            ffn_forward_kernel,
            ways[layer][0],
            ROW_LOW,
            layer,
            (second, vectors_of(layer)[1]),
            (),
            weights,
            (),
            sizes,
            [(half, width)],
            3,
            moves,
        )

    def ffn_gather(layer, kind):
        return FfnGather(of_layer(layer, parts[kind], section, 0), ways[layer][1])

    _, _, ((attn_zero,),) = kernel_call(
        move_kernel, 9, (), (), (), (), (), 0, [AttnGather(of_layer(0, attn_halves, section, 0))]
    )
    _, (second, *kept, _), weights_zero = attend(
        0, entry, attn_zero, [ffn_gather(0, kind) for kind in range(3)]
    )
    _, (result, *kept_ffn), ((attn_one,), *weights_one) = feed(
        0, second, weights_zero, [AttnGather(of_layer(1, attn_halves, section, 0)), ffn_gather(1, 0)]
    )
    saved.append((entry[0], attn_zero, weights_zero, second, kept, kept_ffn))
    _, (second, *kept, first_result), more_weights = attend(
        1, result, attn_one, [ffn_gather(1, kind) for kind in (1, 2)]
    )
    weights_one += more_weights
    entry = result.astype(BF16)
    grad_own = lax.dynamic_slice(
        cotangent, (2 * section + high, low * half, 0), (1, half, width)
    )[0]
    _, (result, *kept_ffn), ((grad_all,),) = feed(
        1, second, weights_one, [TokenGather(grad_own, ways[1][0], ROW_LOW, True)]
    )
    saved.append((entry, attn_one, weights_one, second, kept, kept_ffn))
    last_result = result.astype(BF16)

    unit = hidden // 2

    def grad_of(left, right):
        return dot(left, right.reshape(-1, width), 0, 0).astype(BF16)

    def blocked(grad, arrived):
        total = (grad[:unit].astype(F32) + arrived.astype(F32)).astype(BF16)
        return jnp.stack([total[:, i * depth : (i + 1) * depth] for i in range(rows)])

    def feed_back(layer, grad_own, gathered, after, moves):
        _, _, weights, second, _, (normed_two, gate, up, act) = saved[layer]
        return ffn_call(
            functools.partial(ffn_backward_kernel, gathered is None),
            ways[layer][0],
            ROW_LOW,
            2 + layer,
            (grad_own, second, vectors_of(layer)[1]),
            (gate, up) if gathered is None else (gate, up, gathered),
            weights,
            after,
            sizes,
            [(half, width), (1, width)],
            2,
            moves,
        )

    def attend_back(layer, d_second, after, moves):
        own, weights, _, _, (normed, query, mixed, lse, kv), _ = saved[layer]
        _, outs, moved = attention_backward(
            6 + layer,
            (d_second, own, vectors_of(layer)[0], *tables, query, kv, lse),
            weights,
            after,
            sizes,
            moves,
        )
        d_own, d_gain, d_query, d_pair, d_bias_query, d_bias_pair, d_attn = outs
        normed_own = normed.reshape(2, 2, half, width)[:, 0].reshape(-1, width)
        grads = jnp.concatenate(
            [grad_of(d_query, normed), grad_of(mixed, d_attn), grad_of(d_pair, normed_own)]
        )
        return d_own, grads, (d_gain[0], d_bias_query[0], d_bias_pair[0]), moved

    normed_two, _, _, act = saved[1][5]
    down_one = grad_of(act, grad_all)
    _, (d_second, d_gain_one, _, d_gate, d_up), ((down_across,),) = feed_back(
        1, grad_own, grad_all, (), [Across(down_one, unit, ways[1][1])]
    )
    gate_one, up_one = grad_of(d_gate, normed_two), grad_of(d_up, normed_two)
    down_one = blocked(down_one, down_across)
    grad_one, attn_grad_one, small_one, ((down_rows,), (gate_across,), (up_across,)) = attend_back(
        1,
        d_second,
        (),
        [Rows(down_one), Across(gate_one, unit, ways[1][1]), Across(up_one, unit, ways[1][1])],
    )
    gate_one, up_one = blocked(gate_one, gate_across), blocked(up_one, up_across)
    normed_two, _, _, act = saved[0][5]
    _, (d_second, d_gain_zero, grad_all, d_gate, d_up), ((gate_rows,), (last_blocks,), (grad_one_blocks,)) = feed_back(
        0,
        grad_one,
        None,
        (attn_grad_one, up_one),
        [
            Rows(gate_one),
            TokenGather(last_result, COL_LOW, COL_HIGH, False),
            TokenGather(grad_one, COL_LOW, COL_HIGH, False),
        ],
    )
    zero_grads = [grad_of(act, grad_all), grad_of(d_gate, normed_two), grad_of(d_up, normed_two)]
    grad_zero, attn_grad_zero, small_zero, moved = attend_back(
        0,
        d_second,
        (),
        [Rows(up_one)] + [GradScatter(grad, unit, ways[0][1]) for grad in zero_grads] + [AttnScatter(attn_grad_one)],
    )
    (up_rows,), *scattered, (attn_one_half,) = moved
    near_far_zero = [scattered[i] for i in (1, 2, 0)]
    near_far_one = [(pick(total, row), arrived) for total, arrived in ((gate_one, gate_rows), (up_one, up_rows), (down_one, down_rows))]

    def by_row_bit(own, arrived):
        near, far = own.astype(F32), 0.0
        for flip in range(1, rows):
            if flip & 1:
                far = far + arrived[flip].astype(F32)
            else:
                near = near + arrived[flip].astype(F32)
        return ordered(near.astype(BF16)[None], far.astype(BF16)[None], row & 1, 0)

    ffn_grads = [[by_row_bit(*pair) for pair in pairs] for pairs in (near_far_zero, near_far_one)]

    vectors = []
    for (d_gain, d_bias_query, d_bias_pair), d_gain_two in ((small_zero, d_gain_zero), (small_one, d_gain_one)):
        spread_query = jnp.where(
            (jnp.arange(cols) == col)[:, None], d_bias_query[None], 0.0
        ).reshape(-1)
        spread_pair = jnp.where(
            (jnp.arange(2) == high)[None, :, None],
            d_bias_pair.reshape(2, 1, HEAD),
            0.0,
        ).reshape(-1)
        vectors.append(jnp.concatenate([d_gain, d_gain_two[0], spread_query, spread_pair]))
    _, (sums,), ((attn_zero_half,), (grad_zero_blocks,)) = sum_all(
        jnp.stack(vectors).reshape(-1, 128),
        8,
        [AttnScatter(attn_grad_zero), TokenGather(grad_zero, COL_LOW, COL_HIGH, False)],
    )
    sums = sums.reshape(2, -1)
    sums = jnp.where(section == 0, sums[0], sums[1])
    grad_norm_attn = sums[:width]
    grad_norm_ffn = sums[width : 2 * width]
    spread = sums[2 * width : 2 * width + cols * heads_width].reshape(cols, -1)
    grad_b_query = pick(spread, col)
    grad_b_keyval = sums[2 * width + cols * heads_width :]

    def assemble(first, second):
        def placed(blocks):
            blocks = blocks.reshape(2, 2, half, width)
            blocks = jnp.where(high == 0, blocks, blocks[::-1])
            blocks = jnp.where(low == 0, blocks, blocks[:, ::-1])
            return blocks.reshape(2, row_count, width)

        zeroth, later = to_owner(placed(first), placed(second), section)
        return jnp.concatenate([zeroth, later])[None]

    outputs = assemble(first_result, last_blocks)
    grads_in = assemble(grad_zero_blocks, grad_one_blocks)

    def ffn_grad(kind):
        zeroth, later = to_owner(ffn_grads[0][kind], ffn_grads[1][kind], section)
        whole = jnp.stack([zeroth, later], axis=1)
        return whole.reshape(-1, whole.shape[-1])

    grad_gate = ffn_grad(0).T.astype(F32)
    grad_up = ffn_grad(1).T.astype(F32)
    grad_down = ffn_grad(2).astype(F32)

    total = jnp.concatenate(to_owner(attn_zero_half, attn_one_half, section)).astype(F32)
    grad_query = total[:heads_width].T
    grad_out = total[heads_width : 2 * heads_width]
    pair = total[2 * heads_width :].T.reshape(2, 2, depth // 4, 2 * HEAD)
    pair = pick(pair, low, 1) + swap(pick(pair, 1 - low, 1).astype(BF16), *COL_LOW).astype(F32)
    pair = pair.astype(BF16)
    pair = ordered(
        pick(pair, high)[:, None], swap(pick(pair, 1 - high), *COL_HIGH)[:, None], high, 1
    )
    grad_keyval = (
        pair.reshape(-1, 2, 2, HEAD).transpose(0, 2, 1, 3).reshape(-1, 2 * KV * HEAD).astype(F32)
    )

    return (
        outputs,
        grads_in,
        grad_norm_attn[None],
        grad_query[None],
        grad_b_query[None],
        grad_keyval[None],
        grad_b_keyval[None],
        grad_out[None],
        grad_norm_ffn[None],
        grad_gate[None],
        grad_up[None],
        grad_down[None],
    )


def solution(mesh):
    in_specs = (
        P(None, "row", None),
        P(None, "row", None),
        P(),
        P("section", None),
        P("section", "row", "col"),
        P("section", "col"),
        P("section", ("row", "col"), None),
        P("section", None),
        P("section", "col", "row"),
        P("section", None),
        P("section", "row", "col"),
        P("section", "row", "col"),
        P("section", "col", "row"),
    )
    out_specs = (
        P("section", None, "row", None),
        P("section", None, "row", None),
        P("section", None),
        P("section", "row", "col"),
        P("section", "col"),
        P("section", ("row", "col"), None),
        P("section", None),
        P("section", "col", "row"),
        P("section", None),
        P("section", "row", "col"),
        P("section", "row", "col"),
        P("section", "col", "row"),
    )
    return jax.shard_map(local, mesh=mesh, in_specs=in_specs, out_specs=out_specs, check_vma=False)
```

time: 2860 us -> 1200 us (0.42)
  waiting for transfers between devices: 1730 us -> 4.36 us
  Pallas kernels: 0 us -> 1010 us
  matrix products: 506 us -> 48.7 us
  blocking collectives: 167 us -> 0 us
  local copies, waits for them, and re-layouts: 196 us -> 39.4 us
  other arithmetic: 201 us -> 71 us
    pallas_call x0 -> x10, Pallas kernels: none -> 1010 us  [kernel_call(): pl.pallas_call(body, out_shape=[jax.ShapeDtypeStruct((8, 128), jnp.int32)...]
    psum x19 -> x0, waiting for transfers between devices: 845 us -> none  [the longest x11 480 us: column_sum(): return lax.psum(partial_sum.astype(jnp.bfloat16), 'col').astype(jnp.float32)]
    all_gather x6 -> x0, waiting for transfers between devices: 449 us -> none  [the longest x1 125 us: local(): lax.all_gather(w_up[0], 'row', axis=0, tiled=True)]
    dot_general x140 -> x12, matrix products: 461 us -> 48.7 us  [dot(): lax.dot_general(left, right, (((left_dim,), (right_dim,)), ((), ())), pre...]
    unnamed x40 -> x0, waiting for transfers between devices: 266 us -> none
    reduce_scatter x7 -> x0, waiting for transfers between devices: 153 us -> none  [the longest x1 124 us: local(): lax.psum_scatter(acc_keyval, ('row', 'col'), scatter_dimension=0, tiled=T...]
    all_gather x10 -> x0, blocking collectives: 142 us -> none  [forward_layer(): gathered = lax.all_gather(local_pair, 'row', axis=0, tiled=True)]
    unnamed x803 -> x157, local copies, waits for them, and re-layouts: 120 us -> 11.2 us
  transfers between devices with their start and end apart: 49 -> 15, of which waited for: 39 -> 2; matrix products, arithmetic and copies ran while one was open for 17% -> 6% of each run, Pallas kernels for 0% -> 3%
where the time goes in v1:
time: 1200 us
  Pallas kernels  1010 us (84%)
  other arithmetic  71 us (6%)
  matrix products  48.7 us (4%)
  local copies, waits for them, and re-layouts  39.4 us (3%)
  starting transfers between devices  13.9 us (1%)
    pallas_call x10, Pallas kernels, kernel_call(): pl.pallas_call(body, out_shape=[jax.ShapeDtypeStruct((8, 128), jnp.int32)...  1010 us
    dot_general x12, matrix products, dot(): lax.dot_general(left, right, (((left_dim,), (right_dim,)), ((), ())), pre...  48.7 us
  transfers between devices with their start and end apart: 15, of which 2 were waited for; matrix products, arithmetic and copies ran while one was open for 6% of the time, Pallas kernels for 3%

profile of v1, /device:TPU:9, one launch (start us, length us, event | category | flops | bytes accessed | tf_op | source)
XLA Modules:
  0.0 1197.1 jit_solution(8740124183474820905)
XLA Ops:
  3.7 2.3 dynamic-slice_bitcast_fusion
  15.9 2.6 fusion.8
  28.4 2.7 collective-permute-done.2
  38.4 34.8 %shard_map.220 = (s32[8,128]{1,0:T(8,128)}, bf16[2,4,512,384]{3,2,1,0:T(8,128)(2,1)}) custom-call(bf16[512,384]{1,0:T(8,128)(2,1)} %get-tuple-element.271.refs_0_), custom_call_target="tpu_custom_call" | custom-call | bytes 16777216 | tf_op jit(solution)/shard_map/pallas_call | solution.py:409
  73.2 2.6 bitcast_select_fusion.4
  75.8 2.6 bitcast_select_fusion.6
  78.5 2.5 bitcast_select_fusion.8
  81.0 145.1 %shard_map.221 = (s32[8,128]{1,0:T(8,128)}, f32[128,1536]{1,0:T(8,128)}, bf16[512,1536]{1,0:T(8,128)(2,1)}, bf16[512,384]{1,0:T(8,128)(2,1)}, bf16[512,384]{1,0:...) custom-call(bf16[4,128,1536]{2,1,0:T(8,128)(2,1)} %pad_maximum_fusio, ...), custom_call_target="tpu_custom_call" | custom-call | flops 1509949440 | bytes 16777216 | tf_op jit(solution)/shard_map/pallas_call | solution.py:409
  226.1 112.5 %shard_map.222 = (s32[8,128]{1,0:T(8,128)}, f32[128,1536]{1,0:T(8,128)}, bf16[4,2,128,1536]{3,2,1,0:T(8,128)(2,1)}, bf16[1024,1152]{1,0:T(8,128)(2,1)}, bf16[102...) custom-call(f32[128,1536]{1,0:T(8,128)} %get-tuple-element.92.refs_0, ...), custom_call_target="tpu_custom_call" | custom-call | flops 10871635968 | bytes 16777216 | tf_op jit(solution)/shard_map/pallas_call | solution.py:409
  340.6 128.4 %shard_map.223 = (s32[8,128]{1,0:T(8,128)}, f32[128,1536]{1,0:T(8,128)}, bf16[512,1536]{1,0:T(8,128)(2,1)}, bf16[512,384]{1,0:T(8,128)(2,1)}, bf16[512,384]{1,0:...) custom-call(f32[128,1536]{1,0:T(8,128)} %get-tuple-element.99.refs_0, ...), custom_call_target="tpu_custom_call" | custom-call | flops 1509949440 | bytes 16777216 | tf_op jit(solution)/shard_map/pallas_call | solution.py:409
  469.0 67.0 %shard_map.224 = (s32[8,128]{1,0:T(8,128)}, f32[128,1536]{1,0:T(8,128)}, bf16[4,2,128,1536]{3,2,1,0:T(8,128)(2,1)}, bf16[1024,1152]{1,0:T(8,128)(2,1)}, bf16[102...) custom-call(f32[128,1536]{1,0:T(8,128)} %get-tuple-element.102.refs_0_.refs_1_, ...), custom_call_target="tpu_custom_call" | custom-call | flops 10871635968 | bytes 16777216 | tf_op jit(solution)/shard_map/pallas_call | solution.py:409
  536.0 8.2 convolution_convert_fusion.5.refs_12_
  544.2 58.0 %shard_map.225 = (s32[8,128]{1,0:T(8,128)}, f32[128,1536]{1,0:T(8,128)}, f32[1,1536]{1,0:T(1,128)}, bf16[4,2,128,1536]{3,2,1,0:T(8,128)(2,1)}, bf16[1024,1152]{1...) custom-call(bf16[128,1536]{1,0:T(8,128)(2,1)} %dynamic-slice_bitcast_fusion.3.refs_8_.refs_0_, ...), custom_call_target="tpu_custom_call" | custom-call | flops 10871635968 | bytes 16777216 | tf_op jit(solution)/shard_map/pallas_call | solution.py:409
  602.3 8.6 convolution_convert_fusion.3.refs_14_
  610.9 5.5 convolution_convert_fusion.4.refs_13_
  619.9 107.9 %shard_map.226 = (s32[8,128]{1,0:T(8,128)}, bf16[128,1536]{1,0:T(8,128)(2,1)}, f32[1,1536]{1,0:T(1,128)}, bf16[512,384]{1,0:T(8,128)(2,1)}, bf16[256,256]{1,0:T(...) custom-call(f32[128,1536]{1,0:T(8,128)} %get-tuple-element.113.refs_, ...), custom_call_target="tpu_custom_call" | custom-call | flops 1509949440 | bytes 16777216 | tf_op jit(solution)/shard_map/pallas_call | solution.py:409
  727.8 2.4 add_convert_fusion
  744.1 92.7 %shard_map.227 = (s32[8,128]{1,0:T(8,128)}, f32[128,1536]{1,0:T(8,128)}, f32[1,1536]{1,0:T(1,128)}, bf16[4,2,128,1536]{3,2,1,0:T(8,128)(2,1)}, bf16[1024,1152]{1...) custom-call(bf16[128,1536]{1,0:T(8,128)(2,1)} %get-tuple-element.121, ...), custom_call_target="tpu_custom_call" | custom-call | flops 10871635968 | bytes 16777216 | tf_op jit(solution)/shard_map/pallas_call | solution.py:409
  836.9 8.4 convolution_convert_fusion.refs_15_
  845.3 5.4 convolution_convert_fusion.1.refs_14_
  850.8 5.6 convolution_convert_fusion.2.refs_13_
  856.4 202.5 %shard_map.228 = (s32[8,128]{1,0:T(8,128)}, bf16[128,1536]{1,0:T(8,128)(2,1)}, f32[1,1536]{1,0:T(1,128)}, bf16[512,384]{1,0:T(8,128)(2,1)}, bf16[256,256]{1,0:T(...) custom-call(f32[128,1536]{1,0:T(8,128)} %get-tuple-element.133.refs_, ...), custom_call_target="tpu_custom_call" | custom-call | flops 1509949440 | bytes 16777216 | tf_op jit(solution)/shard_map/pallas_call | solution.py:409
  1066.8 64.7 %shard_map.229 = (s32[8,128]{1,0:T(8,128)}, f32[80,128]{1,0:T(8,128)}, bf16[512,384]{1,0:T(8,128)(2,1)}, bf16[4,1,128,1536]{3,2,1,0:T(8,128)(2,1)}) custom-call(f32[80,128]{1,0:T(8,128)} %reshape.418.refs_0_, bf16[1024,1536]{1,0:T(8,128)(2,1)} %pad_maximum_fusion.1.refs_1_, bf16[128,1536]{1,0:T(8,128)(2,1)} %get-tuple-element.155.refs_2_), custom_call_target="tpu_custom_call" | custom-call | flops 1048576 | bytes 16777216 | tf_op jit(solution)/shard_map/pallas_call | solution.py:409
  1155.6 2.5 broadcast_select_fusion.3
  (320 shorter events, 115.3 us)
Async XLA Ops:
  0.6 20.6 %copy-start = (bf16[4,256,1536]{2,1,0:T(8,128)(2,1)S(1)}, bf16[4,256,1536]{2,1,0:T(8,128)(2,1)}, u32[]{:S(2)}) copy-start(bf16[4,256,1536]{2,1,0:T(8,128)(2,1)} %param.14) | copy-start | bytes 9437188
  2.4 23.8 %collective-permute-start.1 = (bf16[96,256]{1,0:T(8,128)(2,1)S(1)}, bf16[96,256]{1,0:T(8,128)(2,1)}, u32[]{:S(2)}, u32[]{:S(2)}) collective-permute-start(bf16[96,256]{1,0:T(8,128)(2,1)S(1)} %bitcast.309), channel_id=1, source_target_pairs={{0,2},{1,3},{2,0},{3,1},{4,6},{5,7},{6,4},{7,5},{8,10},{9,11},{10,... | collective-permute-start | bytes 147464 | tf_op jit(solution)/shard_map/ppermute | solution.py:29
  6.0 67.1 %collective-permute-start.6 = (bf16[2,560,384]{2,1,0:T(8,128)(2,1)}, bf16[2,560,384]{2,1,0:T(8,128)(2,1)}, u32[]{:S(2)}, u32[]{:S(2)}) collective-permute-start(bf16[2,560,384]{2,1,0:T(8,128)(2,1)} %dynamic-slice_bitcast_fusion), channel_id=1, source_target_pairs={{0,16},{16,0},{1,17},{17,1},{2,18},{18,2},{3,19},{19,3},{4,20},{20... | collective-permute-start | bytes 2580488 | tf_op jit(solution)/shard_map/ppermute | solution.py:29
  8.0 67.8 %collective-permute-start.5 = (bf16[2,560,384]{2,1,0:T(8,128)(2,1)}, bf16[2,560,384]{2,1,0:T(8,128)(2,1)}, u32[]{:S(2)}, u32[]{:S(2)}) collective-permute-start(bf16[2,560,384]{2,1,0:T(8,128)(2,1)} %dynamic-slice_bitcast_fusion.1), channel_id=1, source_target_pairs={{0,16},{16,0},{1,17},{17,1},{2,18},{18,2},{3,19},{19,3},{4,20},{20... | collective-permute-start | bytes 2580488 | tf_op jit(solution)/shard_map/ppermute | solution.py:29
  9.0 69.4 %collective-permute-start.4 = (bf16[2,560,384]{2,1,0:T(8,128)(2,1)}, bf16[2,560,384]{2,1,0:T(8,128)(2,1)}, u32[]{:S(2)}, u32[]{:S(2)}) collective-permute-start(bf16[2,560,384]{2,1,0:T(8,128)(2,1)} %dynamic-slice_bitcast_fusion.2), channel_id=1, source_target_pairs={{0,16},{16,0},{1,17},{17,1},{2,18},{18,2},{3,19},{19,3},{4,20},{20... | collective-permute-start | bytes 2580488 | tf_op jit(solution)/shard_map/ppermute | solution.py:29
  9.7 18.6 %collective-permute-start = (bf16[3968]{0:T(1024)(128)(2,1)S(1)}, bf16[3968]{0:T(1024)(128)(2,1)S(1)}, u32[]{:S(2)}, u32[]{:S(2)}) collective-permute-start(bf16[3968]{0:T(1024)(128)(2,1)S(1)} %pad_maximum_fusion.20), channel_id=1, source_target_pairs={{0,16},{16,0},{1,17},{17,1},{2,18},{18,2},{3,19},{19,3},{4,20},{20... | collective-permute-start | bytes 23816 | tf_op jit(solution)/shard_map/ppermute | solution.py:29
  15.9 7.7 copy-start.50
  27.0 4.0 collective-permute-start.2
  31.4 6.0 collective-permute-start.3
  37.4 35.7 %copy-start.22 = (bf16[1,2240,384]{2,1,0:T(8,128)(2,1)S(1)}, bf16[1,2240,384]{2,1,0:T(8,128)(2,1)}, u32[]{:S(2)}) copy-start(bf16[1,2240,384]{2,1,0:T(8,128)(2,1)} %param.25) | copy-start | bytes 5160964
  602.2 8.6 copy-start.69
  602.3 8.6 copy-start.73
  836.9 8.4 copy-start.68
  836.9 8.4 copy-start.72
  856.4 202.5 %copy-start.43 = (bf16[512,1536]{1,0:T(8,128)(2,1)S(1)}, bf16[512,1536]{1,0:T(8,128)(2,1)}, u32[]{:S(2)}) copy-start(bf16[512,1536]{1,0:T(8,128)(2,1)} %get-tuple-element.151) | copy-start | bytes 4718596
  1066.8 66.2 %copy-start.42 = (bf16[560,384]{1,0:T(8,128)(2,1)S(1)}, bf16[560,384]{1,0:T(8,128)(2,1)}, u32[]{:S(2)}) copy-start(bf16[560,384]{1,0:T(8,128)(2,1)} %get-tuple-element.167) | copy-start | bytes 1290244
  1137.2 38.6 %collective-permute-start.14 = (bf16[2,560,384]{2,1,0:T(8,128)(2,1)}, bf16[2,560,384]{2,1,0:T(8,128)(2,1)}, u32[]{:S(2)}, u32[]{:S(2)}) collective-permute-start(bf16[2,560,384]{2,1,0:T(8,128)(2,1)} %broadcast_select_fusion.4), channel_id=1, source_target_pairs={{0,16},{16,0},{1,17},{17,1},{2,18},{18,2},{3,19},{19,3},{4,20},{20... | collective-permute-start | bytes 2580488 | tf_op jit(solution)/shard_map/ppermute | solution.py:29
  1142.2 35.8 %collective-permute-start.13 = (bf16[2,560,384]{2,1,0:T(8,128)(2,1)}, bf16[2,560,384]{2,1,0:T(8,128)(2,1)}, u32[]{:S(2)}, u32[]{:S(2)}) collective-permute-start(bf16[2,560,384]{2,1,0:T(8,128)(2,1)} %broadcast_select_fusion.6), channel_id=1, source_target_pairs={{0,16},{16,0},{1,17},{17,1},{2,18},{18,2},{3,19},{19,3},{4,20},{20... | collective-permute-start | bytes 2580488 | tf_op jit(solution)/shard_map/ppermute | solution.py:29
  1145.9 38.9 %collective-permute-start.12 = (bf16[2,560,384]{2,1,0:T(8,128)(2,1)}, bf16[2,560,384]{2,1,0:T(8,128)(2,1)}, u32[]{:S(2)}, u32[]{:S(2)}) collective-permute-start(bf16[2,560,384]{2,1,0:T(8,128)(2,1)} %broadcast_select_fusion.8), channel_id=1, source_target_pairs={{0,16},{16,0},{1,17},{17,1},{2,18},{18,2},{3,19},{19,3},{4,20},{20... | collective-permute-start | bytes 2580488 | tf_op jit(solution)/shard_map/ppermute | solution.py:29
  1146.9 11.2 collective-permute-start.9
  1150.6 37.9 %collective-permute-start.8 = (bf16[2,256,1536]{2,1,0:T(8,128)(2,1)}, bf16[2,256,1536]{2,1,0:T(8,128)(2,1)}, u32[]{:S(2)}, u32[]{:S(2)}) collective-permute-start(bf16[2,256,1536]{2,1,0:T(8,128)(2,1)} %bitcast.71), channel_id=1, source_target_pairs={{0,16},{16,0},{1,17},{17,1},{2,18},{18,2},{3,19},{19,3},{4,20},{20... | collective-permute-start | bytes 4718600 | tf_op jit(solution)/shard_map/ppermute | solution.py:29
  1164.1 4.5 collective-permute-start.10
  1169.6 4.0 collective-permute-start.11
  1173.6 18.5 %collective-permute-start.7 = (bf16[2,256,1536]{2,1,0:T(8,128)(2,1)}, bf16[2,256,1536]{2,1,0:T(8,128)(2,1)}, u32[]{:S(2)}, u32[]{:S(2)}) collective-permute-start(bf16[2,256,1536]{2,1,0:T(8,128)(2,1)} %bitcast.297), channel_id=1, source_target_pairs={{0,16},{16,0},{1,17},{17,1},{2,18},{18,2},{3,19},{19,3},{4,20},{20... | collective-permute-start | bytes 4718600 | tf_op jit(solution)/shard_map/ppermute | solution.py:29
  (65 other events, 165.9 us)

commit v2 on v0

v2 whole, which is shorter than its diff:
```python
import functools
import math

import jax
import jax.numpy as jnp
from jax import lax
from jax.experimental import pallas as pl
from jax.experimental.pallas import tpu as pltpu
from jax.sharding import PartitionSpec as P

HEADS = 12
KV = 2
HEAD = 128

EPS = 1e-06
THETA = 1000000.0

ROW, SEC, COL = "row", "section", "col"

F32 = jnp.float32
BF16 = jnp.bfloat16

COL_LOW = (COL, 1)
COL_HIGH = (COL, 2)
ROW_LOW = (ROW, 1)
SECTION = (SEC, 1)


def swap(value, axis, flip):
    pairs = [(i, i ^ flip) for i in range(lax.axis_size(axis))]
    return lax.ppermute(value, axis, pairs)


def bit_of(index, bit):
    return (index >> bit) & 1


def pick(array, index, axis=0):
    return lax.dynamic_index_in_dim(array, index, axis, keepdims=False)


def ordered(mine, other, bit, axis):
    first = jnp.where(bit == 0, mine, other)
    second = jnp.where(bit == 0, other, mine)
    return jnp.concatenate([first, second], axis=axis)


def row_bits():
    return lax.axis_size(ROW).bit_length() - 1


def norm_backward(stream, inverse, gain, gradient):
    inner = jnp.mean(gradient * gain * stream, axis=-1, keepdims=True)
    d_stream = gain * gradient * inverse - stream * (inverse * inverse * inverse) * inner
    return (d_stream, jnp.sum(gradient * stream * inverse, axis=0, keepdims=True))


def dot(left, right, left_dim, right_dim):
    return lax.dot_general(
        left, right, (((left_dim,), (right_dim,)), ((), ())), preferred_element_type=F32
    )


def layout(lengths, place, row_count):
    section, row, low, high = place
    rows = lax.axis_size(ROW)
    half = row_count // 2
    inside = jnp.arange(row_count, dtype=jnp.int32)
    inside = (((inside // half) ^ low) * half) + inside % half
    own_index = row * row_count + inside
    key_index = ((jnp.arange(rows, dtype=jnp.int32) ^ row) * row_count)[:, None] + inside[None, :]
    slots = 2 * section + (jnp.arange(2, dtype=jnp.int32) ^ high)
    picked = jnp.stack([pick(lengths, slots[0]), pick(lengths, slots[1])])
    ends = jnp.cumsum(picked, axis=1)
    starts = ends - picked
    inside_piece = (own_index[None, None, :] >= starts[:, :, None]) & (
        own_index[None, None, :] < ends[:, :, None]
    )
    first = jnp.sum(jnp.where(inside_piece, starts[:, :, None], 0), axis=1)
    inverse = THETA ** (-(jnp.arange(HEAD // 2, dtype=F32) * 2.0 / HEAD))
    angle = (own_index[None, :] - first).astype(F32).reshape(-1, 1) * inverse
    cosine, sine = jnp.cos(angle), jnp.sin(angle)
    return (
        jnp.concatenate([cosine, cosine], axis=1),
        jnp.concatenate([-sine, sine], axis=1),
        first,
        own_index[None, :],
        key_index.reshape(-1, 1),
    )


MESH = pl.DeviceIdType.MESH
VMEM_LIMIT = 62 * 1024 * 1024


def partner_of(way):
    axis, flip = way
    return {axis: lax.axis_index(axis) ^ flip}


def enter(ways):
    barrier = pltpu.get_barrier_semaphore()
    for way in ways:
        pl.semaphore_signal(barrier, inc=1, device_id=partner_of(way), device_id_type=MESH)
    pl.semaphore_wait(barrier, len(ways))


def remote(source, target, send, recv, way):
    return pltpu.make_async_remote_copy(
        src_ref=source,
        dst_ref=target,
        send_sem=send,
        recv_sem=recv,
        device_id=partner_of(way),
        device_id_type=MESH,
    )


class Links:
    def __init__(self, sems):
        self.send, self.recv = sems
        self.used = 0

    def copy(self, source, target, way):
        slot = self.used
        self.used += 1
        return remote(source, target, self.send.at[slot], self.recv.at[slot], way)


def semaphores(*counts):
    return [pltpu.SemaphoreType.DMA((count,)) for count in counts]


def wait_all(arriving, leaving):
    for copy in arriving:
        copy.wait_recv()
    for copy in leaving:
        copy.wait_send()


class Refs:
    def __init__(self, named, layer=None):
        self.named, self.layer = named, layer

    def __getattr__(self, name):
        return self.named[name] if name in self.named else self.named[name + str(self.layer)]

    def of(self, layer):
        return Refs(self.named, layer)


def layered(layer, **values):
    return {name + str(layer): value for name, value in values.items()}


class Pump:
    def __init__(self, schedule, number=None):
        self.schedule, self.number = schedule, number

    def __call__(self, number):
        return Pump(self.schedule, number)

    def __getattr__(self, point):
        def run():
            for move in self.schedule.get(point[0] + str(self.number) + point[1:], ()):
                move.advance()

        return run


def kernel_call(kernel, collective_id, ways, operands, outs, scratch, flops, moves, schedule):
    vmem = pl.BlockSpec(memory_space=pltpu.VMEM)
    hbm = pl.BlockSpec(memory_space=pl.ANY)
    moved_in = [array for move in moves for array in move.operands]
    moved_out = [out for move in moves for out in move.outs]
    every = list(ways)
    for move in moves:
        every += [way for way in move.ways if way not in every]
    scratch_list = []
    for spec in scratch.values():
        scratch_list += spec if isinstance(spec, list) else [spec]

    def body(*refs):
        refs = list(refs)

        def take(count):
            taken, refs[:] = refs[:count], refs[count:]
            return taken

        named = dict(zip(operands, take(len(operands))))
        sources = [take(len(move.operands)) for move in moves]
        named.update(zip(outs, take(len(outs))))
        targets = [take(len(move.outs)) for move in moves]
        for name, spec in scratch.items():
            named[name] = take(len(spec)) if isinstance(spec, list) else take(1)[0]
        for move, source, target in zip(moves, sources, targets, strict=True):
            if move.name:
                source = [named[move.name]]
            move.bind(source, target, take(len(move.scratch)))

        enter(every)
        kernel(Refs(named), Pump(schedule))
        while any(move.at < len(move.steps) for move in moves):
            for move in moves:
                move.advance()

    results = pl.pallas_call(
        body,
        out_shape=[jax.ShapeDtypeStruct(shape, dtype) for shape, dtype, _ in outs.values()]
        + [jax.ShapeDtypeStruct(shape, BF16) for shape in moved_out],
        in_specs=[vmem if inside else hbm for _, inside in operands.values()] + [hbm] * len(moved_in),
        out_specs=[vmem if inside else hbm for _, _, inside in outs.values()] + [hbm] * len(moved_out),
        scratch_shapes=scratch_list + [ref for move in moves for ref in move.scratch],
        compiler_params=pltpu.CompilerParams(
            collective_id=collective_id, has_side_effects=True, vmem_limit_bytes=VMEM_LIMIT
        ),
        cost_estimate=pl.CostEstimate(flops=flops, bytes_accessed=32 << 20, transcendentals=1 << 20),
    )(*[array for array, _ in operands.values()], *moved_in)
    moved = results[len(outs) :]
    for move in moves:
        move.results, moved = moved[: len(move.outs)], moved[len(move.outs) :]
    return Refs(dict(zip(outs, results)))


def row_hops(bits):
    hops, known = [], [0]
    for bit in reversed(range(bits)):
        step = 1 << bit
        hops += [(slot, slot | step, bit) for slot in known]
        known += [slot | step for slot in known]
    return hops


class Move:
    def __init__(self, source, outs, scratch, ways):
        self.name = source if isinstance(source, str) else None
        self.operands = [] if self.name else [source]
        self.outs, self.scratch, self.ways = outs, scratch, ways
        self.steps, self.at = [], 0

    def advance(self):
        if self.at < len(self.steps):
            self.steps[self.at]()
            self.at += 1


class FfnGather(Move):
    def __init__(self, part, across):
        rows = lax.axis_size(ROW)
        self.flips, self.across = list(range(rows - 1, 0, -1)), across
        outs = [(rows, *part.shape[1:])] * 2
        ways = [(ROW, flip) for flip in self.flips] + [across]
        super().__init__(part, outs, semaphores(rows, rows, rows, rows, 1), ways)

    def bind(self, sources, targets, scratch):
        (part,), (own, other) = sources, targets
        self.blocks = [own, other]
        row_send, row_recv, far_send, far_recv, local_sem = scratch
        row = lax.axis_index(ROW)
        near = part.at[row & 1]
        local = pltpu.make_async_copy(near, own.at[row], local_sem.at[0])
        hops = {
            flip: remote(
                part.at[(row ^ flip) & 1], own.at[row], row_send.at[flip], row_recv.at[flip], (ROW, flip)
            )
            for flip in self.flips
        }
        far = {
            flip: remote(
                own.at[row ^ flip] if flip else near,
                other.at[row ^ flip],
                far_send.at[flip],
                far_recv.at[flip],
                self.across,
            )
            for flip in [0] + self.flips
        }

        def start():
            local.start()
            hops[self.flips[0]].start()

        def start_rest():
            for flip in self.flips[1:]:
                hops[flip].start()

        def forward(flip):
            def step():
                if flip:
                    hops[flip].wait_recv()
                far[flip].start()

            return step

        def finish():
            local.wait()
            wait_all(far.values(), [*hops.values(), *far.values()])

        self.steps = [start, start_rest, *[forward(flip) for flip in [0] + self.flips], finish]


class AttnGather(Move):
    def __init__(self, part):
        rows = lax.axis_size(ROW)
        self.bits = rows.bit_length() - 1
        ways = [(ROW, 1 << bit) for bit in range(self.bits)] + [SECTION]
        super().__init__(part, [(2, rows, *part.shape)], semaphores(rows, rows, rows, rows, 1), ways)

    def bind(self, sources, targets, scratch):
        (part,), (blocks,) = sources, targets
        self.blocks = [blocks.at[0], blocks.at[1]]
        row_send, row_recv, side_send, side_recv, local_sem = scratch
        section, row = lax.axis_index(SEC), lax.axis_index(ROW)

        def place(slot):
            return blocks.at[section, row ^ slot]

        def source(slot):
            return place(slot) if slot else part

        local = pltpu.make_async_copy(part, place(0), local_sem.at[0])
        hops = [
            (slot, filled, remote(source(slot), place(slot), row_send.at[filled], row_recv.at[filled], (ROW, 1 << bit)))
            for slot, filled, bit in row_hops(self.bits)
        ]
        sides = [
            remote(source(slot), place(slot), side_send.at[slot], side_recv.at[slot], SECTION)
            for slot in range(1 << self.bits)
        ]
        arrived = {0}

        def arrive(slot):
            if slot not in arrived:
                arrived.add(slot)
                for _, filled, copy in hops:
                    if filled == slot:
                        copy.wait_recv()
                sides[slot].start()

        def start():
            local.start()
            for slot, _, copy in hops:
                if slot == 0:
                    copy.start()
            sides[0].start()

        def forward():
            for slot, _, copy in hops:
                if slot:
                    arrive(slot)
                    copy.start()

        def finish():
            for slot in range(len(sides)):
                arrive(slot)
            local.wait()
            wait_all(sides, [copy for _, _, copy in hops] + sides)

        self.steps = [start, forward, finish]


class TokenGather(Move):
    def __init__(self, own, shape, a, b, sides):
        self.a, self.b, self.sides = a, b, sides
        ways = [a, b] + ([SECTION] if sides else [])
        super().__init__(own, [(4, 1 + sides, *shape)], semaphores(8, 8, 1), ways)

    def bind(self, sources, targets, scratch):
        (own,), (blocks,) = sources, targets
        send, recv, local_sem = scratch
        local = pltpu.make_async_copy(own, blocks.at[0, 0], local_sem.at[0])
        gather = BlockGather(Links((send, recv)), blocks, self.a, self.b, self.sides, own)

        def start():
            local.start()
            for copy in (gather.a, gather.b, gather.sides[0]):
                copy.start()

        def forward():
            gather.a.wait_recv()
            gather.ab.start()
            gather.sides[1].start()
            gather.b.wait_recv()
            gather.ba.start()
            gather.sides[2].start()

        def last():
            gather.ab.wait_recv()
            gather.ba.wait_recv()
            gather.sides[3].start()

        def finish():
            local.wait()
            wait_all(gather.sides, gather.copies)

        self.steps = [start, forward, last, finish]


class Across(Move):
    def __init__(self, grad, n, way):
        self.n, self.way = n, way
        super().__init__(grad, [(n, grad.shape[1])], semaphores(1, 1), [way])

    def bind(self, sources, targets, scratch):
        (grad,), (arrived,) = sources, targets
        send, recv = scratch
        copy = remote(grad.at[pl.ds(self.n, self.n)], arrived, send.at[0], recv.at[0], self.way)
        self.steps = [copy.start, lambda: wait_all([copy], [copy])]


class Rows(Move):
    def __init__(self, total):
        rows = total.shape[0]
        self.flips = list(range(1, rows))
        ways = [(ROW, flip) for flip in self.flips]
        super().__init__(total, [total.shape], semaphores(rows, rows), ways)

    def bind(self, sources, targets, scratch):
        (total,), (arrived,) = sources, targets
        send, recv = scratch
        copies = row_copies(total, arrived, send, recv, self.flips)

        def start():
            for copy in copies:
                copy.start()

        self.steps = [start, lambda: wait_all(copies, copies)]


def row_copies(total, arrived, send, recv, flips):
    row = lax.axis_index(ROW)
    return [
        remote(total.at[row ^ flip], arrived.at[flip], send.at[flip], recv.at[flip], (ROW, flip))
        for flip in flips
    ]


class GradScatter(Move):
    def __init__(self, grad, n, way):
        rows, width = lax.axis_size(ROW), grad.shape[1]
        self.n, self.way, self.flips = n, way, list(range(1, rows))
        shape = (rows, n, width // rows)
        scratch = [pltpu.VMEM((n, width), BF16), pltpu.VMEM((n, width), BF16), pltpu.VMEM(shape, BF16)]
        scratch += semaphores(1, 1, 1, 1, rows, rows)
        ways = [way] + [(ROW, flip) for flip in self.flips]
        super().__init__(grad, [shape[1:], shape], scratch, ways)

    def bind(self, sources, targets, scratch):
        (grad,), (own, arrived) = sources, targets
        mine, theirs, total, local_sem, own_sem, far_send, far_recv, row_send, row_recv = scratch
        n, row = self.n, lax.axis_index(ROW)
        depth = total.shape[2]
        local = pltpu.make_async_copy(grad.at[pl.ds(0, n)], mine, local_sem.at[0])
        far = remote(grad.at[pl.ds(n, n)], theirs, far_send.at[0], far_recv.at[0], self.way)
        keep = pltpu.make_async_copy(total.at[row], own, own_sem.at[0])
        copies = row_copies(total, arrived, row_send, row_recv, self.flips)

        def start():
            local.start()
            far.start()

        def forward():
            local.wait()
            far.wait_recv()
            for block in range(total.shape[0]):
                at = slice(block * depth, (block + 1) * depth)
                total[block] = (mine[:, at].astype(F32) + theirs[:, at].astype(F32)).astype(BF16)
            for copy in copies + [keep]:
                copy.start()

        def finish():
            keep.wait()
            wait_all(copies, copies + [far])

        self.steps = [start, forward, finish]


class AttnScatter(Move):
    def __init__(self, name, shape):
        rows, width, m = lax.axis_size(ROW), shape[1], shape[0] // 2
        self.bits, self.m = rows.bit_length() - 1, m
        blocks = (rows, m, width // rows)
        scratch = [
            pltpu.VMEM((m, width), BF16),
            pltpu.VMEM(blocks, F32),
            pltpu.VMEM(blocks, BF16),
            pltpu.VMEM(blocks, BF16),
        ]
        scratch += semaphores(1, 1, 1, rows, rows)
        ways = [SECTION] + [(ROW, 1 << bit) for bit in range(self.bits)]
        super().__init__(name, [blocks[1:]], scratch, ways)

    def bind(self, sources, targets, scratch):
        (grad,), (out,) = sources, targets
        theirs, total, going, coming, out_sem, side_send, side_recv, send, recv = scratch
        m, row, section = self.m, lax.axis_index(ROW), lax.axis_index(SEC)
        depth = total.shape[2]
        mine = grad.at[pl.ds(pl.multiple_of(section * m, m), m)]
        side = remote(
            grad.at[pl.ds(pl.multiple_of((1 - section) * m, m), m)],
            theirs,
            side_send.at[0],
            side_recv.at[0],
            SECTION,
        )
        keep = pltpu.make_async_copy(going.at[0], out, out_sem.at[0])
        hops = [
            (slot, filled, remote(going.at[filled], coming.at[filled], send.at[filled], recv.at[filled], (ROW, 1 << bit)))
            for slot, filled, bit in reversed(row_hops(self.bits))
        ]

        def sum_sides():
            side.wait_recv()
            for block in range(total.shape[0]):
                at = slice(block * depth, (block + 1) * depth)
                total[row ^ block] = mine[:, at].astype(F32) + theirs[:, at].astype(F32)
            send_bit(0)

        def send_bit(bit):
            for slot, filled, copy in hops:
                if filled - slot == 1 << bit:
                    going[filled] = total[filled].astype(BF16)
                    copy.start()

        def add_bit(bit):
            for slot, filled, copy in hops:
                if filled - slot == 1 << bit:
                    copy.wait_recv()
                    total[slot] = total[slot] + coming[filled].astype(F32)

        def hop(bit):
            def step():
                add_bit(bit - 1)
                send_bit(bit)

            return step

        def finish():
            add_bit(self.bits - 1)
            going[0] = total[0].astype(BF16)
            keep.start()
            keep.wait()
            wait_all([], [copy for _, _, copy in hops] + [side])

        self.steps = [side.start, sum_sides, *[hop(bit) for bit in range(1, self.bits)], finish]


class NoCopy:
    def start(self):
        pass

    wait_recv = wait_send = start


class BlockGather:
    def __init__(self, links, blocks, a, b, sides=True, own=None, there=False):
        h = blocks.shape[2] // 2
        own = blocks.at[0, 0] if own is None else own
        if there:
            self.a = self.b = self.ab = self.ba = NoCopy()
        else:
            self.a = links.copy(own, blocks.at[1, 0], a)
            self.b = links.copy(own, blocks.at[2, 0], b)
            self.ab = links.copy(blocks.at[1, 0, pl.ds(0, h)], blocks.at[3, 0, pl.ds(0, h)], b)
            self.ba = links.copy(blocks.at[2, 0, pl.ds(h, h)], blocks.at[3, 0, pl.ds(h, h)], a)
        self.sides = [NoCopy()] * 4
        if sides and not there:
            self.sides = [
                links.copy(blocks.at[k, 0] if k else own, blocks.at[k, 1], SECTION) for k in range(4)
            ]
        self.copies = [self.a, self.b, self.ab, self.ba, *self.sides]


class Scatter:
    def __init__(self, links, r, corner_in, edge_in, a, b):
        self.r, self.corner_in, self.edge_in = r, corner_in, edge_in
        self.corner_b = links.copy(r.corner_out.at[0], corner_in.at[0], b)
        self.corner_a = links.copy(r.corner_out.at[1], corner_in.at[1], a)
        self.edge_a = links.copy(r.edge_out.at[0], edge_in.at[0], a)
        self.edge_b = links.copy(r.edge_out.at[1], edge_in.at[1], b)
        self.copies = [self.corner_b, self.corner_a, self.edge_a, self.edge_b]

    def send_corner(self, value):
        corner = self.r.corner_out
        corner[...] = value.astype(BF16).reshape(corner.shape)
        self.corner_b.start()
        self.corner_a.start()

    def send_edge_a(self, value):
        edge, h = self.r.edge_out, value.shape[0] // 2
        self.corner_b.wait_recv()
        edge[0, :h] = (value[:h] + self.corner_in[0].astype(F32)).astype(BF16)
        edge[0, h:] = value[h:].astype(BF16)
        self.edge_a.start()

    def send_edge_b(self, value):
        edge, h = self.r.edge_out, value.shape[0] // 2
        self.corner_a.wait_recv()
        edge[1, :h] = value[:h].astype(BF16)
        edge[1, h:] = (value[h:] + self.corner_in[1].astype(F32)).astype(BF16)
        self.edge_b.start()

    def total(self, value):
        self.edge_a.wait_recv()
        self.edge_b.wait_recv()
        return value + self.edge_in[0].astype(F32) + self.edge_in[1].astype(F32)


def save(started, sems, pairs):
    for source, target in pairs:
        started.append(pltpu.make_async_copy(source, target, sems.at[len(started)]))
        started[-1].start()


class Load:
    def __init__(self, sources, target, stage, sems):
        self.sources, self.target, self.stage, self.copies, self.sems = sources, target, stage, [], sems
        if stage is None:
            for i, source in enumerate(sources):
                blocks, rows, columns = source.shape
                for block in range(blocks):
                    place = target.at[pl.ds(i * rows, rows), pl.ds(block * columns, columns)]
                    self.copies.append(
                        pltpu.make_async_copy(source.at[block], place, sems.at[len(self.copies)])
                    )

    def start(self):
        for copy in self.copies:
            copy.start()
        filled = sum(source.shape[1] for source in self.sources)
        if filled < self.target.shape[0]:
            self.target[filled:] = jnp.zeros((self.target.shape[0] - filled, self.target.shape[1]), BF16)

    def wait(self):
        for copy in self.copies:
            copy.wait()
        if self.stage is not None:
            for i, source in enumerate(self.sources):
                blocks, rows, columns = source.shape
                buffer = self.stage.at[:, pl.ds(0, rows)]
                copy = pltpu.make_async_copy(source, buffer, self.sems.at[0])
                copy.start()
                copy.wait()
                for block in range(blocks):
                    self.target[i * rows : (i + 1) * rows, block * columns : (block + 1) * columns] = (
                        self.stage[block, :rows]
                    )


def stage_of(sizes):
    if sizes.depth % 128 == 0:
        return {}
    return dict(stage=pltpu.VMEM((sizes.rows, max(sizes.unit, sizes.attn // 2), sizes.depth), BF16))


def stage_in(r):
    return r.named.get("stage")


def hidden_tiles(hidden):
    return [(at, min(384, hidden - at)) for at in range(0, hidden, 384)]


def padded(hidden):
    return -(-hidden // 128) * 128


def width_tiles(width):
    return [(at, 512) for at in range(0, width, 512)]


def put_partial(r, k, at, size, value):
    n = value.shape[0] // 2
    r.partial[k, :, pl.ds(at, size)] = value[:n]
    r.side_out[k, :, pl.ds(at, size)] = value[n:].astype(BF16)


def side_copies(links, r):
    return [links.copy(r.side_out.at[k], r.side_in.at[k], SECTION) for k in range(4)]


def with_side(r, k):
    return r.partial[k] + r.side_in[k].astype(F32)


def ffn_forward(r, layer, a, at, weights):
    r = r.of(layer)
    links = Links(r.f_sems)
    blocks, result_ref, second_ref = r.f_blocks, r.result, r.second
    gate_out, up_out, act_out = r.hidden[0], r.hidden[1], r.hidden[2]
    n, width = blocks.shape[2:]
    hidden = r.w_gate.shape[0]
    second = second_ref[...]
    inverse = lax.rsqrt(jnp.mean(second * second, axis=-1, keepdims=True) + EPS)
    blocks[0, 0] = (second * inverse * r.gain_ffn[...]).astype(BF16)
    gather = BlockGather(links, blocks, a, ROW_LOW)
    sides = side_copies(links, r)
    scatter = Scatter(links, r, r.f_corner_in, r.f_edge_in, a, ROW_LOW)
    gather.a.start()
    gather.b.start()
    gather.sides[0].start()
    at(layer).f_sent()
    gather.a.wait_recv()
    gather.ab.start()
    gather.sides[1].start()
    gather.b.wait_recv()
    gather.ba.start()
    gather.sides[2].start()
    gather.ab.wait_recv()
    gather.ba.wait_recv()
    gather.sides[3].start()
    at(layer).f_gathered()
    stage = stage_in(r)
    loads = [
        Load(move.blocks, weight, stage, sems)
        for move, weight, sems in zip(weights, (r.w_gate, r.w_up, r.w_down), r.f_load_sems, strict=True)
    ]
    loads[0].start()
    loads[1].start()
    loads[0].wait()
    loads[1].wait()
    saves = []
    for k in range(4):
        gather.sides[k].wait_recv()
        x = blocks[k].reshape(2 * n, width)
        rows = pl.ds(k * 2 * n, 2 * n)
        for lane, size in hidden_tiles(hidden):
            lanes = pl.ds(lane, size)
            gate = dot(x, r.w_gate[lanes], 1, 1)
            up = dot(x, r.w_up[lanes], 1, 1)
            act = gate / (1.0 + jnp.exp(-gate)) * up
            gate_out[rows, lanes] = gate.astype(BF16)
            up_out[rows, lanes] = up.astype(BF16)
            act_out[rows, lanes] = act.astype(BF16)
        pairs = [(blocks.at[k], r.f_blocks_hbm.at[k])]
        for source, target in ((gate_out, r.gate), (up_out, r.up), (act_out, r.act)):
            pairs.append((source.at[rows], target.at[rows]))
        save(saves, r.f_save_sem, pairs)
        getattr(at(layer), "f_up" + str(k))()
    at(layer).f_up()
    loads[2].start()
    loads[2].wait()

    def down(k):
        act = act_out[pl.ds(k * 2 * n, 2 * n)]
        for lane, size in width_tiles(width):
            put_partial(r, k, lane, size, dot(act, r.w_down[:, pl.ds(lane, size)], 1, 0))
        sides[k].start()

    down(3)
    down(1)
    sides[3].wait_recv()
    scatter.send_corner(with_side(r, 3))
    down(2)
    sides[1].wait_recv()
    scatter.send_edge_a(with_side(r, 1))
    sides[2].wait_recv()
    scatter.send_edge_b(with_side(r, 2))
    down(0)
    at(layer).f_edges()
    sides[0].wait_recv()
    result_ref[...] = second_ref[...] + scatter.total(with_side(r, 0))
    at(layer).f_end()
    wait_all([], [*gather.copies, *sides, *scatter.copies])
    for copy in saves:
        copy.wait()


def ffn_backward(r, layer, a, at, gathers):
    r = r.of(layer)
    links = Links(r.f_sems)
    blocks, second_ref, grad_ref = r.f_blocks, r.second, r.of(layer + 1).d_entry
    gate_in, up_in = r.hidden
    d_gate_out, d_up_out = r.hidden
    n, width = blocks.shape[2:]
    hidden = r.w_gate.shape[0]
    stage = stage_in(r)
    loads = [
        Load(halves, weight, stage, sems)
        for halves, weight, sems in zip(
            ([r.gate_own, r.gate_other], [r.up_own, r.up_other], [r.down_own, r.down_other]),
            (r.w_gate, r.w_up, r.w_down),
            r.f_load_sems,
            strict=True,
        )
    ]
    for load in loads:
        load.start()
    more = [(r.gate, gate_in), (r.up, up_in)]
    if not gathers:
        more.append((r.gathered, blocks))
    extra = []
    save(extra, r.f_extra_sem, more)
    if gathers:
        blocks[0, 0] = grad_ref[...]
    gather = BlockGather(links, blocks, a, ROW_LOW, there=not gathers)
    sides = side_copies(links, r)
    scatter = Scatter(links, r, r.f_corner_in, r.f_edge_in, a, ROW_LOW)
    saves = []

    def step(k):
        g = blocks[k].reshape(2 * n, width)
        rows = pl.ds(k * 2 * n, 2 * n)
        for lane, size in hidden_tiles(hidden):
            lanes = pl.ds(lane, size)
            d_act = dot(g, r.w_down[lanes], 1, 1)
            gate = gate_in[rows, lanes].astype(F32)
            up = up_in[rows, lanes].astype(F32)
            sigma = 1.0 / (1.0 + jnp.exp(-gate))
            d_gate_out[rows, lanes] = (d_act * up * sigma * (1.0 + gate * (1.0 - sigma))).astype(BF16)
            d_up_out[rows, lanes] = (d_act * gate * sigma).astype(BF16)
        pairs = [(d_gate_out.at[rows], r.d_gate.at[rows]), (d_up_out.at[rows], r.d_up.at[rows])]
        if gathers:
            pairs.append((blocks.at[k], r.f_blocks_hbm.at[k]))
        save(saves, r.f_save_sem, pairs)
        d_gate = d_gate_out[rows]
        d_up = d_up_out[rows]
        for lane, size in width_tiles(width):
            lanes = pl.ds(lane, size)
            value = dot(d_gate, r.w_gate[:, lanes], 1, 0) + dot(d_up, r.w_up[:, lanes], 1, 0)
            put_partial(r, k, lane, size, value)
        sides[k].start()

    gather.a.start()
    gather.b.start()
    gather.sides[0].start()
    at(layer).f_sent()
    for load in loads:
        load.wait()
    for copy in extra:
        copy.wait()
    gather.sides[0].wait_recv()
    step(0)
    gather.a.wait_recv()
    gather.ab.start()
    gather.sides[1].start()
    gather.b.wait_recv()
    gather.ba.start()
    gather.sides[2].start()
    gather.sides[1].wait_recv()
    step(1)
    gather.ab.wait_recv()
    gather.ba.wait_recv()
    gather.sides[3].start()
    gather.sides[3].wait_recv()
    step(3)
    sides[3].wait_recv()
    scatter.send_corner(with_side(r, 3))
    at(layer).f_corner()
    gather.sides[2].wait_recv()
    step(2)
    sides[1].wait_recv()
    scatter.send_edge_a(with_side(r, 1))
    sides[2].wait_recv()
    scatter.send_edge_b(with_side(r, 2))
    at(layer).f_edges()
    sides[0].wait_recv()
    d_normed = scatter.total(with_side(r, 0))
    second = second_ref[...]
    inverse = lax.rsqrt(jnp.mean(second * second, axis=-1, keepdims=True) + EPS)
    d_second, d_gain = norm_backward(second, inverse, r.gain_ffn[...], d_normed)
    r.d_gain_ffn[...] = d_gain
    r.d_second[...] = grad_ref[...].astype(F32) + d_second
    at(layer).f_end()
    wait_all([], [*gather.copies, *sides, *scatter.copies])
    for copy in saves:
        copy.wait()


def turn(vectors, cosine, sine):
    return vectors * cosine + pltpu.roll(vectors, HEAD // 2, 1) * sine


def seen(r, slot):
    key = r.key[...]
    visible = (key >= r.start[pl.ds(slot, 1)]) & (key <= r.own[...])
    return jnp.where(visible, 0.0, -1e30)


def attention_weights(r):
    weights = r.w_attn
    heads_width = (weights.shape[0] - 2 * HEAD) // 2
    return (
        weights.at[pl.ds(0, heads_width)],
        weights.at[pl.ds(heads_width, heads_width)],
        weights.at[pl.ds(2 * heads_width, 2 * HEAD)],
    )


def column_gather(links, blocks):
    h = blocks.shape[1] // 2
    return (
        links.copy(blocks.at[0], blocks.at[1], COL_LOW),
        links.copy(blocks.at[0], blocks.at[2], COL_HIGH),
        links.copy(blocks.at[1, pl.ds(0, h)], blocks.at[3, pl.ds(0, h)], COL_HIGH),
        links.copy(blocks.at[2, pl.ds(h, h)], blocks.at[3, pl.ds(h, h)], COL_LOW),
    )


def attention_forward(r, layer, at, gather):
    r = r.of(layer)
    links = Links(r.a_sems)
    entry, kv, bias, partial = r.entry, r.kv, r.bias, r.partial
    normed, query, mixed, lse_ref = r.normed, r.query, r.mixed, r.lse
    cos_ref, sin_ref = r.cos, r.sin
    n, width = entry.shape[1:]
    tokens = 2 * n
    rows = kv.shape[1]
    w_query, w_out, w_pair = attention_weights(r)
    heads = w_query.shape[0] // HEAD
    bits = rows.bit_length() - 1
    scale = 1.0 / math.sqrt(HEAD)
    stage = stage_in(r)
    load = Load(gather.blocks, r.w_attn, stage, r.a_load_sem)
    scatter = Scatter(links, r, r.a_corner_in, r.a_edge_in, COL_LOW, COL_HIGH)
    hops = [
        [(slot, filled, links.copy(kv.at[b, slot], kv.at[b, filled], (ROW, 1 << bit)))
         for slot, filled, bit in row_hops(bits)]
        for b in range(2)
    ]
    copies = scatter.copies + [copy for group in hops for _, _, copy in group]

    def normalise(k):
        x = entry[k].astype(F32)
        inverse = lax.rsqrt(jnp.mean(x * x, axis=-1, keepdims=True) + EPS)
        normed[pl.ds(k * n, n)] = (x * inverse * r.gain_attn[...]).astype(BF16)

    def project_pair(b):
        where = pl.ds(b * tokens, tokens)
        pair = dot(normed[where], w_pair[...], 1, 1) + r.b_pair[...]
        kv[b, 0, :, :HEAD] = turn(pair[:, :HEAD], cos_ref[where], sin_ref[where]).astype(BF16)
        kv[b, 0, :, HEAD:] = pair[:, HEAD:].astype(BF16)
        for slot, _, copy in hops[b]:
            if slot == 0:
                copy.start()

    def project_query(b):
        where = pl.ds(b * tokens, tokens)
        projected = dot(normed[where], w_query[...], 1, 1) + r.b_query[...]
        for head in range(heads):
            lanes = slice(head * HEAD, (head + 1) * HEAD)
            query[where, lanes] = turn(projected[:, lanes], cos_ref[where], sin_ref[where]).astype(BF16)

    arrived = [set(), set()]

    def arrive(b, slot):
        for _, filled, copy in hops[b]:
            if filled == slot and slot not in arrived[b]:
                copy.wait_recv()
                arrived[b].add(slot)

    if layer:
        entry[0] = r.result0[...].astype(BF16)
        to_low, to_high, corner_high, corner_low = column_gather(links, entry)
        copies += [to_low, to_high, corner_high, corner_low]
        to_low.start()
        to_high.start()
        at(layer).a_begin()
        load.start()
        normalise(0)
        to_low.wait_recv()
        corner_high.start()
        to_high.wait_recv()
        corner_low.start()
        normalise(1)
        normalise(2)
        load.wait()
        project_pair(0)
        corner_high.wait_recv()
        corner_low.wait_recv()
        normalise(3)
        project_pair(1)
    else:
        at(layer).a_begin()
        for k in range(4):
            normalise(k)
        at(layer).a_normed()
        load.start()
        load.wait()
        project_pair(1)
        project_pair(0)
    at(layer).a_pairs()
    project_query(1)
    project_query(0)
    at(layer).a_queries()
    for b in (1, 0):
        for slot, _, copy in hops[b]:
            if slot:
                arrive(b, slot)
                copy.start()
    at(layer).a_relayed()
    saves = []
    for b in (1, 0):
        for slot in range(1, rows):
            arrive(b, slot)
        save(saves, r.a_save_sem, [(kv.at[b], r.kv_hbm.at[b])])
        keys = kv[b, :, :, :HEAD].reshape(rows * tokens, HEAD)
        values = kv[b, :, :, HEAD:].reshape(rows * tokens, HEAD)
        where = pl.ds(b * tokens, tokens)
        bias[...] = seen(r, b)
        for head in range(heads):
            lanes = slice(head * HEAD, (head + 1) * HEAD)
            scores = dot(keys, query[where, lanes], 1, 1) * scale + bias[...]
            top = jnp.max(scores, axis=0, keepdims=True)
            raised = jnp.exp(scores - top)
            total = jnp.sum(raised, axis=0, keepdims=True)
            lse_ref[b, pl.ds(head, 1)] = top + jnp.log(total)
            probs = (raised * (1.0 / total)).astype(BF16)
            mixed[where, lanes] = dot(probs, values, 0, 0).astype(BF16)
            if b == 0:
                getattr(at(layer), "a_head" + str(head))()
        for k in (2 * b + 1, 2 * b):
            for lane, size in width_tiles(width):
                partial[k, :, pl.ds(lane, size)] = dot(
                    mixed[pl.ds(k * n, n)], w_out[:, pl.ds(lane, size)], 1, 0
                )
        if b == 1:
            scatter.send_corner(partial[3])
            at(layer).a_half()
    scatter.send_edge_b(partial[2])
    scatter.send_edge_a(partial[1])
    if layer:
        save(saves, r.a_save_sem, [(entry, r.entry_hbm)])
    at(layer).a_edges()
    r.second[...] = entry[0].astype(F32) + scatter.total(partial[0])
    at(layer).a_end()
    wait_all([], copies)
    for copy in saves:
        copy.wait()


def attention_backward(r, layer, at):
    r = r.of(layer)
    links = Links(r.a_sems)
    blocks, kv, bias, partial = r.a_blocks, r.kv, r.bias, r.partial
    d_mixed, d_kv, d_kv_out, d_kv_in = r.d_mixed, r.d_kv, r.d_kv_out, r.d_kv_in
    query, d_query, d_pair = r.query, r.d_query, r.d_pair
    share_out, share_in = r.share_out, r.share_in
    cos_ref, sin_ref = r.cos, r.sin
    n, width = blocks.shape[1:]
    tokens = 2 * n
    rows = kv.shape[1]
    w_query, w_out, w_pair = attention_weights(r)
    heads_width = w_query.shape[0]
    heads = heads_width // HEAD
    bits = rows.bit_length() - 1
    scale = 1.0 / math.sqrt(HEAD)
    stage = stage_in(r)
    load = Load([r.attn_blocks.at[0], r.attn_blocks.at[1]], r.w_attn, stage, r.a_load_sem)
    load.start()
    blocks[0] = r.d_second[...].astype(BF16)
    to_low, to_high, corner_high, corner_low = column_gather(links, blocks)
    hops = [
        [(slot, filled, links.copy(d_kv_out.at[b, filled], d_kv_in.at[b, filled], (ROW, 1 << bit)))
         for slot, filled, bit in reversed(row_hops(bits))]
        for b in range(2)
    ]
    share = [links.copy(share_out.at[b], share_in.at[b], COL_LOW) for b in range(2)]
    scatter = Scatter(links, r, r.a_corner_in, r.a_edge_in, COL_LOW, COL_HIGH)

    def unmix(k):
        d_mixed[pl.ds(k * n, n)] = dot(blocks[k], w_out[...], 1, 1).astype(BF16)

    def attend(b):
        keys = kv[b, :, :, :HEAD].reshape(rows * tokens, HEAD)
        values = kv[b, :, :, HEAD:].reshape(rows * tokens, HEAD)
        where = pl.ds(b * tokens, tokens)
        bias[...] = seen(r, b)
        for head in range(heads):
            lanes = slice(head * HEAD, (head + 1) * HEAD)
            q = query[where, lanes]
            d_o = d_mixed[where, lanes]
            scores = dot(keys, q, 1, 1) * scale + bias[...]
            probs = jnp.exp(scores - r.lse[b, pl.ds(head, 1)])
            d_probs = dot(values, d_o, 1, 1)
            delta = jnp.sum(d_probs * probs, axis=0, keepdims=True)
            d_scores = (probs * (d_probs - delta)).astype(BF16)
            d_keys = (dot(d_scores, q, 1, 0) * scale).reshape(rows, tokens, HEAD)
            d_values = dot(probs.astype(BF16), d_o, 1, 0).reshape(rows, tokens, HEAD)
            if head:
                d_keys = d_keys + d_kv[b, :, :, :HEAD]
                d_values = d_values + d_kv[b, :, :, HEAD:]
            d_kv[b, :, :, :HEAD] = d_keys
            d_kv[b, :, :, HEAD:] = d_values
            turned = dot(d_scores, keys, 0, 0) * scale
            d_query[where, lanes] = turn(turned, cos_ref[where], -sin_ref[where]).astype(BF16)

    def send_bit(b, step):
        for slot, filled, copy in hops[b]:
            if filled - slot == step:
                d_kv_out[b, filled] = d_kv[b, filled].astype(BF16)
                copy.start()

    def add_bit(b, step):
        for slot, filled, copy in hops[b]:
            if filled - slot == step:
                copy.wait_recv()
                d_kv[b, slot] = d_kv[b, slot] + d_kv_in[b, filled].astype(F32)

    def share_pair(b):
        share_out[b] = d_kv[b, 0, n:].astype(BF16)
        share[b].start()

    def finish_pair(b):
        share[b].wait_recv()
        total = d_kv[b, 0, :n] + share_in[b].astype(F32)
        where = pl.ds(b * tokens, n)
        rows_of = pl.ds(b * n, n)
        d_pair[rows_of, :HEAD] = turn(total[:, :HEAD], cos_ref[where], -sin_ref[where]).astype(BF16)
        d_pair[rows_of, HEAD:] = total[:, HEAD:].astype(BF16)

    def unproject(k):
        for lane, size in width_tiles(width):
            lanes = pl.ds(lane, size)
            value = dot(d_query[pl.ds(k * n, n)], w_query[:, lanes], 1, 0)
            if k % 2 == 0:
                value = value + dot(d_pair[pl.ds(k // 2 * n, n)], w_pair[:, lanes], 1, 0)
            partial[k, :, lanes] = value

    to_low.start()
    to_high.start()
    at(layer).a_sent()
    load.wait()
    unmix(0)
    to_low.wait_recv()
    corner_high.start()
    to_high.wait_recv()
    corner_low.start()
    at(layer).a_relayed()
    unmix(1)
    unmix(2)
    corner_high.wait_recv()
    corner_low.wait_recv()
    unmix(3)
    attend(1)
    send_bit(1, 1)
    unproject(3)
    scatter.send_corner(partial[3])
    attend(0)
    send_bit(0, 1)
    for bit in range(1, bits):
        for b in (1, 0):
            add_bit(b, 1 << (bit - 1))
            send_bit(b, 1 << bit)
    at(layer).a_hops()
    unproject(1)
    scatter.send_edge_a(partial[1])
    for b in (1, 0):
        add_bit(b, 1 << (bits - 1))
        share_pair(b)
    finish_pair(1)
    unproject(2)
    scatter.send_edge_b(partial[2])
    at(layer).a_edges()
    finish_pair(0)
    unproject(0)
    r.d_bias_query[...] = jnp.sum(d_query[...].astype(F32), axis=0, keepdims=True)
    r.d_bias_pair[...] = jnp.sum(d_pair[...].astype(F32), axis=0, keepdims=True)
    a_grad, normed = r.a_grad, r.normed
    own_blocks = blocks[...].reshape(4 * n, width)
    for lane, size in width_tiles(width):
        lanes = pl.ds(lane, size)
        a_grad[:heads_width, lanes] = dot(d_query[...], normed[:, lanes], 0, 0).astype(BF16)
        a_grad[heads_width : 2 * heads_width, lanes] = dot(
            r.mixed[...], own_blocks[:, lane : lane + size], 0, 0
        ).astype(BF16)
        normed_own = jnp.concatenate([normed[:n, lanes], normed[tokens : tokens + n, lanes]])
        a_grad[2 * heads_width :, lanes] = dot(d_pair[...], normed_own, 0, 0).astype(BF16)
    at(layer).a_grads()
    d_normed = scatter.total(partial[0])
    stream = r.entry[...].astype(F32)
    inverse = lax.rsqrt(jnp.mean(stream * stream, axis=-1, keepdims=True) + EPS)
    d_first, d_gain = norm_backward(stream, inverse, r.gain_attn[...], d_normed)
    r.d_gain_attn[...] = d_gain
    r.d_entry[...] = (r.d_second[...] + d_first).astype(BF16)
    at(layer).a_end()
    copies = [to_low, to_high, corner_high, corner_low, *share, *scatter.copies]
    wait_all([], copies + [copy for group in hops for _, _, copy in group])


def sum_vectors(r, at, links):
    vector = r.vector
    vector[...] = jnp.zeros_like(vector)
    col = lax.axis_index(COL)
    lanes = r.d_gain_ffn0.shape[1] // HEAD
    heads = r.d_bias_query0.shape[1] // HEAD
    each = vector.shape[0] // 2
    for layer in range(2):
        of = r.of(layer)
        for gain, first in ((of.d_gain_attn, 0), (of.d_gain_ffn, lanes)):
            for i in range(lanes):
                vector[pl.ds(layer * each + first + i, 1)] = gain[:, i * HEAD : (i + 1) * HEAD]
        for i in range(heads):
            place = layer * each + 2 * lanes + col * heads + i
            vector[pl.ds(place, 1)] = of.d_bias_query[:, i * HEAD : (i + 1) * HEAD]
        for i in range(2):
            place = layer * each + 3 * lanes + i * KV + (col >> 1)
            vector[pl.ds(place, 1)] = of.d_bias_pair[:, i * HEAD : (i + 1) * HEAD]
    ways = [SECTION, COL_LOW, COL_HIGH] + [(ROW, 1 << bit) for bit in range(row_bits())]
    copies = []
    for i, way in enumerate(ways):
        r.vector_out[i] = vector[...]
        copies.append(links.copy(r.vector_out.at[i], r.vector_in.at[i], way))
        copies[-1].start()
        at(i).s_step()
        copies[-1].wait_recv()
        vector[...] = vector[...] + r.vector_in[i]
    r.sums[...] = vector[...]
    wait_all([], copies)


class Sizes:
    def __init__(self, n, width, rows, hidden, attn, depth):
        self.n, self.width, self.rows, self.depth = n, width, rows, depth
        self.unit, self.hidden, self.attn = hidden // 2, padded(hidden), attn
        self.heads_width = (attn - 2 * HEAD) // 2
        self.heads = self.heads_width // HEAD


def common_scratch(sizes):
    n, width = sizes.n, sizes.width
    return dict(
        partial=pltpu.VMEM((4, n, width), F32),
        corner_out=pltpu.VMEM((2, n // 2, width), BF16),
        edge_out=pltpu.VMEM((2, n, width), BF16),
        **stage_of(sizes),
    )


def ffn_scratch(sizes, count, saves):
    n, width, hidden = sizes.n, sizes.width, sizes.hidden
    each = 2 * sizes.rows
    return dict(
        w_gate=pltpu.VMEM((hidden, width), BF16),
        w_up=pltpu.VMEM((hidden, width), BF16),
        w_down=pltpu.VMEM((hidden, width), BF16),
        hidden=[pltpu.VMEM((8 * n, hidden), BF16) for _ in range(count)],
        side_out=pltpu.VMEM((4, n, width), BF16),
        f_load_sems=semaphores(each, each, each),
        f_extra_sem=pltpu.SemaphoreType.DMA((3,)),
        f_save_sem=pltpu.SemaphoreType.DMA((4 * saves,)),
    )


def ffn_buffers(sizes, layer):
    n, width = sizes.n, sizes.width
    return layered(
        layer,
        f_blocks=pltpu.VMEM((4, 2, n, width), BF16),
        side_in=pltpu.VMEM((4, n, width), BF16),
        f_corner_in=pltpu.VMEM((2, n // 2, width), BF16),
        f_edge_in=pltpu.VMEM((2, n, width), BF16),
        f_sems=semaphores(16, 16),
    )


def attention_scratch(sizes):
    tokens = 2 * sizes.n
    return dict(
        w_attn=pltpu.VMEM((sizes.attn, sizes.width), BF16),
        bias=pltpu.VMEM((sizes.rows * tokens, tokens), F32),
        a_load_sem=pltpu.SemaphoreType.DMA((2 * sizes.rows,)),
        a_save_sem=pltpu.SemaphoreType.DMA((3,)),
    )


def attention_buffers(sizes, layer, backward):
    n, width, rows = sizes.n, sizes.width, sizes.rows
    pairs = (2, rows, 2 * n, 2 * HEAD)
    count = 10 + 2 * (rows - 1)
    buffers = dict(
        a_corner_in=pltpu.VMEM((2, n // 2, width), BF16),
        a_edge_in=pltpu.VMEM((2, n, width), BF16),
        a_sems=semaphores(count, count),
    )
    if backward:
        buffers.update(a_blocks=pltpu.VMEM((4, n, width), BF16))
        buffers.update(d_kv_in=pltpu.VMEM(pairs, BF16))
        buffers.update(share_in=pltpu.VMEM((2, n, 2 * HEAD), BF16))
    else:
        buffers.update(kv=pltpu.VMEM(pairs, BF16))
    return layered(layer, **buffers)


def attention_back_scratch(sizes):
    n, rows = sizes.n, sizes.rows
    pairs = (2, rows, 2 * n, 2 * HEAD)
    return dict(
        **attention_scratch(sizes),
        d_mixed=pltpu.VMEM((4 * n, sizes.heads_width), BF16),
        d_kv=pltpu.VMEM(pairs, F32),
        d_kv_out=pltpu.VMEM(pairs, BF16),
        share_out=pltpu.VMEM((2, n, 2 * HEAD), BF16),
        d_query=pltpu.VMEM((4 * n, sizes.heads_width), BF16),
        d_pair=pltpu.VMEM((2 * n, 2 * HEAD), BF16),
        a_grad=pltpu.VMEM((sizes.attn, sizes.width), BF16),
    )


def small_outs(sizes, layer):
    return layered(
        layer,
        d_gain_attn=((1, sizes.width), F32, True),
        d_bias_query=((1, sizes.heads_width), F32, True),
        d_bias_pair=((1, 2 * HEAD), F32, True),
    )


def exchange_halves(parts, section):
    return pick(parts, section), swap(pick(parts, 1 - section), *SECTION)


def of_layer(layer, parts, section, token):
    own, other = parts
    return jnp.where(section + token == layer, own, other)


def to_owner(first, second, section):
    keep = jnp.where(section == 0, first, second)
    away = jnp.where(section == 0, second, first)
    other = swap(away, *SECTION)
    return jnp.where(section == 0, keep, other), jnp.where(section == 0, other, keep)


def local(
    tokens,
    cotangent,
    lengths,
    norm_attn,
    w_query,
    b_query,
    w_keyval,
    b_keyval,
    w_out,
    norm_ffn,
    w_gate,
    w_up,
    w_down,
):
    section = lax.axis_index(SEC)
    row = lax.axis_index(ROW)
    col = lax.axis_index(COL)
    rows = lax.axis_size(ROW)
    cols = lax.axis_size(COL)
    low, high = bit_of(col, 0), bit_of(col, 1)
    place = (section, row, low, high)
    row_count = tokens.shape[1]
    width = tokens.shape[2]
    half = row_count // 2
    depth = w_query.shape[1]
    heads_width = w_query.shape[2]

    def blocks_of(array):
        return jnp.concatenate(
            [
                lax.dynamic_slice(
                    array, (2 * section + (high ^ j), (low ^ k) * half, 0), (1, half, width)
                )
                for j in range(2)
                for k in range(2)
            ]
        )

    small = jnp.concatenate([norm_attn[0], norm_ffn[0], b_keyval[0], b_query[0]])
    small = (small, swap(small, *SECTION))
    small = [of_layer(layer, small, section, 0).astype(F32) for layer in range(2)]

    pair_cols = w_keyval[0].reshape(-1, 2, KV, HEAD)
    mine = pick(pair_cols, high, 2).reshape(-1, 2 * HEAD)
    away = pick(pair_cols, 1 - high, 2).reshape(-1, 2 * HEAD)
    pair_rows = ordered(mine[None, None], swap(away, *COL_HIGH)[None, None], high, 0)
    pair_rows = ordered(pair_rows, swap(pair_rows, *COL_LOW), low, 1)
    pair_rows = pair_rows.reshape(depth, 2 * HEAD)
    attn_own = jnp.concatenate([w_query[0].T, w_out[0], pair_rows.T])
    attn_halves = exchange_halves(attn_own.reshape(2, -1, depth), section)

    def ffn_parts(shard):
        hidden = shard.shape[0]
        parts = shard.reshape(2, 2, hidden // 4, shard.shape[1]).transpose(1, 0, 2, 3)
        return exchange_halves(parts, section)

    parts = [ffn_parts(shard) for shard in (w_gate[0].T, w_up[0].T, w_down[0])]
    ways = [(COL_LOW, COL_HIGH), (COL_HIGH, COL_LOW)]

    hidden = w_gate.shape[2] // 2

    tables = layout(lengths, place, row_count)
    sizes = Sizes(half, width, rows, hidden, 2 * attn_halves[0].shape[0], depth)
    entry = blocks_of(tokens)

    ffn_ways = [way for way, _ in ways]
    across = [way for _, way in ways]
    cosine, sine, start, own_index, key_index = tables
    shared = dict(
        cos=(cosine, True),
        sin=(sine, True),
        start=(start, True),
        own=(own_index, True),
        key=(key_index, True),
    )
    gains_attn, gains_ffn, vectors = [], [], []
    for layer in range(2):
        bias_pair = small[layer][2 * width : 2 * width + 2 * KV * HEAD].reshape(2, KV, HEAD)
        gains_attn.append(layered(layer, gain_attn=(small[layer][None, :width], True)))
        gains_ffn.append(layered(layer, gain_ffn=(small[layer][None, width : 2 * width], True)))
        vectors.append(
            layered(
                layer,
                b_query=(small[layer][None, 2 * width + 2 * KV * HEAD :], True),
                b_pair=(pick(bias_pair, high, 1).reshape(1, -1), True),
            )
        )
    chip_ways = [COL_LOW, COL_HIGH, SECTION] + [(ROW, 1 << bit) for bit in range(row_bits())]

    attn_moves = [AttnGather(of_layer(layer, attn_halves, section, 0)) for layer in range(2)]
    ffn_moves = [
        [FfnGather(of_layer(layer, parts[kind], section, 0), across[layer]) for kind in range(3)]
        for layer in range(2)
    ]
    grad_own = lax.dynamic_slice(
        cotangent, (2 * section + high, low * half, 0), (1, half, width)
    )[0]
    grad_move = TokenGather(grad_own, grad_own.shape, ffn_ways[1], ROW_LOW, True)
    (attn_a, attn_b), ((gate_a, up_a, down_a), (gate_b, up_b, down_b)) = attn_moves, ffn_moves
    some, rest = rows // 2, rows - rows // 2
    schedule = dict(
        a0_begin=[attn_a],
        a0_normed=[attn_a, gate_a, gate_a, attn_a],
        a0_queries=[gate_a] * rows,
        a0_relayed=[up_a, up_a, down_a, down_a],
        a0_head0=[up_a] * some,
        a0_head1=[up_a] * rest,
        f0_sent=[down_a] * some + [attn_b],
        f0_gathered=[gate_a] + [down_a] * rest + [up_a],
        f0_up=[down_a, attn_b],
        f0_edges=[gate_b, gate_b],
        f0_end=[attn_b],
        a1_queries=[gate_b] * rows,
        a1_relayed=[up_b, up_b, down_b, down_b],
        a1_head0=[up_b] * some,
        a1_head1=[up_b] * rest,
        f1_sent=[down_b] * some,
        f1_gathered=[gate_b] + [down_b] * rest + [up_b, grad_move],
        f1_up=[down_b, grad_move],
        f1_edges=[grad_move],
    )

    def forward_kernel(r, at):
        for layer in range(2):
            attention_forward(r, layer, at, attn_moves[layer])
            ffn_forward(r, layer, ffn_ways[layer], at, ffn_moves[layer])

    tokens_here = 4 * half
    outs = dict(entry_hbm1=((4, half, width), BF16, False), result1=((half, width), F32, True))
    buffers = dict(
        entry1=pltpu.VMEM((4, half, width), BF16), result0=pltpu.VMEM((half, width), F32)
    )
    units = ((8 * half, sizes.hidden), BF16, False)
    for layer in range(2):
        outs.update(
            layered(
                layer,
                second=((half, width), F32, True),
                normed=((tokens_here, width), BF16, True),
                query=((tokens_here, heads_width), BF16, True),
                mixed=((tokens_here, heads_width), BF16, True),
                lse=((2, sizes.heads, 2 * half), F32, True),
                kv_hbm=((2, rows, 2 * half, 2 * HEAD), BF16, False),
                f_blocks_hbm=((4, 2, half, width), BF16, False),
                gate=units,
                up=units,
                act=units,
            )
        )
        buffers.update(ffn_buffers(sizes, layer))
        buffers.update(attention_buffers(sizes, layer, False))
    done = kernel_call(
        forward_kernel,
        0,
        chip_ways,
        dict(
            entry0=(entry, True),
            **shared,
            **gains_attn[0],
            **gains_attn[1],
            **gains_ffn[0],
            **gains_ffn[1],
            **vectors[0],
            **vectors[1],
        ),
        outs,
        {**common_scratch(sizes), **ffn_scratch(sizes, 3, 4), **attention_scratch(sizes), **buffers},
        1 << 34,
        [*attn_moves, *ffn_moves[0], *ffn_moves[1], grad_move],
        schedule,
    )
    (grad_all,) = grad_move.results
    last_result = done.result1.astype(BF16)

    def grad_of(left, right):
        return dot(left, right.reshape(-1, width), 0, 0).astype(BF16)

    unit = sizes.unit

    def blocked(grad, arrived):
        total = (grad[:unit].astype(F32) + arrived.astype(F32)).astype(BF16)
        return jnp.stack([total[:, i * depth : (i + 1) * depth] for i in range(rows)])

    def ffn_back_operands(layer):
        of = done.of(layer)
        (gate, gate_far), (up, up_far), (down, down_far) = (move.results for move in ffn_moves[layer])
        return {
            **gains_ffn[layer],
            **layered(
                layer,
                second=(of.second, True),
                gate=(of.gate, False),
                up=(of.up, False),
                gate_own=(gate, False),
                gate_other=(gate_far, False),
                up_own=(up, False),
                up_other=(up_far, False),
                down_own=(down, False),
                down_other=(down_far, False),
            ),
        }

    def ffn_back_outs(layer):
        return layered(
            layer,
            d_second=((half, width), F32, True),
            d_gain_ffn=((1, width), F32, True),
            d_gate=units,
            d_up=units,
        )

    def attention_back_operands(layer, own):
        of = done.of(layer)
        return {
            **gains_attn[layer],
            **shared,
            **layered(
                layer,
                entry=(own, True),
                attn_blocks=(attn_moves[layer].results[0], False),
                kv=(of.kv_hbm, True),
                normed=(of.normed, True),
                query=(of.query, True),
                mixed=(of.mixed, True),
                lse=(of.lse, True),
            ),
        }

    down_grad = grad_of(done.act1, grad_all)
    down_move = Across(down_grad, unit, across[1])
    back = kernel_call(
        lambda r, at: ffn_backward(r, 1, ffn_ways[1], at, False),
        1,
        [ffn_ways[1], ROW_LOW, SECTION],
        dict(d_entry2=(grad_own, True), gathered1=(grad_all, False), **ffn_back_operands(1)),
        ffn_back_outs(1),
        {**common_scratch(sizes), **ffn_scratch(sizes, 2, 2), **ffn_buffers(sizes, 1)},
        1 << 33,
        [down_move],
        dict(f1_sent=[down_move]),
    )
    gate_grad = grad_of(back.d_gate1, done.f_blocks_hbm1)
    up_grad = grad_of(back.d_up1, done.f_blocks_hbm1)
    down_one = blocked(down_grad, down_move.results[0])

    down_rows = Rows(down_one)
    gate_move = GradScatter(gate_grad, unit, across[1])
    up_move = Across(up_grad, unit, across[1])
    last_move = TokenGather(last_result, last_result.shape, COL_LOW, COL_HIGH, False)
    entry_move = TokenGather("d_entry1", (half, width), COL_LOW, COL_HIGH, False)
    attn_move_one = AttnScatter("a_grad", (sizes.attn, width))

    def middle_kernel(r, at):
        attention_backward(r, 1, at)
        ffn_backward(r, 0, ffn_ways[0], at, True)

    middle = kernel_call(
        middle_kernel,
        2,
        chip_ways,
        dict(
            d_second1=(back.d_second1, True),
            **attention_back_operands(1, done.entry_hbm1[0]),
            **ffn_back_operands(0),
        ),
        dict(
            d_entry1=((half, width), BF16, True),
            f_blocks_hbm0=((4, 2, half, width), BF16, False),
            **small_outs(sizes, 1),
            **ffn_back_outs(0),
        ),
        {
            **common_scratch(sizes),
            **attention_back_scratch(sizes),
            **attention_buffers(sizes, 1, True),
            **ffn_scratch(sizes, 2, 3),
            **ffn_buffers(sizes, 0),
        },
        1 << 33,
        [down_rows, gate_move, up_move, last_move, entry_move, attn_move_one],
        dict(
            a1_relayed=[down_rows, gate_move],
            a1_grads=[attn_move_one],
            f0_edges=[gate_move, up_move, attn_move_one, last_move, entry_move],
        ),
    )
    up_one = blocked(up_grad, up_move.results[0])
    zero_grads = [
        grad_of(done.act0, middle.f_blocks_hbm0),
        grad_of(middle.d_gate0, done.f_blocks_hbm0),
        grad_of(middle.d_up0, done.f_blocks_hbm0),
    ]

    up_rows = Rows(up_one)
    zero_moves = [GradScatter(grad, unit, across[0]) for grad in zero_grads]
    attn_move_zero = AttnScatter("a_grad", (sizes.attn, width))
    first_move = TokenGather("d_entry0", (half, width), COL_LOW, COL_HIGH, False)
    sum_rows = 2 * (3 * width // HEAD + 2 * KV)
    sum_ways = 3 + row_bits()

    def last_kernel(r, at):
        attention_backward(r, 0, at)
        sum_vectors(r, at, Links(r.sum_sems))

    down_zero, gate_zero, up_zero = zero_moves
    final = kernel_call(
        last_kernel,
        3,
        chip_ways,
        dict(
            d_second0=(middle.d_second0, True),
            d_gain_ffn0=(middle.d_gain_ffn0, True),
            d_gain_ffn1=(back.d_gain_ffn1, True),
            **attention_back_operands(0, entry[0]),
            **{name: (middle.named[name], True) for name in small_outs(sizes, 1)},
        ),
        dict(d_entry0=((half, width), BF16, True), sums=((sum_rows, HEAD), F32, True)),
        {
            **common_scratch(sizes),
            **attention_back_scratch(sizes),
            **attention_buffers(sizes, 0, True),
            **{name: pltpu.VMEM(shape, F32) for name, (shape, _, _) in small_outs(sizes, 0).items()},
            **dict(
                vector=pltpu.VMEM((sum_rows, HEAD), F32),
                vector_out=pltpu.VMEM((sum_ways, sum_rows, HEAD), F32),
                vector_in=pltpu.VMEM((sum_ways, sum_rows, HEAD), F32),
                sum_sems=semaphores(sum_ways, sum_ways),
            ),
        },
        1 << 32,
        [up_rows, *zero_moves, attn_move_zero, first_move],
        dict(
            a0_relayed=[down_zero],
            a0_hops=[up_rows],
            a0_edges=[gate_zero, up_zero],
            a0_grads=[down_zero, attn_move_zero],
            a0_end=[attn_move_zero, gate_zero, first_move],
            s1_step=[attn_move_zero],
            s2_step=[first_move],
            s3_step=[attn_move_zero],
        ),
    )

    def by_row_bit(own, arrived):
        near, far = own.astype(F32), 0.0
        for flip in range(1, rows):
            if flip & 1:
                far = far + arrived[flip].astype(F32)
            else:
                near = near + arrived[flip].astype(F32)
        return ordered(near.astype(BF16)[None], far.astype(BF16)[None], row & 1, 0)

    ffn_grads = [
        [by_row_bit(*move.results) for move in (gate_zero, up_zero, down_zero)],
        [
            by_row_bit(*gate_move.results),
            by_row_bit(pick(up_one, row), up_rows.results[0]),
            by_row_bit(pick(down_one, row), down_rows.results[0]),
        ],
    ]
    sums = final.sums.reshape(2, -1)
    sums = jnp.where(section == 0, sums[0], sums[1])
    grad_norm_attn = sums[:width]
    grad_norm_ffn = sums[width : 2 * width]
    spread = sums[2 * width : 2 * width + cols * heads_width].reshape(cols, -1)
    grad_b_query = pick(spread, col)
    grad_b_keyval = sums[2 * width + cols * heads_width :]
    first_result, (last_blocks,) = done.entry_hbm1, last_move.results
    (grad_one_blocks,), (grad_zero_blocks,) = entry_move.results, first_move.results
    (attn_one_half,), (attn_zero_half,) = attn_move_one.results, attn_move_zero.results

    def assemble(first, second):
        def placed(blocks):
            blocks = blocks.reshape(2, 2, half, width)
            blocks = jnp.where(high == 0, blocks, blocks[::-1])
            blocks = jnp.where(low == 0, blocks, blocks[:, ::-1])
            return blocks.reshape(2, row_count, width)

        zeroth, later = to_owner(placed(first), placed(second), section)
        return jnp.concatenate([zeroth, later])[None]

    outputs = assemble(first_result, last_blocks)
    grads_in = assemble(grad_zero_blocks, grad_one_blocks)

    def ffn_grad(kind):
        zeroth, later = to_owner(ffn_grads[0][kind], ffn_grads[1][kind], section)
        whole = jnp.stack([zeroth, later], axis=1)
        return whole.reshape(-1, whole.shape[-1])

    grad_gate = ffn_grad(0).T.astype(F32)
    grad_up = ffn_grad(1).T.astype(F32)
    grad_down = ffn_grad(2).astype(F32)

    total = jnp.concatenate(to_owner(attn_zero_half, attn_one_half, section)).astype(F32)
    grad_query = total[:heads_width].T
    grad_out = total[heads_width : 2 * heads_width]
    pair = total[2 * heads_width :].T.reshape(2, 2, depth // 4, 2 * HEAD)
    pair = pick(pair, low, 1) + swap(pick(pair, 1 - low, 1).astype(BF16), *COL_LOW).astype(F32)
    pair = pair.astype(BF16)
    pair = ordered(
        pick(pair, high)[:, None], swap(pick(pair, 1 - high), *COL_HIGH)[:, None], high, 1
    )
    grad_keyval = (
        pair.reshape(-1, 2, 2, HEAD).transpose(0, 2, 1, 3).reshape(-1, 2 * KV * HEAD).astype(F32)
    )

    return (
        outputs,
        grads_in,
        grad_norm_attn[None],
        grad_query[None],
        grad_b_query[None],
        grad_keyval[None],
        grad_b_keyval[None],
        grad_out[None],
        grad_norm_ffn[None],
        grad_gate[None],
        grad_up[None],
        grad_down[None],
    )


def solution(mesh):
    in_specs = (
        P(None, ROW, None),
        P(None, ROW, None),
        P(),
        P(SEC, None),
        P(SEC, ROW, COL),
        P(SEC, COL),
        P(SEC, (ROW, COL), None),
        P(SEC, None),
        P(SEC, COL, ROW),
        P(SEC, None),
        P(SEC, ROW, COL),
        P(SEC, ROW, COL),
        P(SEC, COL, ROW),
    )
    out_specs = (
        P(SEC, None, ROW, None),
        P(SEC, None, ROW, None),
        P(SEC, None),
        P(SEC, ROW, COL),
        P(SEC, COL),
        P(SEC, (ROW, COL), None),
        P(SEC, None),
        P(SEC, COL, ROW),
        P(SEC, None),
        P(SEC, ROW, COL),
        P(SEC, ROW, COL),
        P(SEC, COL, ROW),
    )
    return jax.shard_map(local, mesh=mesh, in_specs=in_specs, out_specs=out_specs, check_vma=False)
```

time: 2860 us -> 1030 us (0.36)
  waiting for transfers between devices: 1730 us -> 3.34 us
  Pallas kernels: 0 us -> 853 us
  matrix products: 506 us -> 42.2 us
  blocking collectives: 167 us -> 0 us
  local copies, waits for them, and re-layouts: 196 us -> 37 us
  other arithmetic: 201 us -> 59.1 us
    pallas_call x0 -> x4, Pallas kernels: none -> 853 us  [kernel_call(): pl.pallas_call(body, out_shape=[jax.ShapeDtypeStruct(shape, dtype) for sh...]
    psum x19 -> x0, waiting for transfers between devices: 845 us -> none  [the longest x11 480 us: column_sum(): return lax.psum(partial_sum.astype(jnp.bfloat16), 'col').astype(jnp.float32)]
    all_gather x6 -> x0, waiting for transfers between devices: 449 us -> none  [the longest x1 125 us: local(): lax.all_gather(w_up[0], 'row', axis=0, tiled=True)]
    dot_general x140 -> x6, matrix products: 461 us -> 42.2 us  [dot(): lax.dot_general(left, right, (((left_dim,), (right_dim,)), ((), ())), pre...]
    unnamed x40 -> x0, waiting for transfers between devices: 266 us -> none
    reduce_scatter x7 -> x0, waiting for transfers between devices: 153 us -> none  [the longest x1 124 us: local(): lax.psum_scatter(acc_keyval, ('row', 'col'), scatter_dimension=0, tiled=T...]
    all_gather x10 -> x0, blocking collectives: 142 us -> none  [forward_layer(): gathered = lax.all_gather(local_pair, 'row', axis=0, tiled=True)]
    unnamed x803 -> x111, local copies, waits for them, and re-layouts: 120 us -> 9.45 us
  transfers between devices with their start and end apart: 49 -> 15, of which waited for: 39 -> 2; matrix products, arithmetic and copies ran while one was open for 17% -> 7% of each run, Pallas kernels for 0% -> 0%
where the time goes in v2:
time: 1030 us; the launch traced here: 1020 us
  Pallas kernels  853 us (83%)
  other arithmetic  59.1 us (6%)
  matrix products  42.2 us (4%)
  local copies, waits for them, and re-layouts  37 us (4%)
  starting transfers between devices  17.6 us (2%)
    pallas_call x4, Pallas kernels, kernel_call(): pl.pallas_call(body, out_shape=[jax.ShapeDtypeStruct(shape, dtype) for sh...  853 us
    dot_general x6, matrix products, dot(): lax.dot_general(left, right, (((left_dim,), (right_dim,)), ((), ())), pre...  42.2 us
  transfers between devices with their start and end apart: 15, of which 2 were waited for; matrix products, arithmetic and copies ran while one was open for 7% of the time, Pallas kernels for 0%

profile of v2, /device:TPU:9, one launch (start us, length us, event | category | flops | bytes accessed | tf_op | source)
XLA Modules:
  0.0 1017.9 jit_solution(566860169625706894)
XLA Ops:
  7.6 2.3 dynamic-slice_bitcast_fusion
  26.3 2.1 collective-permute-done.2
  35.3 2.7 bitcast_select_fusion.4
  38.0 2.6 bitcast_select_fusion.6
  40.6 2.5 bitcast_select_fusion.8
  43.2 405.4 %shard_map.220 = (bf16[4,128,1536]{2,1,0:T(8,128)(2,1)}, f32[128,1536]{1,0:T(8,128)}, f32[128,1536]{1,0:T(8,128)}, bf16[512,1536]{1,0:T(8,128)(2,1)}, bf16[512,3...) custom-call(bf16[4,128,1536]{2,1,0:T(8,128)(2,1)} %pad_maximum_fusio, ...), custom_call_target="tpu_custom_call" | custom-call | flops 17179869184 | bytes 33554432 | tf_op jit(solution)/shard_map/pallas_call | solution.py:207
  448.6 8.8 convolution_convert_fusion.5.refs_12_
  457.4 44.5 %shard_map.221 = (f32[128,1536]{1,0:T(8,128)}, f32[1,1536]{1,0:T(1,128)}, bf16[1024,1152]{1,0:T(8,128)(2,1)}, bf16[1024,1152]{1,0:T(8,128)(2,1)}, bf16[560,1536]{1,0:T(8,128)(2,1)}) custom-call(bf16[128,1536]{1,0:T(8,128)(2,1)} %dynamic-slice_bitcast_fusion.3.refs_22_.refs_0_, bf16[4,2,128,1536]{3,2,1,0:T(8,128)(2,1)} %get-tuple-element.80.refs_1_, ...), custom_call_target="tpu_custom_call" | custom-call | flops 8589934592 | bytes 33554432 | tf_op jit(solution)/shard_map/pallas_call | solution.py:207
  501.9 8.4 convolution_convert_fusion.3.refs_26_
  510.3 5.5 convolution_convert_fusion.4.refs_25_
  522.8 189.9 %shard_map.222 = (bf16[128,1536]{1,0:T(8,128)(2,1)}, bf16[4,2,128,1536]{3,2,1,0:T(8,128)(2,1)}, f32[1,1536]{1,0:T(1,128)}, f32[1,384]{1,0:T(1,128)}, f32[1,256]{...) custom-call(f32[128,1536]{1,0:T(8,128)} %get-tuple-element.91.refs_0, ...), custom_call_target="tpu_custom_call" | custom-call | flops 8589934592 | bytes 33554432 | tf_op jit(solution)/shard_map/pallas_call | solution.py:207
  712.7 8.4 convolution_convert_fusion.refs_22_
  721.1 5.5 convolution_convert_fusion.1.refs_21_
  726.7 2.0 add_convert_fusion
  730.6 5.6 convolution_convert_fusion.2.refs_20_
  737.8 213.1 %shard_map.223 = (bf16[128,1536]{1,0:T(8,128)(2,1)}, f32[80,128]{1,0:T(8,128)}, bf16[4,560,384]{2,1,0:T(8,128)(2,1)}, bf16[560,384]{1,0:T(8,128)(2,1)}, bf16[4,5...) custom-call(f32[128,1536]{1,0:T(8,128)} %get-tuple-element.113.refs_, ...), custom_call_target="tpu_custom_call" | custom-call | flops 4294967296 | bytes 33554432 | tf_op jit(solution)/shard_map/pallas_call | solution.py:207
  956.7 3.8 collective-permute-start.14
  973.0 2.3 reverse_select_fusion.5
  976.2 2.5 broadcast_select_fusion.3
  990.6 2.1 collective-permute-start.11
  993.6 2.1 copy.95
  1002.7 2.0 copy.94
  1004.7 2.0 copy.93
  1008.4 2.0 copy.92
  (238 shorter events, 84.2 us)
Async XLA Ops:
  0.6 9.3 copy-start.22
  2.4 22.0 %collective-permute-start.1 = (bf16[96,256]{1,0:T(8,128)(2,1)S(1)}, bf16[96,256]{1,0:T(8,128)(2,1)S(1)}, u32[]{:S(2)}, u32[]{:S(2)}) collective-permute-start(bf16[96,256]{1,0:T(8,128)(2,1)S(1)} %bitcast.289), channel_id=1, source_target_pairs={{0,2},{1,3},{2,0},{3,1},{4,6},{5,7},{6,4},{7,5},{8,10},{9,11},{10,... | collective-permute-start | bytes 147464 | tf_op jit(solution)/shard_map/ppermute | solution.py:31
  6.6 23.6 %collective-permute-start = (bf16[3968]{0:T(1024)(128)(2,1)S(1)}, bf16[3968]{0:T(1024)(128)(2,1)S(1)}, u32[]{:S(2)}, u32[]{:S(2)}) collective-permute-start(bf16[3968]{0:T(1024)(128)(2,1)S(1)} %pad_maximum_fusion.14), channel_id=1, source_target_pairs={{0,16},{16,0},{1,17},{17,1},{2,18},{18,2},{3,19},{19,3},{4,20},{20... | collective-permute-start | bytes 23816 | tf_op jit(solution)/shard_map/ppermute | solution.py:31
  9.9 25.5 %collective-permute-start.6 = (bf16[2,560,384]{2,1,0:T(8,128)(2,1)}, bf16[2,560,384]{2,1,0:T(8,128)(2,1)}, u32[]{:S(2)}, u32[]{:S(2)}) collective-permute-start(bf16[2,560,384]{2,1,0:T(8,128)(2,1)} %dynamic-slice_bitcast_fusion), channel_id=1, source_target_pairs={{0,16},{16,0},{1,17},{17,1},{2,18},{18,2},{3,19},{19,3},{4,20},{20... | collective-permute-start | bytes 2580488 | tf_op jit(solution)/shard_map/ppermute | solution.py:31
  10.0 28.0 %collective-permute-start.5 = (bf16[2,560,384]{2,1,0:T(8,128)(2,1)S(1)}, bf16[2,560,384]{2,1,0:T(8,128)(2,1)}, u32[]{:S(2)}, u32[]{:S(2)}) collective-permute-start(bf16[2,560,384]{2,1,0:T(8,128)(2,1)S(1)} %dynamic-slice_bitcast_fusion.1), channel_id=1, source_target_pairs={{0,16},{16,0},{1,17},{17,1},{2,18},{18,2},{3,19},{19,3},{4,20},{20... | collective-permute-start | bytes 2580488 | tf_op jit(solution)/shard_map/ppermute | solution.py:31
  10.6 30.0 %collective-permute-start.4 = (bf16[2,560,384]{2,1,0:T(8,128)(2,1)S(1)}, bf16[2,560,384]{2,1,0:T(8,128)(2,1)}, u32[]{:S(2)}, u32[]{:S(2)}) collective-permute-start(bf16[2,560,384]{2,1,0:T(8,128)(2,1)S(1)} %dynamic-slice_bitcast_fusion.2), channel_id=1, source_target_pairs={{0,16},{16,0},{1,17},{17,1},{2,18},{18,2},{3,19},{19,3},{4,20},{20... | collective-permute-start | bytes 2580488 | tf_op jit(solution)/shard_map/ppermute | solution.py:31
  22.3 6.3 copy-start.42
  24.4 4.0 collective-permute-start.2
  28.6 6.7 copy-start.21
  28.8 5.6 collective-permute-start.3
  501.9 8.4 copy-start.48
  501.9 8.4 copy-start.49
  712.7 8.4 copy-start.46
  712.7 8.4 copy-start.47
  955.6 6.2 copy-start.1
  955.6 6.2 copy-start.2
  956.7 41.2 %collective-permute-start.14 = (bf16[2,560,384]{2,1,0:T(8,128)(2,1)}, bf16[2,560,384]{2,1,0:T(8,128)(2,1)}, u32[]{:S(2)}, u32[]{:S(2)}) collective-permute-start(bf16[2,560,384]{2,1,0:T(8,128)(2,1)} %broadcast_select_fusion.4), channel_id=1, source_target_pairs={{0,16},{16,0},{1,17},{17,1},{2,18},{18,2},{3,19},{19,3},{4,20},{20... | collective-permute-start | bytes 2580488 | tf_op jit(solution)/shard_map/ppermute | solution.py:31
  963.3 36.8 %collective-permute-start.13 = (bf16[2,560,384]{2,1,0:T(8,128)(2,1)}, bf16[2,560,384]{2,1,0:T(8,128)(2,1)}, u32[]{:S(2)}, u32[]{:S(2)}) collective-permute-start(bf16[2,560,384]{2,1,0:T(8,128)(2,1)} %broadcast_select_fusion.6), channel_id=1, source_target_pairs={{0,16},{16,0},{1,17},{17,1},{2,18},{18,2},{3,19},{19,3},{4,20},{20... | collective-permute-start | bytes 2580488 | tf_op jit(solution)/shard_map/ppermute | solution.py:31
  966.5 40.1 %collective-permute-start.12 = (bf16[2,560,384]{2,1,0:T(8,128)(2,1)}, bf16[2,560,384]{2,1,0:T(8,128)(2,1)}, u32[]{:S(2)}, u32[]{:S(2)}) collective-permute-start(bf16[2,560,384]{2,1,0:T(8,128)(2,1)} %broadcast_select_fusion.8), channel_id=1, source_target_pairs={{0,16},{16,0},{1,17},{17,1},{2,18},{18,2},{3,19},{19,3},{4,20},{20... | collective-permute-start | bytes 2580488 | tf_op jit(solution)/shard_map/ppermute | solution.py:31
  967.5 11.2 %collective-permute-start.9 = (bf16[512,384]{1,0:T(8,128)(2,1)S(1)}, bf16[512,384]{1,0:T(8,128)(2,1)}, u32[]{:S(2)}, u32[]{:S(2)}) collective-permute-start(bf16[512,384]{1,0:T(8,128)(2,1)S(1)} %broadcast_select_fusion.16), channel_id=1, source_target_pairs={{0,16},{16,0},{1,17},{17,1},{2,18},{18,2},{3,19},{19,3},{4,20},{20... | collective-permute-start | bytes 1179656 | tf_op jit(solution)/shard_map/ppermute | solution.py:31
  971.2 39.2 %collective-permute-start.8 = (bf16[2,256,1536]{2,1,0:T(8,128)(2,1)}, bf16[2,256,1536]{2,1,0:T(8,128)(2,1)}, u32[]{:S(2)}, u32[]{:S(2)}) collective-permute-start(bf16[2,256,1536]{2,1,0:T(8,128)(2,1)} %bitcast.56), channel_id=1, source_target_pairs={{0,16},{16,0},{1,17},{17,1},{2,18},{18,2},{3,19},{19,3},{4,20},{20... | collective-permute-start | bytes 4718600 | tf_op jit(solution)/shard_map/ppermute | solution.py:31
  984.6 5.0 collective-permute-start.10
  990.6 5.0 collective-permute-start.11
  995.7 18.3 %collective-permute-start.7 = (bf16[2,256,1536]{2,1,0:T(8,128)(2,1)}, bf16[2,256,1536]{2,1,0:T(8,128)(2,1)}, u32[]{:S(2)}, u32[]{:S(2)}) collective-permute-start(bf16[2,256,1536]{2,1,0:T(8,128)(2,1)} %bitcast.281), channel_id=1, source_target_pairs={{0,16},{16,0},{1,17},{17,1},{2,18},{18,2},{3,19},{19,3},{4,20},{20... | collective-permute-start | bytes 4718600 | tf_op jit(solution)/shard_map/ppermute | solution.py:31
  (42 other events, 111.8 us)

commit v3 on v2

--- a/solution.py
+++ b/solution.py
@@ -355,6 +355,40 @@
                 arrive(slot)
             local.wait()
             wait_all(sides, [copy for _, _, copy in hops] + sides)
+
+        self.steps = [start, forward, finish]
+
+
+class ColumnGather(Move):
+    def __init__(self, own, shape):
+        super().__init__(own, [(4, *shape)], semaphores(8, 8, 1), [COL_LOW, COL_HIGH])
+
+    def bind(self, sources, targets, scratch):
+        (own,), (blocks,) = sources, targets
+        send, recv, local_sem = scratch
+        col = lax.axis_index(COL)
+        h = own.shape[0] // 2
+        links = Links((send, recv))
+        place = blocks.at[col]
+        local = pltpu.make_async_copy(own, place, local_sem.at[0])
+        first = [links.copy(own, place, COL_LOW), links.copy(own, place, COL_HIGH)]
+        top = blocks.at[col ^ COL_LOW[1], pl.ds(0, h)]
+        bottom = blocks.at[col ^ COL_HIGH[1], pl.ds(h, h)]
+        second = [links.copy(top, top, COL_HIGH), links.copy(bottom, bottom, COL_LOW)]
+
+        def start():
+            local.start()
+            for copy in first:
+                copy.start()
+
+        def forward():
+            for arrived, copy in zip(first, second, strict=True):
+                arrived.wait_recv()
+                copy.start()
+
+        def finish():
+            local.wait()
+            wait_all(second, first + second)
 
         self.steps = [start, forward, finish]
 
@@ -766,14 +800,8 @@
         copy.wait()
 
 
-def ffn_backward(r, layer, a, at, gathers):
+def ffn_backward_loads(r, layer, gathers):
     r = r.of(layer)
-    links = Links(r.f_sems)
-    blocks, second_ref, grad_ref = r.f_blocks, r.second, r.of(layer + 1).d_entry
-    gate_in, up_in = r.hidden
-    d_gate_out, d_up_out = r.hidden
-    n, width = blocks.shape[2:]
-    hidden = r.w_gate.shape[0]
     stage = stage_in(r)
     loads = [
         Load(halves, weight, stage, sems)
@@ -786,11 +814,22 @@
     ]
     for load in loads:
         load.start()
-    more = [(r.gate, gate_in), (r.up, up_in)]
+    more = [(r.gate, r.hidden[0]), (r.up, r.hidden[1])]
     if not gathers:
-        more.append((r.gathered, blocks))
+        more.append((r.gathered, r.f_blocks))
     extra = []
     save(extra, r.f_extra_sem, more)
+    return loads + extra
+
+
+def ffn_backward(r, layer, a, at, gathers, loads):
+    r = r.of(layer)
+    links = Links(r.f_sems)
+    blocks, second_ref, grad_ref = r.f_blocks, r.second, r.of(layer + 1).d_entry
+    gate_in, up_in = r.hidden
+    d_gate_out, d_up_out = r.hidden
+    n, width = blocks.shape[2:]
+    hidden = r.w_gate.shape[0]
     if gathers:
         blocks[0, 0] = grad_ref[...]
     gather = BlockGather(links, blocks, a, ROW_LOW, there=not gathers)
@@ -827,8 +866,6 @@
     at(layer).f_sent()
     for load in loads:
         load.wait()
-    for copy in extra:
-        copy.wait()
     gather.sides[0].wait_recv()
     step(0)
     gather.a.wait_recv()
@@ -1020,7 +1057,7 @@
     scatter.send_edge_b(partial[2])
     scatter.send_edge_a(partial[1])
     if layer:
-        save(saves, r.a_save_sem, [(entry, r.entry_hbm)])
+        save(saves, r.a_save_sem, [(entry.at[0], r.entry_hbm)])
     at(layer).a_edges()
     r.second[...] = entry[0].astype(F32) + scatter.total(partial[0])
     at(layer).a_end()
@@ -1157,15 +1194,15 @@
     r.d_bias_query[...] = jnp.sum(d_query[...].astype(F32), axis=0, keepdims=True)
     r.d_bias_pair[...] = jnp.sum(d_pair[...].astype(F32), axis=0, keepdims=True)
     a_grad, normed = r.a_grad, r.normed
-    own_blocks = blocks[...].reshape(4 * n, width)
+    turned_query, turned_mixed, turned_pair = d_query[...].T, r.mixed[...].T, d_pair[...].T
     for lane, size in width_tiles(width):
         lanes = pl.ds(lane, size)
-        a_grad[:heads_width, lanes] = dot(d_query[...], normed[:, lanes], 0, 0).astype(BF16)
+        a_grad[:heads_width, lanes] = dot(turned_query, normed[:, lanes], 1, 0).astype(BF16)
         a_grad[heads_width : 2 * heads_width, lanes] = dot(
-            r.mixed[...], own_blocks[:, lane : lane + size], 0, 0
+            turned_mixed, blocks[:, :, lanes].reshape(4 * n, size), 1, 0
         ).astype(BF16)
         normed_own = jnp.concatenate([normed[:n, lanes], normed[tokens : tokens + n, lanes]])
-        a_grad[2 * heads_width :, lanes] = dot(d_pair[...], normed_own, 0, 0).astype(BF16)
+        a_grad[2 * heads_width :, lanes] = dot(turned_pair, normed_own, 1, 0).astype(BF16)
     at(layer).a_grads()
     d_normed = scatter.total(partial[0])
     stream = r.entry[...].astype(F32)
@@ -1451,7 +1488,7 @@
             ffn_forward(r, layer, ffn_ways[layer], at, ffn_moves[layer])
 
     tokens_here = 4 * half
-    outs = dict(entry_hbm1=((4, half, width), BF16, False), result1=((half, width), F32, True))
+    outs = dict(entry_hbm1=((half, width), BF16, False), result1=((half, width), F32, True))
     buffers = dict(
         entry1=pltpu.VMEM((4, half, width), BF16), result0=pltpu.VMEM((half, width), F32)
     )
@@ -1554,7 +1591,7 @@
     down_grad = grad_of(done.act1, grad_all)
     down_move = Across(down_grad, unit, across[1])
     back = kernel_call(
-        lambda r, at: ffn_backward(r, 1, ffn_ways[1], at, False),
+        lambda r, at: ffn_backward(r, 1, ffn_ways[1], at, False, ffn_backward_loads(r, 1, False)),
         1,
         [ffn_ways[1], ROW_LOW, SECTION],
         dict(d_entry2=(grad_own, True), gathered1=(grad_all, False), **ffn_back_operands(1)),
@@ -1571,13 +1608,14 @@
     down_rows = Rows(down_one)
     gate_move = GradScatter(gate_grad, unit, across[1])
     up_move = Across(up_grad, unit, across[1])
-    last_move = TokenGather(last_result, last_result.shape, COL_LOW, COL_HIGH, False)
-    entry_move = TokenGather("d_entry1", (half, width), COL_LOW, COL_HIGH, False)
+    last_move = ColumnGather(last_result, last_result.shape)
+    entry_move = ColumnGather("d_entry1", (half, width))
     attn_move_one = AttnScatter("a_grad", (sizes.attn, width))
 
     def middle_kernel(r, at):
+        loads = ffn_backward_loads(r, 0, True)
         attention_backward(r, 1, at)
-        ffn_backward(r, 0, ffn_ways[0], at, True)
+        ffn_backward(r, 0, ffn_ways[0], at, True, loads)
 
     middle = kernel_call(
         middle_kernel,
@@ -1585,7 +1623,7 @@
         chip_ways,
         dict(
             d_second1=(back.d_second1, True),
-            **attention_back_operands(1, done.entry_hbm1[0]),
+            **attention_back_operands(1, done.entry_hbm1),
             **ffn_back_operands(0),
         ),
         dict(
@@ -1619,7 +1657,8 @@
     up_rows = Rows(up_one)
     zero_moves = [GradScatter(grad, unit, across[0]) for grad in zero_grads]
     attn_move_zero = AttnScatter("a_grad", (sizes.attn, width))
-    first_move = TokenGather("d_entry0", (half, width), COL_LOW, COL_HIGH, False)
+    first_move = ColumnGather("d_entry0", (half, width))
+    result_move = ColumnGather(done.entry_hbm1, (half, width))
     sum_rows = 2 * (3 * width // HEAD + 2 * KV)
     sum_ways = 3 + row_bits()
 
@@ -1653,12 +1692,12 @@
             ),
         },
         1 << 32,
-        [up_rows, *zero_moves, attn_move_zero, first_move],
+        [up_rows, *zero_moves, attn_move_zero, first_move, result_move],
         dict(
             a0_relayed=[down_zero],
-            a0_hops=[up_rows],
+            a0_hops=[up_rows, result_move],
             a0_edges=[gate_zero, up_zero],
-            a0_grads=[down_zero, attn_move_zero],
+            a0_grads=[down_zero, attn_move_zero, result_move],
             a0_end=[attn_move_zero, gate_zero, first_move],
             s1_step=[attn_move_zero],
             s2_step=[first_move],
@@ -1690,18 +1729,13 @@
     spread = sums[2 * width : 2 * width + cols * heads_width].reshape(cols, -1)
     grad_b_query = pick(spread, col)
     grad_b_keyval = sums[2 * width + cols * heads_width :]
-    first_result, (last_blocks,) = done.entry_hbm1, last_move.results
+    (first_result,), (last_blocks,) = result_move.results, last_move.results
     (grad_one_blocks,), (grad_zero_blocks,) = entry_move.results, first_move.results
     (attn_one_half,), (attn_zero_half,) = attn_move_one.results, attn_move_zero.results
 
     def assemble(first, second):
-        def placed(blocks):
-            blocks = blocks.reshape(2, 2, half, width)
-            blocks = jnp.where(high == 0, blocks, blocks[::-1])
-            blocks = jnp.where(low == 0, blocks, blocks[:, ::-1])
-            return blocks.reshape(2, row_count, width)
-
-        zeroth, later = to_owner(placed(first), placed(second), section)
+        shape = (2, row_count, width)
+        zeroth, later = to_owner(first.reshape(shape), second.reshape(shape), section)
         return jnp.concatenate([zeroth, later])[None]
 
     outputs = assemble(first_result, last_blocks)

time: 1030 us -> 1010 us (0.981)
  transfers between devices with their start and end apart: 15 -> 15, of which waited for: 2 -> 2; matrix products, arithmetic and copies ran while one was open for 7% -> 6% of each run, Pallas kernels for 0% -> 0%
where the time goes in v3:
time: 1010 us; the launch traced here: 1000 us
  Pallas kernels  852 us (84%)
  other arithmetic  55.9 us (6%)
  local copies, waits for them, and re-layouts  38.9 us (4%)
  matrix products  36 us (4%)
  starting transfers between devices  11.5 us (1%)
    pallas_call x4, Pallas kernels, kernel_call(): pl.pallas_call(body, out_shape=[jax.ShapeDtypeStruct(shape, dtype) for sh...  852 us
    dot_general x6, matrix products, dot(): lax.dot_general(left, right, (((left_dim,), (right_dim,)), ((), ())), pre...  36 us
  transfers between devices with their start and end apart: 15, of which 2 were waited for; matrix products, arithmetic and copies ran while one was open for 6% of the time, Pallas kernels for 0%

profile of v3, /device:TPU:9, one launch (start us, length us, event | category | flops | bytes accessed | tf_op | source)
XLA Modules:
  0.0 1004.8 jit_solution(3071004672080280871)
XLA Ops:
  7.3 2.3 dynamic-slice_bitcast_fusion
  26.3 2.4 collective-permute-done.2
  35.3 2.7 bitcast_select_fusion.4
  38.0 2.6 bitcast_select_fusion.6
  40.7 2.5 bitcast_select_fusion.8
  43.2 405.4 %shard_map.220 = (bf16[128,1536]{1,0:T(8,128)(2,1)}, f32[128,1536]{1,0:T(8,128)}, f32[128,1536]{1,0:T(8,128)}, bf16[512,1536]{1,0:T(8,128)(2,1)}, bf16[512,384]{...) custom-call(bf16[4,128,1536]{2,1,0:T(8,128)(2,1)} %pad_maximum_fusio, ...), custom_call_target="tpu_custom_call" | custom-call | flops 17179869184 | bytes 33554432 | tf_op jit(solution)/shard_map/pallas_call | solution.py:207
  450.5 8.7 convolution_convert_fusion.5.refs_12_
  459.2 44.5 %shard_map.221 = (f32[128,1536]{1,0:T(8,128)}, f32[1,1536]{1,0:T(1,128)}, bf16[1024,1152]{1,0:T(8,128)(2,1)}, bf16[1024,1152]{1,0:T(8,128)(2,1)}, bf16[560,1536]{1,0:T(8,128)(2,1)}) custom-call(bf16[128,1536]{1,0:T(8,128)(2,1)} %dynamic-slice_bitcast_fusion.4.refs_22_.refs_0_, bf16[4,2,128,1536]{3,2,1,0:T(8,128)(2,1)} %get-tuple-element.80.refs_1_, ...), custom_call_target="tpu_custom_call" | custom-call | flops 8589934592 | bytes 33554432 | tf_op jit(solution)/shard_map/pallas_call | solution.py:207
  503.7 2.6 add_convert_fusion.1
  508.2 5.4 convolution_convert_fusion.3.refs_26_
  513.6 5.4 convolution_convert_fusion.4.refs_25_
  520.5 188.1 %shard_map.222 = (bf16[128,1536]{1,0:T(8,128)(2,1)}, bf16[4,2,128,1536]{3,2,1,0:T(8,128)(2,1)}, f32[1,1536]{1,0:T(1,128)}, f32[1,384]{1,0:T(1,128)}, f32[1,256]{...) custom-call(f32[128,1536]{1,0:T(8,128)} %get-tuple-element.91.refs_0, ...), custom_call_target="tpu_custom_call" | custom-call | flops 8589934592 | bytes 33554432 | tf_op jit(solution)/shard_map/pallas_call | solution.py:207
  708.6 2.6 add_convert_fusion
  712.9 5.4 convolution_convert_fusion.1.refs_21_
  718.4 5.4 convolution_convert_fusion.refs_22_
  723.8 5.6 convolution_convert_fusion.2.refs_20_
  730.9 213.7 %shard_map.223 = (bf16[128,1536]{1,0:T(8,128)(2,1)}, f32[80,128]{1,0:T(8,128)}, bf16[4,560,384]{2,1,0:T(8,128)(2,1)}, bf16[560,384]{1,0:T(8,128)(2,1)}, bf16[4,5...) custom-call(f32[128,1536]{1,0:T(8,128)} %get-tuple-element.113.refs_, ...), custom_call_target="tpu_custom_call" | custom-call | flops 4294967296 | bytes 33554432 | tf_op jit(solution)/shard_map/pallas_call | solution.py:207
  950.1 4.1 collective-permute-start.9
  975.0 2.5 collective-permute-done.10
  979.3 2.1 copy.95
  989.6 2.0 copy.92
  991.5 2.0 copy.93
  995.2 2.0 copy.94
  998.8 1.9 maximum_bitcast_fusion.1
  (235 shorter events, 77.2 us)
Async XLA Ops:
  0.6 9.2 copy-start.19
  3.6 26.5 %collective-permute-start = (bf16[3968]{0:T(1024)(128)(2,1)S(1)}, bf16[3968]{0:T(1024)(128)(2,1)S(1)}, u32[]{:S(2)}, u32[]{:S(2)}) collective-permute-start(bf16[3968]{0:T(1024)(128)(2,1)S(1)} %pad_maximum_fusion.14), channel_id=1, source_target_pairs={{0,16},{16,0},{1,17},{17,1},{2,18},{18,2},{3,19},{19,3},{4,20},{20... | collective-permute-start | bytes 23816 | tf_op jit(solution)/shard_map/ppermute | solution.py:31
  6.0 18.4 %collective-permute-start.1 = (bf16[96,256]{1,0:T(8,128)(2,1)S(1)}, bf16[96,256]{1,0:T(8,128)(2,1)S(1)}, u32[]{:S(2)}, u32[]{:S(2)}) collective-permute-start(bf16[96,256]{1,0:T(8,128)(2,1)S(1)} %bitcast.283), channel_id=1, source_target_pairs={{0,2},{1,3},{2,0},{3,1},{4,6},{5,7},{6,4},{7,5},{8,10},{9,11},{10,... | collective-permute-start | bytes 147464 | tf_op jit(solution)/shard_map/ppermute | solution.py:31
  9.6 25.7 %collective-permute-start.6 = (bf16[2,560,384]{2,1,0:T(8,128)(2,1)}, bf16[2,560,384]{2,1,0:T(8,128)(2,1)}, u32[]{:S(2)}, u32[]{:S(2)}) collective-permute-start(bf16[2,560,384]{2,1,0:T(8,128)(2,1)} %dynamic-slice_bitcast_fusion), channel_id=1, source_target_pairs={{0,16},{16,0},{1,17},{17,1},{2,18},{18,2},{3,19},{19,3},{4,20},{20... | collective-permute-start | bytes 2580488 | tf_op jit(solution)/shard_map/ppermute | solution.py:31
  10.0 28.0 %collective-permute-start.5 = (bf16[2,560,384]{2,1,0:T(8,128)(2,1)S(1)}, bf16[2,560,384]{2,1,0:T(8,128)(2,1)}, u32[]{:S(2)}, u32[]{:S(2)}) collective-permute-start(bf16[2,560,384]{2,1,0:T(8,128)(2,1)S(1)} %dynamic-slice_bitcast_fusion.1), channel_id=1, source_target_pairs={{0,16},{16,0},{1,17},{17,1},{2,18},{18,2},{3,19},{19,3},{4,20},{20... | collective-permute-start | bytes 2580488 | tf_op jit(solution)/shard_map/ppermute | solution.py:31
  10.3 30.3 %collective-permute-start.4 = (bf16[2,560,384]{2,1,0:T(8,128)(2,1)S(1)}, bf16[2,560,384]{2,1,0:T(8,128)(2,1)}, u32[]{:S(2)}, u32[]{:S(2)}) collective-permute-start(bf16[2,560,384]{2,1,0:T(8,128)(2,1)S(1)} %dynamic-slice_bitcast_fusion.2), channel_id=1, source_target_pairs={{0,16},{16,0},{1,17},{17,1},{2,18},{18,2},{3,19},{19,3},{4,20},{20... | collective-permute-start | bytes 2580488 | tf_op jit(solution)/shard_map/ppermute | solution.py:31
  22.2 6.6 copy-start.41
  24.4 4.3 collective-permute-start.2
  28.9 6.4 copy-start.18
  29.1 5.3 collective-permute-start.3
  718.4 5.4 copy-start.44
  718.4 5.4 copy-start.51
  730.9 215.2 %copy-start.31 = (bf16[4,560,384]{2,1,0:T(8,128)(2,1)S(1)}, bf16[4,560,384]{2,1,0:T(8,128)(2,1)}, u32[]{:S(2)}) copy-start(bf16[4,560,384]{2,1,0:T(8,128)(2,1)} %get-tuple-element.147) | copy-start | bytes 5160964
  947.4 6.8 copy-start.39
  948.8 9.4 copy-start.1
  948.8 9.4 copy-start.3
  950.1 17.9 %collective-permute-start.9 = (bf16[512,384]{1,0:T(8,128)(2,1)S(1)}, bf16[512,384]{1,0:T(8,128)(2,1)S(1)}, u32[]{:S(2)}, u32[]{:S(2)}) collective-permute-start(bf16[512,384]{1,0:T(8,128)(2,1)S(1)} %broadcast_select_fusion.16), channel_id=1, source_target_pairs={{0,16},{16,0},{1,17},{17,1},{2,18},{18,2},{3,19},{19,3},{4,20},{20... | collective-permute-start | bytes 1179656 | tf_op jit(solution)/shard_map/ppermute | solution.py:31
  956.9 36.7 %collective-permute-start.14 = (bf16[2,560,384]{2,1,0:T(8,128)(2,1)}, bf16[2,560,384]{2,1,0:T(8,128)(2,1)}, u32[]{:S(2)}, u32[]{:S(2)}) collective-permute-start(bf16[2,560,384]{2,1,0:T(8,128)(2,1)} %broadcast_select_fusion.4), channel_id=1, source_target_pairs={{0,16},{16,0},{1,17},{17,1},{2,18},{18,2},{3,19},{19,3},{4,20},{20... | collective-permute-start | bytes 2580488 | tf_op jit(solution)/shard_map/ppermute | solution.py:31
  959.3 27.4 %collective-permute-start.13 = (bf16[2,560,384]{2,1,0:T(8,128)(2,1)}, bf16[2,560,384]{2,1,0:T(8,128)(2,1)}, u32[]{:S(2)}, u32[]{:S(2)}) collective-permute-start(bf16[2,560,384]{2,1,0:T(8,128)(2,1)} %broadcast_select_fusion.6), channel_id=1, source_target_pairs={{0,16},{16,0},{1,17},{17,1},{2,18},{18,2},{3,19},{19,3},{4,20},{20... | collective-permute-start | bytes 2580488 | tf_op jit(solution)/shard_map/ppermute | solution.py:31
  962.5 22.1 %collective-permute-start.12 = (bf16[2,560,384]{2,1,0:T(8,128)(2,1)}, bf16[2,560,384]{2,1,0:T(8,128)(2,1)}, u32[]{:S(2)}, u32[]{:S(2)}) collective-permute-start(bf16[2,560,384]{2,1,0:T(8,128)(2,1)} %broadcast_select_fusion.8), channel_id=1, source_target_pairs={{0,16},{16,0},{1,17},{17,1},{2,18},{18,2},{3,19},{19,3},{4,20},{20... | collective-permute-start | bytes 2580488 | tf_op jit(solution)/shard_map/ppermute | solution.py:31
  965.5 31.7 %collective-permute-start.8 = (bf16[2,256,1536]{2,1,0:T(8,128)(2,1)}, bf16[2,256,1536]{2,1,0:T(8,128)(2,1)}, u32[]{:S(2)}, u32[]{:S(2)}) collective-permute-start(bf16[2,256,1536]{2,1,0:T(8,128)(2,1)} %bitcast.51), channel_id=1, source_target_pairs={{0,16},{16,0},{1,17},{17,1},{2,18},{18,2},{3,19},{19,3},{4,20},{20... | collective-permute-start | bytes 4718600 | tf_op jit(solution)/shard_map/ppermute | solution.py:31
  973.0 4.5 collective-permute-start.10
  978.4 3.1 collective-permute-start.11
  981.5 19.3 %collective-permute-start.7 = (bf16[2,256,1536]{2,1,0:T(8,128)(2,1)}, bf16[2,256,1536]{2,1,0:T(8,128)(2,1)}, u32[]{:S(2)}, u32[]{:S(2)}) collective-permute-start(bf16[2,256,1536]{2,1,0:T(8,128)(2,1)} %bitcast.275), channel_id=1, source_target_pairs={{0,16},{16,0},{1,17},{17,1},{2,18},{18,2},{3,19},{19,3},{4,20},{20... | collective-permute-start | bytes 4718600 | tf_op jit(solution)/shard_map/ppermute | solution.py:31
  (43 other events, 102.3 us)

commit v4 on v3

--- a/solution.py
+++ b/solution.py
@@ -234,7 +234,8 @@
 class Move:
     def __init__(self, source, outs, scratch, ways):
         self.name = source if isinstance(source, str) else None
-        self.operands = [] if self.name else [source]
+        sources = list(source) if isinstance(source, tuple) else [source]
+        self.operands = [] if self.name else sources
         self.outs, self.scratch, self.ways = outs, scratch, ways
         self.steps, self.at = [], 0
 
@@ -245,36 +246,56 @@
 
 
 class FfnGather(Move):
-    def __init__(self, part, across):
-        rows = lax.axis_size(ROW)
+    def __init__(self, layer, parts, across):
+        rows, part = lax.axis_size(ROW), parts[0]
+        self.layer = layer
         self.flips, self.across = list(range(rows - 1, 0, -1)), across
         outs = [(rows, *part.shape[1:])] * 2
         ways = [(ROW, flip) for flip in self.flips] + [across]
-        super().__init__(part, outs, semaphores(rows, rows, rows, rows, 1), ways)
+        super().__init__(tuple(parts), outs, semaphores(rows, rows, rows, rows, 1), ways)
 
     def bind(self, sources, targets, scratch):
-        (part,), (own, other) = sources, targets
+        own, other = targets
         self.blocks = [own, other]
         row_send, row_recv, far_send, far_recv, local_sem = scratch
         row = lax.axis_index(ROW)
-        near = part.at[row & 1]
-        local = pltpu.make_async_copy(near, own.at[row], local_sem.at[0])
-        hops = {
+        is_own = lax.axis_index(SEC) == self.layer
+
+        class Either:
+            def __init__(self, make):
+                self.made = [make(part) for part in sources]
+
+            def start(self):
+                pl.when(is_own)(self.made[0].start)
+                pl.when(jnp.logical_not(is_own))(self.made[1].start)
+
+            def wait(self):
+                self.made[0].wait()
+
+            def wait_recv(self):
+                self.made[0].wait_recv()
+
+            def wait_send(self):
+                self.made[0].wait_send()
+
+        def exchange(flip):
+            return Either(
+                lambda part: remote(
+                    part.at[(row ^ flip) & 1], own.at[row], row_send.at[flip], row_recv.at[flip], (ROW, flip)
+                )
+            )
+
+        local = Either(lambda part: pltpu.make_async_copy(part.at[row & 1], own.at[row], local_sem.at[0]))
+        hops = {flip: exchange(flip) for flip in self.flips}
+        far = {
             flip: remote(
-                part.at[(row ^ flip) & 1], own.at[row], row_send.at[flip], row_recv.at[flip], (ROW, flip)
+                own.at[row ^ flip], other.at[row ^ flip], far_send.at[flip], far_recv.at[flip], self.across
             )
             for flip in self.flips
         }
-        far = {
-            flip: remote(
-                own.at[row ^ flip] if flip else near,
-                other.at[row ^ flip],
-                far_send.at[flip],
-                far_recv.at[flip],
-                self.across,
-            )
-            for flip in [0] + self.flips
-        }
+        far[0] = Either(
+            lambda part: remote(part.at[row & 1], other.at[row], far_send.at[0], far_recv.at[0], self.across)
+        )
 
         def start():
             local.start()
@@ -1451,7 +1472,7 @@
 
     attn_moves = [AttnGather(of_layer(layer, attn_halves, section, 0)) for layer in range(2)]
     ffn_moves = [
-        [FfnGather(of_layer(layer, parts[kind], section, 0), across[layer]) for kind in range(3)]
+        [FfnGather(layer, parts[kind], across[layer]) for kind in range(3)]
         for layer in range(2)
     ]
     grad_own = lax.dynamic_slice(

time: 1010 us -> 1010 us (level)
  no operation moved by 1% of the time
where the time goes in v4:
time: 1010 us; the launch traced here: 999 us
  Pallas kernels  852 us (84%)
  other arithmetic  47.3 us (5%)
  local copies, waits for them, and re-layouts  42.1 us (4%)
  matrix products  36.1 us (4%)
  starting transfers between devices  11.6 us (1%)
    pallas_call x4, Pallas kernels, kernel_call(): pl.pallas_call(body, out_shape=[jax.ShapeDtypeStruct(shape, dtype) for sh...  852 us
    dot_general x6, matrix products, dot(): lax.dot_general(left, right, (((left_dim,), (right_dim,)), ((), ())), pre...  36.1 us
  transfers between devices with their start and end apart: 15, of which 2 were waited for; matrix products, arithmetic and copies ran while one was open for 6% of the time, Pallas kernels for 0%

profile of v4, /device:TPU:9, one launch (start us, length us, event | category | flops | bytes accessed | tf_op | source)
XLA Modules:
  0.0 999.3 jit_solution(4953823204016338285)
XLA Ops:
  7.2 2.6 dynamic-slice_bitcast_fusion.4
  28.4 2.2 collective-permute-done.2
  37.4 405.5 %shard_map.220 = (bf16[128,1536]{1,0:T(8,128)(2,1)}, f32[128,1536]{1,0:T(8,128)}, f32[128,1536]{1,0:T(8,128)}, bf16[512,1536]{1,0:T(8,128)(2,1)}, bf16[512,384]{...) custom-call(bf16[4,128,1536]{2,1,0:T(8,128)(2,1)} %pad_maximum_fusio, ...), custom_call_target="tpu_custom_call" | custom-call | flops 17179869184 | bytes 33554432 | tf_op jit(solution)/shard_map/pallas_call | solution.py:207
  442.9 1.9 convert_element_type.287.refs_27_
  444.8 8.7 convolution_convert_fusion.5.refs_12_
  453.6 44.5 %shard_map.221 = (f32[128,1536]{1,0:T(8,128)}, f32[1,1536]{1,0:T(1,128)}, bf16[1024,1152]{1,0:T(8,128)(2,1)}, bf16[1024,1152]{1,0:T(8,128)(2,1)}, bf16[560,1536]{1,0:T(8,128)(2,1)}) custom-call(bf16[128,1536]{1,0:T(8,128)(2,1)} %dynamic-slice_bitcast_fusion.7.refs_28_.refs_0_, bf16[4,2,128,1536]{3,2,1,0:T(8,128)(2,1)} %get-tuple-element.80.refs_1_, ...), custom_call_target="tpu_custom_call" | custom-call | flops 8589934592 | bytes 33554432 | tf_op jit(solution)/shard_map/pallas_call | solution.py:207
  498.1 2.6 add_convert_fusion.1
  502.6 5.4 convolution_convert_fusion.3.refs_26_
  508.0 5.4 convolution_convert_fusion.4.refs_25_
  514.9 188.0 %shard_map.222 = (bf16[128,1536]{1,0:T(8,128)(2,1)}, bf16[4,2,128,1536]{3,2,1,0:T(8,128)(2,1)}, f32[1,1536]{1,0:T(1,128)}, f32[1,384]{1,0:T(1,128)}, f32[1,256]{...) custom-call(f32[128,1536]{1,0:T(8,128)} %get-tuple-element.91.refs_0, ...), custom_call_target="tpu_custom_call" | custom-call | flops 8589934592 | bytes 33554432 | tf_op jit(solution)/shard_map/pallas_call | solution.py:207
  703.0 2.6 add_convert_fusion
  707.3 5.4 convolution_convert_fusion.1.refs_21_
  712.7 5.4 convolution_convert_fusion.refs_22_
  718.2 5.6 convolution_convert_fusion.2.refs_20_
  725.3 213.6 %shard_map.223 = (bf16[128,1536]{1,0:T(8,128)(2,1)}, f32[80,128]{1,0:T(8,128)}, bf16[4,560,384]{2,1,0:T(8,128)(2,1)}, bf16[560,384]{1,0:T(8,128)(2,1)}, bf16[4,5...) custom-call(f32[128,1536]{1,0:T(8,128)} %get-tuple-element.113.refs_, ...), custom_call_target="tpu_custom_call" | custom-call | flops 4294967296 | bytes 33554432 | tf_op jit(solution)/shard_map/pallas_call | solution.py:207
  944.4 4.3 collective-permute-start.9
  967.5 1.9 slice_bitcast_fusion
  969.5 2.5 collective-permute-done.10
  973.8 2.1 copy.95
  984.0 2.0 copy.92
  986.0 2.0 copy.93
  989.7 2.0 copy.94
  993.3 1.9 maximum_bitcast_fusion.1
  996.9 1.9 maximum_bitcast_fusion
  (226 shorter events, 73.2 us)
Async XLA Ops:
  3.5 28.7 %collective-permute-start = (bf16[3968]{0:T(1024)(128)(2,1)S(1)}, bf16[3968]{0:T(1024)(128)(2,1)S(1)}, u32[]{:S(2)}, u32[]{:S(2)}) collective-permute-start(bf16[3968]{0:T(1024)(128)(2,1)S(1)} %pad_maximum_fusion.14), channel_id=1, source_target_pairs={{0,16},{16,0},{1,17},{17,1},{2,18},{18,2},{3,19},{19,3},{4,20},{20... | collective-permute-start | bytes 23816 | tf_op jit(solution)/shard_map/ppermute | solution.py:31
  5.9 20.6 %collective-permute-start.1 = (bf16[96,256]{1,0:T(8,128)(2,1)S(1)}, bf16[96,256]{1,0:T(8,128)(2,1)S(1)}, u32[]{:S(2)}, u32[]{:S(2)}) collective-permute-start(bf16[96,256]{1,0:T(8,128)(2,1)S(1)} %bitcast.277), channel_id=1, source_target_pairs={{0,2},{1,3},{2,0},{3,1},{4,6},{5,7},{6,4},{7,5},{8,10},{9,11},{10,... | collective-permute-start | bytes 147464 | tf_op jit(solution)/shard_map/ppermute | solution.py:31
  9.8 27.6 %collective-permute-start.4 = (bf16[2,560,384]{2,1,0:T(8,128)(2,1)S(1)}, bf16[2,560,384]{2,1,0:T(8,128)(2,1)}, u32[]{:S(2)}, u32[]{:S(2)}) collective-permute-start(bf16[2,560,384]{2,1,0:T(8,128)(2,1)S(1)} %get-tuple-element.240), channel_id=1, source_target_pairs={{0,16},{16,0},{1,17},{17,1},{2,18},{18,2},{3,19},{19,3},{4,20},{20... | collective-permute-start | bytes 2580488 | tf_op jit(solution)/shard_map/ppermute | solution.py:31
  11.2 26.2 %collective-permute-start.5 = (bf16[2,560,384]{2,1,0:T(8,128)(2,1)S(1)}, bf16[2,560,384]{2,1,0:T(8,128)(2,1)}, u32[]{:S(2)}, u32[]{:S(2)}) collective-permute-start(bf16[2,560,384]{2,1,0:T(8,128)(2,1)S(1)} %get-tuple-element.238), channel_id=1, source_target_pairs={{0,16},{16,0},{1,17},{17,1},{2,18},{18,2},{3,19},{19,3},{4,20},{20... | collective-permute-start | bytes 2580488 | tf_op jit(solution)/shard_map/ppermute | solution.py:31
  11.9 6.1 copy-start.40
  13.3 24.1 %collective-permute-start.6 = (bf16[2,560,384]{2,1,0:T(8,128)(2,1)}, bf16[2,560,384]{2,1,0:T(8,128)(2,1)}, u32[]{:S(2)}, u32[]{:S(2)}) collective-permute-start(bf16[2,560,384]{2,1,0:T(8,128)(2,1)} %get-tuple-element.236), channel_id=1, source_target_pairs={{0,16},{16,0},{1,17},{17,1},{2,18},{18,2},{3,19},{19,3},{4,20},{20... | collective-permute-start | bytes 2580488 | tf_op jit(solution)/shard_map/ppermute | solution.py:31
  24.2 6.7 copy-start.38
  26.5 4.1 collective-permute-start.2
  31.0 5.4 collective-permute-start.3
  502.6 5.4 copy-start.46
  712.7 5.5 copy-start.41
  712.7 5.5 copy-start.48
  725.3 215.1 %copy-start.28 = (bf16[4,560,384]{2,1,0:T(8,128)(2,1)S(1)}, bf16[4,560,384]{2,1,0:T(8,128)(2,1)}, u32[]{:S(2)}) copy-start(bf16[4,560,384]{2,1,0:T(8,128)(2,1)} %get-tuple-element.147) | copy-start | bytes 5160964
  941.7 7.0 copy-start.36
  943.0 9.7 copy-start.1
  943.1 9.7 copy-start.3
  944.4 18.1 %collective-permute-start.9 = (bf16[512,384]{1,0:T(8,128)(2,1)S(1)}, bf16[512,384]{1,0:T(8,128)(2,1)S(1)}, u32[]{:S(2)}, u32[]{:S(2)}) collective-permute-start(bf16[512,384]{1,0:T(8,128)(2,1)S(1)} %broadcast_select_fusion.16), channel_id=1, source_target_pairs={{0,16},{16,0},{1,17},{17,1},{2,18},{18,2},{3,19},{19,3},{4,20},{20... | collective-permute-start | bytes 1179656 | tf_op jit(solution)/shard_map/ppermute | solution.py:31
  951.3 36.7 %collective-permute-start.14 = (bf16[2,560,384]{2,1,0:T(8,128)(2,1)}, bf16[2,560,384]{2,1,0:T(8,128)(2,1)}, u32[]{:S(2)}, u32[]{:S(2)}) collective-permute-start(bf16[2,560,384]{2,1,0:T(8,128)(2,1)} %broadcast_select_fusion.4), channel_id=1, source_target_pairs={{0,16},{16,0},{1,17},{17,1},{2,18},{18,2},{3,19},{19,3},{4,20},{20... | collective-permute-start | bytes 2580488 | tf_op jit(solution)/shard_map/ppermute | solution.py:31
  953.8 27.4 %collective-permute-start.13 = (bf16[2,560,384]{2,1,0:T(8,128)(2,1)}, bf16[2,560,384]{2,1,0:T(8,128)(2,1)}, u32[]{:S(2)}, u32[]{:S(2)}) collective-permute-start(bf16[2,560,384]{2,1,0:T(8,128)(2,1)} %broadcast_select_fusion.6), channel_id=1, source_target_pairs={{0,16},{16,0},{1,17},{17,1},{2,18},{18,2},{3,19},{19,3},{4,20},{20... | collective-permute-start | bytes 2580488 | tf_op jit(solution)/shard_map/ppermute | solution.py:31
  957.0 22.1 %collective-permute-start.12 = (bf16[2,560,384]{2,1,0:T(8,128)(2,1)}, bf16[2,560,384]{2,1,0:T(8,128)(2,1)}, u32[]{:S(2)}, u32[]{:S(2)}) collective-permute-start(bf16[2,560,384]{2,1,0:T(8,128)(2,1)} %broadcast_select_fusion.8), channel_id=1, source_target_pairs={{0,16},{16,0},{1,17},{17,1},{2,18},{18,2},{3,19},{19,3},{4,20},{20... | collective-permute-start | bytes 2580488 | tf_op jit(solution)/shard_map/ppermute | solution.py:31
  960.0 31.7 %collective-permute-start.8 = (bf16[2,256,1536]{2,1,0:T(8,128)(2,1)}, bf16[2,256,1536]{2,1,0:T(8,128)(2,1)}, u32[]{:S(2)}, u32[]{:S(2)}) collective-permute-start(bf16[2,256,1536]{2,1,0:T(8,128)(2,1)} %bitcast.51), channel_id=1, source_target_pairs={{0,16},{16,0},{1,17},{17,1},{2,18},{18,2},{3,19},{19,3},{4,20},{20... | collective-permute-start | bytes 4718600 | tf_op jit(solution)/shard_map/ppermute | solution.py:31
  967.4 4.5 collective-permute-start.10
  972.9 3.1 collective-permute-start.11
  976.0 19.3 %collective-permute-start.7 = (bf16[2,256,1536]{2,1,0:T(8,128)(2,1)}, bf16[2,256,1536]{2,1,0:T(8,128)(2,1)}, u32[]{:S(2)}, u32[]{:S(2)}) collective-permute-start(bf16[2,256,1536]{2,1,0:T(8,128)(2,1)} %bitcast.269), channel_id=1, source_target_pairs={{0,16},{16,0},{1,17},{17,1},{2,18},{18,2},{3,19},{19,3},{4,20},{20... | collective-permute-start | bytes 4718600 | tf_op jit(solution)/shard_map/ppermute | solution.py:31
  (40 other events, 87.5 us)

commit v5 on v4

--- a/solution.py
+++ b/solution.py
@@ -1715,12 +1715,12 @@
         1 << 32,
         [up_rows, *zero_moves, attn_move_zero, first_move, result_move],
         dict(
-            a0_relayed=[down_zero],
-            a0_hops=[up_rows, result_move],
-            a0_edges=[gate_zero, up_zero],
-            a0_grads=[down_zero, attn_move_zero, result_move],
+            a0_relayed=[down_zero, up_rows],
+            a0_hops=[result_move],
+            a0_edges=[down_zero, gate_zero, up_zero],
+            a0_grads=[attn_move_zero, result_move],
             a0_end=[attn_move_zero, gate_zero, first_move],
-            s1_step=[attn_move_zero],
+            s0_step=[attn_move_zero, up_zero],
             s2_step=[first_move],
             s3_step=[attn_move_zero],
         ),

time: 1010 us -> 1010 us (level)
  no operation moved by 1% of the time
where the time goes in v5:
time: 1010 us; the launch traced here: 996 us
  Pallas kernels  843 us (83%)
  other arithmetic  47.3 us (5%)
  local copies, waits for them, and re-layouts  42.1 us (4%)
  matrix products  36.1 us (4%)
  starting transfers between devices  18.3 us (2%)
    pallas_call x4, Pallas kernels, kernel_call(): pl.pallas_call(body, out_shape=[jax.ShapeDtypeStruct(shape, dtype) for sh...  843 us
    dot_general x6, matrix products, dot(): lax.dot_general(left, right, (((left_dim,), (right_dim,)), ((), ())), pre...  36.1 us
  transfers between devices with their start and end apart: 15, of which 2 were waited for; matrix products, arithmetic and copies ran while one was open for 6% of the time, Pallas kernels for 0%

profile of v5, /device:TPU:9, one launch (start us, length us, event | category | flops | bytes accessed | tf_op | source)
XLA Modules:
  0.0 996.2 jit_solution(17862390951715339146)
XLA Ops:
  7.2 2.6 dynamic-slice_bitcast_fusion.4
  28.4 2.2 collective-permute-done.2
  37.4 405.5 %shard_map.220 = (bf16[128,1536]{1,0:T(8,128)(2,1)}, f32[128,1536]{1,0:T(8,128)}, f32[128,1536]{1,0:T(8,128)}, bf16[512,1536]{1,0:T(8,128)(2,1)}, bf16[512,384]{...) custom-call(bf16[4,128,1536]{2,1,0:T(8,128)(2,1)} %pad_maximum_fusio, ...), custom_call_target="tpu_custom_call" | custom-call | flops 17179869184 | bytes 33554432 | tf_op jit(solution)/shard_map/pallas_call | solution.py:207
  442.9 1.9 convert_element_type.287.refs_27_
  444.8 8.7 convolution_convert_fusion.5.refs_12_
  453.6 44.5 %shard_map.221 = (f32[128,1536]{1,0:T(8,128)}, f32[1,1536]{1,0:T(1,128)}, bf16[1024,1152]{1,0:T(8,128)(2,1)}, bf16[1024,1152]{1,0:T(8,128)(2,1)}, bf16[560,1536]{1,0:T(8,128)(2,1)}) custom-call(bf16[128,1536]{1,0:T(8,128)(2,1)} %dynamic-slice_bitcast_fusion.7.refs_28_.refs_0_, bf16[4,2,128,1536]{3,2,1,0:T(8,128)(2,1)} %get-tuple-element.80.refs_1_, ...), custom_call_target="tpu_custom_call" | custom-call | flops 8589934592 | bytes 33554432 | tf_op jit(solution)/shard_map/pallas_call | solution.py:207
  498.1 2.6 add_convert_fusion.1
  502.6 5.4 convolution_convert_fusion.3.refs_26_
  508.0 5.4 convolution_convert_fusion.4.refs_25_
  514.9 188.0 %shard_map.222 = (bf16[128,1536]{1,0:T(8,128)(2,1)}, bf16[4,2,128,1536]{3,2,1,0:T(8,128)(2,1)}, f32[1,1536]{1,0:T(1,128)}, f32[1,384]{1,0:T(1,128)}, f32[1,256]{...) custom-call(f32[128,1536]{1,0:T(8,128)} %get-tuple-element.91.refs_0, ...), custom_call_target="tpu_custom_call" | custom-call | flops 8589934592 | bytes 33554432 | tf_op jit(solution)/shard_map/pallas_call | solution.py:207
  703.0 2.6 add_convert_fusion
  707.3 5.4 convolution_convert_fusion.1.refs_21_
  712.7 5.4 convolution_convert_fusion.refs_22_
  718.2 5.6 convolution_convert_fusion.2.refs_20_
  725.3 205.0 %shard_map.223 = (bf16[128,1536]{1,0:T(8,128)(2,1)}, f32[80,128]{1,0:T(8,128)}, bf16[4,560,384]{2,1,0:T(8,128)(2,1)}, bf16[560,384]{1,0:T(8,128)(2,1)}, bf16[4,5...) custom-call(f32[128,1536]{1,0:T(8,128)} %get-tuple-element.113.refs_, ...), custom_call_target="tpu_custom_call" | custom-call | flops 4294967296 | bytes 33554432 | tf_op jit(solution)/shard_map/pallas_call | solution.py:207
  935.8 9.9 collective-permute-start.9
  965.6 1.9 slice_bitcast_fusion
  971.2 2.1 copy.95
  976.0 1.9 select_bitcast_fusion.5
  981.0 2.0 copy.92
  983.0 2.0 copy.93
  986.7 2.0 copy.94
  990.3 1.9 maximum_bitcast_fusion.1
  993.8 1.9 maximum_bitcast_fusion
  (226 shorter events, 73.8 us)
Async XLA Ops:
  3.5 28.7 %collective-permute-start = (bf16[3968]{0:T(1024)(128)(2,1)S(1)}, bf16[3968]{0:T(1024)(128)(2,1)S(1)}, u32[]{:S(2)}, u32[]{:S(2)}) collective-permute-start(bf16[3968]{0:T(1024)(128)(2,1)S(1)} %pad_maximum_fusion.14), channel_id=1, source_target_pairs={{0,16},{16,0},{1,17},{17,1},{2,18},{18,2},{3,19},{19,3},{4,20},{20... | collective-permute-start | bytes 23816 | tf_op jit(solution)/shard_map/ppermute | solution.py:31
  5.9 20.6 %collective-permute-start.1 = (bf16[96,256]{1,0:T(8,128)(2,1)S(1)}, bf16[96,256]{1,0:T(8,128)(2,1)S(1)}, u32[]{:S(2)}, u32[]{:S(2)}) collective-permute-start(bf16[96,256]{1,0:T(8,128)(2,1)S(1)} %bitcast.277), channel_id=1, source_target_pairs={{0,2},{1,3},{2,0},{3,1},{4,6},{5,7},{6,4},{7,5},{8,10},{9,11},{10,... | collective-permute-start | bytes 147464 | tf_op jit(solution)/shard_map/ppermute | solution.py:31
  9.8 27.6 %collective-permute-start.4 = (bf16[2,560,384]{2,1,0:T(8,128)(2,1)S(1)}, bf16[2,560,384]{2,1,0:T(8,128)(2,1)}, u32[]{:S(2)}, u32[]{:S(2)}) collective-permute-start(bf16[2,560,384]{2,1,0:T(8,128)(2,1)S(1)} %get-tuple-element.240), channel_id=1, source_target_pairs={{0,16},{16,0},{1,17},{17,1},{2,18},{18,2},{3,19},{19,3},{4,20},{20... | collective-permute-start | bytes 2580488 | tf_op jit(solution)/shard_map/ppermute | solution.py:31
  11.2 26.2 %collective-permute-start.5 = (bf16[2,560,384]{2,1,0:T(8,128)(2,1)S(1)}, bf16[2,560,384]{2,1,0:T(8,128)(2,1)}, u32[]{:S(2)}, u32[]{:S(2)}) collective-permute-start(bf16[2,560,384]{2,1,0:T(8,128)(2,1)S(1)} %get-tuple-element.238), channel_id=1, source_target_pairs={{0,16},{16,0},{1,17},{17,1},{2,18},{18,2},{3,19},{19,3},{4,20},{20... | collective-permute-start | bytes 2580488 | tf_op jit(solution)/shard_map/ppermute | solution.py:31
  11.9 6.1 copy-start.40
  13.3 24.1 %collective-permute-start.6 = (bf16[2,560,384]{2,1,0:T(8,128)(2,1)}, bf16[2,560,384]{2,1,0:T(8,128)(2,1)}, u32[]{:S(2)}, u32[]{:S(2)}) collective-permute-start(bf16[2,560,384]{2,1,0:T(8,128)(2,1)} %get-tuple-element.236), channel_id=1, source_target_pairs={{0,16},{16,0},{1,17},{17,1},{2,18},{18,2},{3,19},{19,3},{4,20},{20... | collective-permute-start | bytes 2580488 | tf_op jit(solution)/shard_map/ppermute | solution.py:31
  24.2 6.7 copy-start.38
  26.5 4.1 collective-permute-start.2
  31.0 5.4 collective-permute-start.3
  502.6 5.4 copy-start.46
  712.7 5.5 copy-start.41
  712.7 5.5 copy-start.48
  725.3 206.5 %copy-start.28 = (bf16[4,560,384]{2,1,0:T(8,128)(2,1)S(1)}, bf16[4,560,384]{2,1,0:T(8,128)(2,1)}, u32[]{:S(2)}) copy-start(bf16[4,560,384]{2,1,0:T(8,128)(2,1)} %get-tuple-element.147) | copy-start | bytes 5160964
  933.0 12.6 %copy-start.36 = (bf16[560,384]{1,0:T(8,128)(2,1)S(1)}, bf16[560,384]{1,0:T(8,128)(2,1)}, u32[]{:S(2)}) copy-start(bf16[560,384]{1,0:T(8,128)(2,1)} %get-tuple-element.145) | copy-start | bytes 1290244
  934.4 15.2 %copy-start.1 = (bf16[1,560,384]{2,1,0:T(8,128)(2,1)}, bf16[1,560,384]{2,1,0:T(8,128)(2,1)S(1)}, u32[]{:S(2)}) copy-start(bf16[1,560,384]{2,1,0:T(8,128)(2,1)S(1)} %get-tuple-element.200) | copy-start | bytes 1290244
  934.4 15.2 %copy-start.3 = (bf16[1,560,384]{2,1,0:T(8,128)(2,1)}, bf16[1,560,384]{2,1,0:T(8,128)(2,1)S(1)}, u32[]{:S(2)}) copy-start(bf16[1,560,384]{2,1,0:T(8,128)(2,1)S(1)} %get-tuple-element.201) | copy-start | bytes 1290244
  935.8 23.7 %collective-permute-start.9 = (bf16[512,384]{1,0:T(8,128)(2,1)S(1)}, bf16[512,384]{1,0:T(8,128)(2,1)S(1)}, u32[]{:S(2)}, u32[]{:S(2)}) collective-permute-start(bf16[512,384]{1,0:T(8,128)(2,1)S(1)} %broadcast_select_fusion.16), channel_id=1, source_target_pairs={{0,16},{16,0},{1,17},{17,1},{2,18},{18,2},{3,19},{19,3},{4,20},{20... | collective-permute-start | bytes 1179656 | tf_op jit(solution)/shard_map/ppermute | solution.py:31
  948.3 36.7 %collective-permute-start.14 = (bf16[2,560,384]{2,1,0:T(8,128)(2,1)}, bf16[2,560,384]{2,1,0:T(8,128)(2,1)}, u32[]{:S(2)}, u32[]{:S(2)}) collective-permute-start(bf16[2,560,384]{2,1,0:T(8,128)(2,1)} %broadcast_select_fusion.4), channel_id=1, source_target_pairs={{0,16},{16,0},{1,17},{17,1},{2,18},{18,2},{3,19},{19,3},{4,20},{20... | collective-permute-start | bytes 2580488 | tf_op jit(solution)/shard_map/ppermute | solution.py:31
  950.8 27.4 %collective-permute-start.13 = (bf16[2,560,384]{2,1,0:T(8,128)(2,1)}, bf16[2,560,384]{2,1,0:T(8,128)(2,1)}, u32[]{:S(2)}, u32[]{:S(2)}) collective-permute-start(bf16[2,560,384]{2,1,0:T(8,128)(2,1)} %broadcast_select_fusion.6), channel_id=1, source_target_pairs={{0,16},{16,0},{1,17},{17,1},{2,18},{18,2},{3,19},{19,3},{4,20},{20... | collective-permute-start | bytes 2580488 | tf_op jit(solution)/shard_map/ppermute | solution.py:31
  953.9 22.1 %collective-permute-start.12 = (bf16[2,560,384]{2,1,0:T(8,128)(2,1)}, bf16[2,560,384]{2,1,0:T(8,128)(2,1)}, u32[]{:S(2)}, u32[]{:S(2)}) collective-permute-start(bf16[2,560,384]{2,1,0:T(8,128)(2,1)} %broadcast_select_fusion.8), channel_id=1, source_target_pairs={{0,16},{16,0},{1,17},{17,1},{2,18},{18,2},{3,19},{19,3},{4,20},{20... | collective-permute-start | bytes 2580488 | tf_op jit(solution)/shard_map/ppermute | solution.py:31
  956.9 31.7 %collective-permute-start.8 = (bf16[2,256,1536]{2,1,0:T(8,128)(2,1)}, bf16[2,256,1536]{2,1,0:T(8,128)(2,1)}, u32[]{:S(2)}, u32[]{:S(2)}) collective-permute-start(bf16[2,256,1536]{2,1,0:T(8,128)(2,1)} %bitcast.51), channel_id=1, source_target_pairs={{0,16},{16,0},{1,17},{17,1},{2,18},{18,2},{3,19},{19,3},{4,20},{20... | collective-permute-start | bytes 4718600 | tf_op jit(solution)/shard_map/ppermute | solution.py:31
  964.4 4.5 collective-permute-start.10
  969.9 3.5 collective-permute-start.11
  973.3 18.9 %collective-permute-start.7 = (bf16[2,256,1536]{2,1,0:T(8,128)(2,1)}, bf16[2,256,1536]{2,1,0:T(8,128)(2,1)}, u32[]{:S(2)}, u32[]{:S(2)}) collective-permute-start(bf16[2,256,1536]{2,1,0:T(8,128)(2,1)} %bitcast.269), channel_id=1, source_target_pairs={{0,16},{16,0},{1,17},{17,1},{2,18},{18,2},{3,19},{19,3},{4,20},{20... | collective-permute-start | bytes 4718600 | tf_op jit(solution)/shard_map/ppermute | solution.py:31
  (40 other events, 87.5 us)
